TPU v7x, 128 devices: a whole 4x4x4 slice. The times are simulated.
128 devices in a mesh: node: 8 (over x, core), dev: 16 (over y, z).
Axes of the slice: x: 4, y: 4, z: 4, core: 2. Of those that a mesh axis runs over, the one named last changes fastest.
Arguments:
- q_nope: bfloat16 [4096, 4096], P('node', 'dev'), may hold values from -6 to 6
- q_rope: bfloat16 [4096, 2048], P('node', 'dev'), may hold values from -75 to 75
- kv_latent: bfloat16 [4096, 512], P('node'), may hold values from -6 to 6
- k_rope: bfloat16 [4096, 64], P('node'), may hold values from -5 to 5
- pool_latent: bfloat16 [256, 128, 512], P(('node', 'dev')), may hold values from -12 to 12
- pool_rope: bfloat16 [256, 128, 64], P(('node', 'dev')), may hold values from -6 to 6
- block_table: int32 [4], replicated, may hold values from 0 to 255, as said below
- absorb_k: bfloat16 [32, 128, 512], P('dev'), may hold values from -0.5 to 0.5
- absorb_v: bfloat16 [32, 512, 128], P('dev'), may hold values from -1 to 1
- out_proj: bfloat16 [4096, 3584], P('dev'), may hold values from -0.375 to 0.375
- residual: bfloat16 [4096, 3584], P(('node', 'dev')), may hold values from -45 to 45
- norm_gain: bfloat16 [3584], replicated, may hold values from 0.25 to 1.75
- router: bfloat16 [3584, 64], replicated, may hold values from -0.09375 to 0.09375
- expert_ids: int32 [4096, 8], P(('node', 'dev')), may hold values from 0 to 63, all different within a row; in each aligned block of 32 rows (0 to 31, 32 to 63, ...) at most 8 rows name the same one
- expert_gate: bfloat16 [128, 3584, 512], P(('node', 'dev')), may hold values from -0.09375 to 0.09375
- expert_up: bfloat16 [128, 3584, 512], P(('node', 'dev')), may hold values from -0.09375 to 0.09375
- expert_down: bfloat16 [128, 512, 3584], P(('node', 'dev')), may hold values from -0.1875 to 0.1875
Outputs:
- attended: bfloat16 [4096, 3584], P(('node', 'dev'))
- expert_out: bfloat16 [4096, 3584], P(('node', 'dev'))
Inputs may be any that keep to these rules, and one draw needn't show every extreme that they name: `block_table`: distinct pool block numbers. `expert_ids`: each row names 8 different experts. In the rows of one device no expert is named more than 8 times, a bound that some block reaches.
All inputs are finite; a program needn't handle non-finite values.
Results may differ from a plain program's by a relative error of at most 0.039.
Values may be sent and summed in bfloat16 or wider, within the bound.
No kernel may reach another device: no remote copies, remote signals or barrier semaphores. Data moves between devices by JAX's collectives and lax.ppermute only.
A program may use at most 128 MiB of HBM per device.

v0:
```python
import math

import jax
import jax.numpy as jnp
from jax import lax
from jax.sharding import PartitionSpec as P

ROUTE_SCALE = 2.827
NORM_EPS = 1e-06
FAR_BELOW = -1e30


def broadcast(value, axis, source):
    kept = jnp.where(lax.axis_index(axis) == source, value, 0).astype(value.dtype)
    return lax.psum(kept, axis)


def fold_keys(carried, keys_lat, keys_rot, visible, q_lat, q_rot, softmax_scale):
    running_top, running_sum, mixed = carried
    scores = (
        jnp.dot(q_lat, keys_lat.T, preferred_element_type=jnp.float32)
        + jnp.dot(q_rot, keys_rot.T, preferred_element_type=jnp.float32)
    ) * softmax_scale
    masked = jnp.where(visible, scores, FAR_BELOW)
    new_top = jnp.maximum(running_top, jnp.max(masked, axis=1, keepdims=True))
    exp_scores = jnp.where(visible, jnp.exp(masked - new_top), 0.0)
    shrink = jnp.exp(running_top - new_top)
    running_sum = running_sum * shrink + jnp.sum(exp_scores, axis=1, keepdims=True)
    mixed = mixed * shrink + jnp.dot(
        exp_scores.astype(jnp.bfloat16), keys_lat, preferred_element_type=jnp.float32
    )
    return (new_top, running_sum, mixed)


def expert_ffn(token_rows, gate_rows, up_rows, down_rows):
    gate_act = jnp.dot(token_rows, gate_rows, preferred_element_type=jnp.float32)
    up_act = jnp.dot(token_rows, up_rows, preferred_element_type=jnp.float32)
    hidden = (jax.nn.silu(gate_act) * up_act).astype(jnp.bfloat16)
    return jnp.dot(hidden, down_rows, preferred_element_type=jnp.float32).astype(jnp.bfloat16)


def on_device(
    q_nope,
    q_rope,
    kv_latent,
    k_rope,
    pool_latent,
    pool_rope,
    block_table,
    absorb_k,
    absorb_v,
    out_proj,
    residual,
    norm_gain,
    router,
    expert_ids,
    expert_gate,
    expert_up,
    expert_down,
):
    node_count = lax.axis_size("node")
    dev_count = lax.axis_size("dev")
    node_index = lax.axis_index("node")
    rows_q = q_nope.shape[0]
    heads_here, nope_dim, lat_rank = absorb_k.shape
    rope_dim = k_rope.shape[1]
    width = residual.shape[1]
    softmax_scale = 1.0 / math.sqrt(nope_dim + rope_dim)
    q_parts = q_nope.reshape(rows_q, heads_here, nope_dim)
    q_lat = jnp.einsum("qhn,hnc->qhc", q_parts, absorb_k, preferred_element_type=jnp.float32)
    q_lat = q_lat.astype(jnp.bfloat16).reshape(rows_q * heads_here, lat_rank)
    q_rot = q_rope.reshape(rows_q * heads_here, rope_dim)
    q_pos = node_index * rows_q + jnp.arange(rows_q * heads_here, dtype=jnp.int32) // heads_here
    carried = (
        jnp.full((rows_q * heads_here, 1), FAR_BELOW, jnp.float32),
        jnp.zeros((rows_q * heads_here, 1), jnp.float32),
        jnp.zeros((rows_q * heads_here, lat_rank), jnp.float32),
    )
    held_here = pool_latent.shape[0]
    block_count = block_table.shape[0]

    def add_listed(block_number, state_now):
        pool_entry = block_table[block_number]
        pool_slot = pool_entry % held_here
        key_piece = jnp.concatenate(
            [
                lax.dynamic_index_in_dim(pool_latent, pool_slot, 0, False),
                lax.dynamic_index_in_dim(pool_rope, pool_slot, 0, False),
            ],
            1,
        )
        key_piece = broadcast(key_piece, ("node", "dev"), pool_entry // held_here)
        return fold_keys(
            state_now,
            key_piece[:, :lat_rank],
            key_piece[:, lat_rank:],
            True,
            q_lat,
            q_rot,
            softmax_scale,
        )

    carried = lax.fori_loop(0, block_count, add_listed, carried)
    piece_lat = lax.all_gather(kv_latent, "node", axis=0, tiled=True)
    piece_rot = lax.all_gather(k_rope, "node", axis=0, tiled=True)
    key_pos = jnp.arange(piece_lat.shape[0], dtype=jnp.int32)
    visible = key_pos[None, :] <= q_pos[:, None]
    running_top, running_sum, mixed = fold_keys(
        carried, piece_lat, piece_rot, visible, q_lat, q_rot, softmax_scale
    )
    head_lat = (mixed / running_sum).astype(jnp.bfloat16).reshape(rows_q, heads_here, lat_rank)
    head_out = jnp.einsum("qhc,hcv->qhv", head_lat, absorb_v, preferred_element_type=jnp.float32)
    head_out = head_out.astype(jnp.bfloat16).reshape(rows_q, -1)
    attn_sum = lax.psum_scatter(
        jnp.dot(head_out, out_proj, preferred_element_type=jnp.float32).astype(jnp.bfloat16),
        "dev",
        scatter_dimension=0,
        tiled=True,
    ).astype(jnp.float32)
    attended = (residual.astype(jnp.float32) + attn_sum).astype(jnp.bfloat16)
    stream = attended.astype(jnp.float32)
    normed = stream * lax.rsqrt(jnp.mean(stream * stream, axis=1, keepdims=True) + NORM_EPS)
    normed = (normed * norm_gain.astype(jnp.float32)).astype(jnp.bfloat16)
    logits = jnp.dot(normed, router, preferred_element_type=jnp.float32)
    expert_count = router.shape[1]
    tokens, top_k = expert_ids.shape
    routed_hit = expert_ids[:, :, None] == jnp.arange(expert_count, dtype=jnp.int32)[None, None, :]
    picked = jnp.sum(jnp.where(routed_hit, logits[:, None, :], 0.0), axis=2)
    gates = jax.nn.sigmoid(picked)
    weights = (ROUTE_SCALE * gates / jnp.sum(gates, axis=1, keepdims=True)).astype(jnp.bfloat16)
    pair_weight = jnp.sum(
        jnp.where(routed_hit, weights[:, :, None], jnp.zeros((), jnp.bfloat16)), axis=1
    )
    is_used = jnp.any(routed_hit, axis=1)
    used_count = is_used.astype(jnp.int32)
    slot_rank = jnp.cumsum(used_count, axis=0) - used_count
    capacity = max(2, 2 * tokens * top_k // expert_count)
    slot_ids = jnp.arange(capacity, dtype=jnp.int32)
    shards = node_count * dev_count // expert_count
    experts_node = expert_count // node_count
    gate_rows = expert_gate[0]
    up_rows = expert_up[0]
    down_rows = expert_down[0]
    slot_fill = (is_used[:, :, None] & (slot_rank[:, :, None] == slot_ids[None, None, :])).astype(
        jnp.bfloat16
    )
    outgoing = jnp.einsum(
        "tec,td->ecd", slot_fill, normed, preferred_element_type=jnp.float32
    ).astype(jnp.bfloat16)
    outgoing = jnp.repeat(
        outgoing.reshape(node_count, experts_node, capacity, width), shards, axis=1
    )
    arrived = lax.all_to_all(
        lax.all_to_all(outgoing, "node", split_axis=0, concat_axis=0, tiled=True),
        "dev",
        split_axis=1,
        concat_axis=1,
        tiled=True,
    )
    served = expert_ffn(arrived.reshape(-1, width), gate_rows, up_rows, down_rows).reshape(
        arrived.shape
    )
    returned = lax.all_to_all(
        lax.all_to_all(served, "node", split_axis=0, concat_axis=0, tiled=True),
        "dev",
        split_axis=1,
        concat_axis=1,
        tiled=True,
    )
    summed = jnp.sum(
        returned.reshape(node_count, experts_node, shards, capacity, width).astype(jnp.float32),
        axis=2,
    )
    shares = slot_fill.astype(jnp.float32) * pair_weight.astype(jnp.float32)[:, :, None]
    shares = shares.reshape(tokens, node_count, experts_node, capacity)
    node_parts = jnp.einsum(
        "tnec,necd->ntd", shares, summed, precision=lax.Precision.HIGHEST
    ).astype(jnp.bfloat16)
    combined = jnp.sum(node_parts.astype(jnp.float32), axis=0)
    return (attended, combined.astype(jnp.bfloat16))


def solution(mesh):
    placed = (
        P("node", "dev"),
        P("node", "dev"),
        P("node", None),
        P("node", None),
        P(("node", "dev"), None, None),
        P(("node", "dev"), None, None),
        P(),
        P("dev", None, None),
        P("dev", None, None),
        P("dev", None),
        P(("node", "dev"), None),
        P(),
        P(),
        P(("node", "dev"), None),
        P(("node", "dev"), None, None),
        P(("node", "dev"), None, None),
        P(("node", "dev"), None, None),
    )
    return jax.shard_map(
        on_device,
        mesh=mesh,
        in_specs=placed,
        out_specs=(P(("node", "dev"), None), P(("node", "dev"), None)),
        check_vma=False,
    )
```

profile of v0, /device:TPU:1, one launch (start us, length us, event | category | flops | bytes accessed | tf_op | source)
XLA Modules:
  0.0 1223.5 jit_solution(13124625727241686604)
XLA Ops:
  9.4 2.1 copy.116
  11.5 1.5 reshape.115
  13.1 16.3 %all_gather.7 = bf16[4096,64]{0,1:T(8,128)(2,1)} all-gather(bf16[512,64]{0,1:T(8,128)(2,1)S(1)} %copy-done.11), channel_id=1, replica_groups=mesh['node'=8,'dev'=16] {'node'}, dimensions={0}, use_global_device_ids=true | all-gather | bytes 589824 | tf_op jit(solution)/shard_map/all_gather | solution.py:105
  29.4 16.5 %all-gather.2.cloned.1.call-done = bf16[4096,512]{1,0:T(8,128)(2,1)} async-done(((bf16[512,512]{1,0:T(8,128)(2,1)}), bf16[4096,512]{1,0:T(8,128)(2,1)}) %all-gather.2.cloned.1.call-update) | async-done | bytes 4194320 | tf_op jit(solution)/shard_map/all_gather | solution.py:104
  45.8 6.4 fusion.79
  52.3 8.1 fusion.77
  60.4 606.8 %while.20 = (s32[]{:T(128)}, f32[1024,1]{0,1:T(1,128)S(1)}, f32[1024,1]{0,1:T(1,128)S(1)}, f32[1024,512]{1,0:T(8,128)}, s32[4]{0:T(128)S(1)}, /*index=5*/bf16[2,...) while((s32[]{:T(128)}, f32[1024,1]{0,1:T(1,128)S(1)}, ...), condition=%wide.region_4.5_spmd.clone, body=%wide.region_0.4_spmd.clone.sunk | while | flops 288150560 | bytes 26673752 | solution.py:103
  65.5 142.5 %all-reduce.2.cloned.1.call-done = bf16[128,576]{1,0:T(8,128)(2,1)} async-done(((bf16[128,576]{1,0:T(8,128)(2,1)}), bf16[128,576]{1,0:T(8,128)(2,1)}) %all-reduce.2.cloned.1.call-update) | async-done | bytes 147472 | tf_op jit(solution)/shard_map/while/body/eval_jaxpr/psum | solution.py:15
  210.7 1.5 fusion.117
  218.5 140.9 %all-reduce.2.cloned.1.call-done = bf16[128,576]{1,0:T(8,128)(2,1)} async-done(((bf16[128,576]{1,0:T(8,128)(2,1)}), bf16[128,576]{1,0:T(8,128)(2,1)}) %all-reduce.2.cloned.1.call-update) | async-done | bytes 147472 | tf_op jit(solution)/shard_map/while/body/eval_jaxpr/psum | solution.py:15
  369.9 140.6 %all-reduce.2.cloned.1.call-done = bf16[128,576]{1,0:T(8,128)(2,1)} async-done(((bf16[128,576]{1,0:T(8,128)(2,1)}), bf16[128,576]{1,0:T(8,128)(2,1)}) %all-reduce.2.cloned.1.call-update) | async-done | bytes 147472 | tf_op jit(solution)/shard_map/while/body/eval_jaxpr/psum | solution.py:15
  513.3 1.5 fusion.117
  521.1 140.6 %all-reduce.2.cloned.1.call-done = bf16[128,576]{1,0:T(8,128)(2,1)} async-done(((bf16[128,576]{1,0:T(8,128)(2,1)}), bf16[128,576]{1,0:T(8,128)(2,1)}) %all-reduce.2.cloned.1.call-update) | async-done | bytes 147472 | tf_op jit(solution)/shard_map/while/body/eval_jaxpr/psum | solution.py:15
  667.2 9.4 fusion.13
  677.9 7.7 divide_convert_fusion
  686.9 1.7 convolution_convert_fusion.4
  688.6 3.0 convolution_convert_fusion.1
  692.3 4.0 fusion.78
  697.0 67.6 %reduce-scatter.2.cloned.1.call-done = bf16[32,3584]{1,0:T(8,128)(2,1)} async-done(((bf16[512,3584]{1,0:T(8,128)(2,1)}), bf16[32,3584]{1,0:T(8,128)(2,1)}) %reduce-scatter.2.cloned.1.call-update) | async-done | bytes 229392 | tf_op jit(solution)/shard_map/reduce_scatter | solution.py:114
  766.9 3.5 broadcast_in_dim.111
  770.5 90.1 %all_to_all.20 = bf16[8,16,8,3584]{3,2,1,0:T(8,128)(2,1)S(1)} all-to-all(bf16[8,16,8,3584]{3,2,1,0:T(8,128)(2,1)} %bitcast.95), channel_id=1, replica_groups=mesh['node'=8,'dev'=16] {'node'}, dimensions={0} | all-to-all | bytes 14680064 | tf_op jit(solution)/shard_map/all_to_all | solution.py:154
  860.6 3.8 copy.129
  864.3 86.6 %all_to_all.21 = bf16[8,16,8,3584]{3,2,0,1:T(8,128)(2,1)S(1)} all-to-all(bf16[8,16,8,3584]{3,2,0,1:T(8,128)(2,1)} %copy.129), channel_id=1, replica_groups=mesh['node'=8,'dev'=16] {'dev'}, dimensions={1} | all-to-all | bytes 14680064 | tf_op jit(solution)/shard_map/all_to_all | solution.py:153
  951.0 3.7 copy.130
  954.6 9.4 fusion.29
  964.0 14.7 %convolution_convert_fusion = bf16[1024,3584]{1,0:T(8,128)(2,1)} fusion(bf16[1,512,3584]{2,1,0:T(8,128)(2,1)} %param.35, f32[1024,512]{1,0:T(8,128)} %fusion.29, bf16[1024,3584]{1,0:T(8,128)(2,1)} %bitcast.98, bf16[1,3584,512]{2,1,0:T(8,128)(2,1)} %param.33), kind=kOutput, calls=%fused_computation.31 | convolution fusion | flops 7523008512 | bytes 24117248 | tf_op jit(solution)/shard_map/dot_general | solution.py:39
  978.7 90.6 %all_to_all.22 = bf16[8,16,8,3584]{3,2,1,0:T(8,128)(2,1)S(1)} all-to-all(bf16[8,16,8,3584]{3,2,1,0:T(8,128)(2,1)} %bitcast.99), channel_id=1, replica_groups=mesh['node'=8,'dev'=16] {'node'}, dimensions={0} | all-to-all | bytes 14680064 | tf_op jit(solution)/shard_map/all_to_all | solution.py:164
  1069.3 3.8 copy.131
  1073.2 5.0 all-to-all-start.3
  1079.8 122.6 %all-to-all-done.3 = bf16[8,16,8,3584]{3,2,0,1:T(8,128)(2,1)} async-done(((bf16[8,16,8,3584]{3,2,0,1:T(8,128)(2,1)}), bf16[8,16,8,3584]{3,2,0,1:T(8,128)(2,1)}, u32[]{:S(2)}, u32[]{:S(2)}) %all-to-all-start.3) | async-done | bytes 7340064 | tf_op jit(solution)/shard_map/all_to_all | solution.py:163
  1202.4 5.2 convert_reduce_fusion
  1207.6 9.0 fusion.40
  (133 shorter events, 38.5 us)
Async XLA Ops:
  7.2 681.4 %copy-start = (bf16[256,3584]{1,0:T(8,128)(2,1)S(1)}, bf16[256,3584]{1,0:T(8,128)(2,1)}, u32[]{:S(2)}) copy-start(bf16[256,3584]{1,0:T(8,128)(2,1)} %param.28) | copy-start | bytes 5505028
  7.2 5.8 copy-start.10
  7.2 5.9 copy-start.11
  7.2 38.6 %all-gather.2.cloned.1.call-start = ((), (), s32[]{:S(2)}) async-start(), calls=%async_computation.5 | async-start | bytes 4718592 | tf_op jit(solution)/shard_map/all_gather | solution.py:104
  45.8 6.4 copy-start.5
  52.3 8.2 copy-start.9
  52.3 8.1 copy-start.15
  60.4 147.6 %all-reduce.2.cloned.1.call-start = ((), (), s32[]{:S(2)}) async-start(), calls=%async_computation.7 | async-start | bytes 327680 | tf_op jit(solution)/shard_map/while/body/eval_jaxpr/psum | solution.py:15
  208.0 2.7 copy-start.3
  212.2 1.3 copy-start.4
  213.5 145.9 %all-reduce.2.cloned.1.call-start = ((), (), s32[]{:S(2)}) async-start(), calls=%async_computation.7 | async-start | bytes 327680 | tf_op jit(solution)/shard_map/while/body/eval_jaxpr/psum | solution.py:15
  359.4 2.7 copy-start.3
  363.6 1.3 copy-start.4
  364.9 145.6 %all-reduce.2.cloned.1.call-start = ((), (), s32[]{:S(2)}) async-start(), calls=%async_computation.7 | async-start | bytes 327680 | tf_op jit(solution)/shard_map/while/body/eval_jaxpr/psum | solution.py:15
  510.6 2.7 copy-start.3
  514.7 1.3 copy-start.4
  516.1 145.6 %all-reduce.2.cloned.1.call-start = ((), (), s32[]{:S(2)}) async-start(), calls=%async_computation.7 | async-start | bytes 327680 | tf_op jit(solution)/shard_map/while/body/eval_jaxpr/psum | solution.py:15
  661.7 2.7 copy-start.3
  665.9 1.3 copy-start.4
  667.2 97.4 %reduce-scatter.2.cloned.1.call-start = ((), (), s32[]{:S(2)}) async-start(), calls=%async_computation.6 | async-start | bytes 3899392 | tf_op jit(solution)/shard_map/reduce_scatter | solution.py:114
  667.2 10.7 copy-start.2
  677.9 9.0 copy-start.14
  688.6 3.0 copy-start.13
  691.6 5.5 copy-start.12
  691.6 73.1 %copy-start.8 = (bf16[32,3584]{1,0:T(8,128)(2,1)S(1)}, bf16[32,3584]{1,0:T(8,128)(2,1)}, u32[]{:S(2)}) copy-start(bf16[32,3584]{1,0:T(8,128)(2,1)} %param.29) | copy-start | bytes 688132
  765.7 313.1 %copy-start.6 = (bf16[32,3584]{1,0:T(8,128)(2,1)}, bf16[32,3584]{1,0:T(8,128)(2,1)S(1)}, u32[]{:S(2)}) copy-start(bf16[32,3584]{1,0:T(8,128)(2,1)S(1)} %get-tuple-element.354) | copy-start | bytes 688132
  1073.2 5.7 copy-start.7
  1073.2 129.3 %all-to-all-start.3 = ((bf16[8,16,8,3584]{3,2,0,1:T(8,128)(2,1)}), bf16[8,16,8,3584]{3,2,0,1:T(8,128)(2,1)}, u32[]{:S(2)}, u32[]{:S(2)}) async-start(bf16[8,16,8,3584]{3,2,0,1:T(8,128)(2,1)} %copy.131), calls=%async_computation.4 | async-start | bytes 14680064 | tf_op jit(solution)/shard_map/all_to_all | solution.py:163
  1202.4 14.2 %copy-start.1 = (bf16[256,3584]{1,0:T(8,128)(2,1)S(1)}, bf16[256,3584]{1,0:T(8,128)(2,1)}, u32[]{:S(2)}) copy-start(bf16[256,3584]{1,0:T(8,128)(2,1)} %param.28) | copy-start | bytes 5505028
Sparse Core Ops, SparseCore 0:
  9.8 36.0 all-gather.1
  66.6 141.3 all-reduce.1
  219.6 139.7 all-reduce.1
  370.7 139.7 all-reduce.1
  521.9 139.7 all-reduce.1
  691.7 72.8 reduce-scatter.1
where the time goes:
time: 1230 us; the launch traced here: 1220 us
  waiting for transfers between devices  772 us (63%)
  blocking collectives  284 us (23%)
  matrix products  78.8 us (6%)
  local copies, waits for them, and re-layouts  34.4 us (3%)
  other arithmetic  24.2 us (2%)
  between operations  14.4 us (1%)
    psum x4, waiting for transfers between devices, broadcast(): return lax.psum(kept, axis)  565 us
    all_to_all x1, waiting for transfers between devices, on_device(): lax.all_to_all(lax.all_to_all(served, 'node', split_axis=0, concat_axis=0...  123 us
    all_to_all x1, blocking collectives, on_device(): lax.all_to_all(served, 'node', split_axis=0, concat_axis=0, tiled=True)  90.6 us
    all_to_all x1, blocking collectives, on_device(): lax.all_to_all(outgoing, 'node', split_axis=0, concat_axis=0, tiled=True)  90.1 us
    all_to_all x1, blocking collectives, on_device(): lax.all_to_all(lax.all_to_all(outgoing, 'node', split_axis=0, concat_axis...  86.6 us
    reduce_scatter x1, waiting for transfers between devices, on_device(): lax.psum_scatter(jnp.dot(head_out, out_proj, preferred_element_type=jnp.f...  67.6 us
  transfers between devices with their start and end apart: 7, of which 7 were waited for; matrix products, arithmetic and copies ran while one was open for 1% of the time, Pallas kernels for 0%

commit v1 on v0

v1 whole, which is shorter than its diff:
```python
import functools
import math

import jax
import jax.numpy as jnp
from jax import lax
from jax.experimental import pallas as pl
from jax.experimental.pallas import tpu as pltpu
from jax.sharding import PartitionSpec as P

ROUTE_SCALE = 2.827
NORM_EPS = 1e-06
FAR_BELOW = -1e30
ALL = ("node", "dev")
VMEM_BYTES = 60 * 1024 * 1024
F32 = jnp.float32
BF16 = jnp.bfloat16


def dot(a, b, dims=(((1,), (0,)), ((), ()))):
    return lax.dot_general(a, b, dims, preferred_element_type=F32)


def swap(value, axis):
    return lax.all_to_all(value, axis, split_axis=0, concat_axis=0, tiled=True)


def attention_kernel(
    q_nope, q_rope, keys, prefix, absorb_k, absorb_v, out_proj, terms, q_lat, top, total, mixed
):
    heads, nope, rank = absorb_k.shape
    tokens = q_nope.shape[0]
    rope = q_rope.shape[1] // heads
    block = prefix.shape[0]
    span = block - rope
    scale = 1.0 / math.sqrt(nope + rope)
    node = lax.axis_index("node")
    first = pl.program_id(0) * tokens

    for h in range(heads):
        part = dot(q_nope[:, h * nope : (h + 1) * nope], absorb_k[h])
        q_lat[h * tokens : (h + 1) * tokens] = part.astype(BF16)

    def fold(lat, rot, mask, fresh):
        for h in range(heads):
            rows = pl.ds(h * tokens, tokens)
            scores = dot(q_lat[rows], lat, (((1,), (1,)), ((), ())))
            scores = scores + dot(q_rope[:, h * rope : (h + 1) * rope], rot)
            if mask is not None:
                scores = jnp.where(mask, scores, FAR_BELOW)
            row_top = jnp.max(scores, axis=1, keepdims=True)
            if not fresh:
                row_top = jnp.maximum(row_top, top[rows])
            exp_scores = jnp.exp((scores - row_top) * scale)
            row_sum = jnp.sum(exp_scores, axis=1, keepdims=True)
            mix = dot(exp_scores.astype(BF16), lat)
            if not fresh:
                shrink = jnp.exp((top[rows] - row_top) * scale)
                row_sum = row_sum + total[rows] * shrink
                mix = mix + mixed[rows] * shrink
            top[rows] = row_top
            total[rows] = row_sum
            mixed[rows] = mix

    fold(prefix[:span], prefix[span:], None, True)

    def earlier(j, carry):
        at = pl.multiple_of(j * block, 64)
        fold(keys[pl.ds(at, span)], keys[pl.ds(at + span, rope)], None, False)
        return carry

    lax.fori_loop(0, node, earlier, 0)
    at = pl.multiple_of(node * block, 64)
    q_pos = first + lax.broadcasted_iota(jnp.int32, (tokens, span), 0)
    key_pos = lax.broadcasted_iota(jnp.int32, (tokens, span), 1)
    fold(keys[pl.ds(at, span)], keys[pl.ds(at + span, rope)], key_pos <= q_pos, False)

    outs = []
    for h in range(heads):
        rows = pl.ds(h * tokens, tokens)
        head_lat = (mixed[rows] / total[rows]).astype(BF16)
        outs.append(dot(head_lat, absorb_v[h]).astype(BF16))
    head_out = jnp.concatenate(outs, axis=1)
    width = out_proj.shape[1]
    step = 512
    for c in range(0, width, step):
        terms[:, c : c + step] = dot(head_out, out_proj[:, c : c + step]).astype(BF16)


def attention(q_nope, q_rope, keys, prefix, absorb_k, absorb_v, out_proj):
    rows = q_nope.shape[0]
    tile = min(256, rows)
    heads, nope, rank = absorb_k.shape
    width = out_proj.shape[1]
    whole = pl.BlockSpec(memory_space=pltpu.VMEM)
    return pl.pallas_call(
        attention_kernel,
        grid=(rows // tile,),
        out_shape=jax.ShapeDtypeStruct((rows, width), BF16),
        in_specs=[
            pl.BlockSpec((tile, q_nope.shape[1]), lambda i: (i, 0)),
            pl.BlockSpec((tile, q_rope.shape[1]), lambda i: (i, 0)),
            whole,
            whole,
            whole,
            whole,
            whole,
        ],
        out_specs=pl.BlockSpec((tile, width), lambda i: (i, 0)),
        scratch_shapes=[
            pltpu.VMEM((heads * tile, rank), BF16),
            pltpu.VMEM((heads * tile, 1), F32),
            pltpu.VMEM((heads * tile, 1), F32),
            pltpu.VMEM((heads * tile, rank), F32),
        ],
        compiler_params=pltpu.CompilerParams(vmem_limit_bytes=VMEM_BYTES),
        name="attention",
    )(q_nope, q_rope, keys, prefix, absorb_k, absorb_v, out_proj)


def route_kernel(terms, residual, gain, router, ids, attended, outgoing, shares, *, shards, cap):
    groups, tokens, width = terms.shape
    experts = router.shape[1]
    top_k = ids.shape[1]
    acc = terms[0].astype(F32)
    for g in range(1, groups):
        acc = acc + terms[g].astype(F32)
    stream = (residual[...].astype(F32) + acc).astype(BF16)
    attended[...] = stream
    stream = stream.astype(F32)
    mean = jnp.mean(stream * stream, axis=1, keepdims=True)
    normed = (stream * lax.rsqrt(mean + NORM_EPS) * gain[...].astype(F32)).astype(BF16)
    logits = dot(normed, router[...])
    expert = lax.broadcasted_iota(jnp.int32, (tokens, experts), 1)
    hits = [ids[:, j : j + 1] == expert for j in range(top_k)]
    gates = [
        jax.nn.sigmoid(jnp.sum(jnp.where(hit, logits, 0.0), axis=1, keepdims=True)) for hit in hits
    ]
    gate_sum = functools.reduce(lambda a, b: a + b, gates)
    weight = jnp.zeros((tokens, experts), F32)
    used = jnp.zeros((tokens, experts), F32)
    for hit, gate in zip(hits, gates):
        weight = jnp.where(hit, ROUTE_SCALE * gate / gate_sum, weight)
        used = jnp.where(hit, 1.0, used)
    weight = weight.astype(BF16)
    used = used.astype(BF16)
    below = lax.broadcasted_iota(jnp.int32, (tokens, tokens), 1) < lax.broadcasted_iota(
        jnp.int32, (tokens, tokens), 0
    )
    rank = dot(below.astype(BF16), used).astype(BF16)
    slots = experts * shards * cap
    owner = lax.broadcasted_iota(jnp.int32, (experts, slots), 1) // (shards * cap)
    spread = (owner == lax.broadcasted_iota(jnp.int32, (experts, slots), 0)).astype(BF16)
    slot = lax.broadcasted_iota(jnp.int32, (tokens, slots), 1) % cap
    filled = (dot(used, spread) > 0.5) & (dot(rank, spread) == slot.astype(F32))
    shares[...] = jnp.where(filled, dot(weight, spread), 0.0).astype(BF16)
    fill = filled.astype(F32).astype(BF16)
    step = 512
    for c in range(0, width, step):
        outgoing[:, c : c + step] = dot(
            fill, normed[:, c : c + step], (((0,), (0,)), ((), ()))
        ).astype(BF16)


def route(terms, residual, gain, router, ids, shards, cap):
    tokens, width = residual.shape
    slots = router.shape[1] * shards * cap
    whole = pl.BlockSpec(memory_space=pltpu.VMEM)
    return pl.pallas_call(
        functools.partial(route_kernel, shards=shards, cap=cap),
        out_shape=(
            jax.ShapeDtypeStruct((tokens, width), BF16),
            jax.ShapeDtypeStruct((slots, width), BF16),
            jax.ShapeDtypeStruct((tokens, slots), BF16),
        ),
        in_specs=[whole] * 5,
        out_specs=(whole, whole, whole),
        compiler_params=pltpu.CompilerParams(vmem_limit_bytes=VMEM_BYTES),
        name="route",
    )(terms, residual, gain, router, ids)


def expert_kernel(rows, gate, up, down, out):
    x = rows[...]
    gate_act = dot(x, gate[...])
    up_act = dot(x, up[...])
    hidden = (jax.nn.silu(gate_act) * up_act).astype(BF16)
    width = down.shape[1]
    step = 512
    for c in range(0, width, step):
        out[:, c : c + step] = dot(hidden, down[:, c : c + step]).astype(BF16)


def experts(rows, gate, up, down):
    count, width = rows.shape
    tile = min(256, count)
    whole = pl.BlockSpec(memory_space=pltpu.VMEM)
    return pl.pallas_call(
        expert_kernel,
        grid=(count // tile,),
        out_shape=jax.ShapeDtypeStruct((count, width), BF16),
        in_specs=[pl.BlockSpec((tile, width), lambda i: (i, 0)), whole, whole, whole],
        out_specs=pl.BlockSpec((tile, width), lambda i: (i, 0)),
        compiler_params=pltpu.CompilerParams(vmem_limit_bytes=VMEM_BYTES),
        name="experts",
    )(rows, gate, up, down)


def combine_kernel(shares, returned, out):
    out[...] = dot(shares[...], returned[...]).astype(BF16)


def combine(shares, returned):
    tokens, slots = shares.shape
    width = returned.shape[1]
    tile = 512
    return pl.pallas_call(
        combine_kernel,
        grid=(width // tile,),
        out_shape=jax.ShapeDtypeStruct((tokens, width), BF16),
        in_specs=[
            pl.BlockSpec((tokens, slots), lambda i: (0, 0)),
            pl.BlockSpec((slots, tile), lambda i: (0, i)),
        ],
        out_specs=pl.BlockSpec((tokens, tile), lambda i: (0, i)),
        compiler_params=pltpu.CompilerParams(vmem_limit_bytes=VMEM_BYTES),
        name="combine",
    )(shares, returned)


def listed_prefix(pool_latent, pool_rope, block_table, devices):
    held, block, rank = pool_latent.shape
    rope = pool_rope.shape[2]
    count = block_table.shape[0]
    me = lax.axis_index(ALL)
    mine = block_table // held == me
    slot = block_table % held
    lat = jnp.where(mine[:, None, None], pool_latent[slot], 0).astype(BF16)
    rot = jnp.where(mine[:, None, None], pool_rope[slot], 0).astype(BF16)
    lat = lat.reshape(count * block, rank)
    rot = jnp.transpose(rot, (2, 0, 1)).reshape(rope * count * block // rank, rank)
    both = jnp.concatenate([lat, rot], 0)
    parts = both.reshape(devices, -1, 128)
    arrived = swap(parts, ALL)
    piece = jnp.sum(arrived.astype(F32), axis=0).astype(BF16)
    return swap(jnp.broadcast_to(piece[None], parts.shape), ALL).reshape(both.shape)


def on_device(
    q_nope,
    q_rope,
    kv_latent,
    k_rope,
    pool_latent,
    pool_rope,
    block_table,
    absorb_k,
    absorb_v,
    out_proj,
    residual,
    norm_gain,
    router,
    expert_ids,
    expert_gate,
    expert_up,
    expert_down,
):
    node_count = lax.axis_size("node")
    dev_count = lax.axis_size("dev")
    devices = node_count * dev_count
    tokens, width = residual.shape
    expert_count = router.shape[1]
    shards = devices // expert_count
    cap = max(2, 2 * tokens * expert_ids.shape[1] // expert_count)

    keys_here = jnp.concatenate([kv_latent, k_rope.T], 0)
    keys = lax.all_gather(keys_here, "node", axis=0, tiled=True)
    prefix = listed_prefix(pool_latent, pool_rope, block_table, devices)

    terms = attention(q_nope, q_rope, keys, prefix, absorb_k, absorb_v, out_proj)
    terms = swap(terms.reshape(dev_count, tokens, width), "dev")
    attended, outgoing, shares = route(
        terms, residual, norm_gain.reshape(1, width), router, expert_ids, shards, cap
    )
    arrived = swap(outgoing.reshape(devices, cap, width), ALL)
    served = experts(
        arrived.reshape(devices * cap, width), expert_gate[0], expert_up[0], expert_down[0]
    )
    returned = swap(served.reshape(devices, cap, width), ALL)
    return attended, combine(shares, returned.reshape(devices * cap, width))


def solution(mesh):
    placed = (
        P("node", "dev"),
        P("node", "dev"),
        P("node", None),
        P("node", None),
        P(ALL, None, None),
        P(ALL, None, None),
        P(),
        P("dev", None, None),
        P("dev", None, None),
        P("dev", None),
        P(ALL, None),
        P(),
        P(),
        P(ALL, None),
        P(ALL, None, None),
        P(ALL, None, None),
        P(ALL, None, None),
    )
    return jax.shard_map(
        on_device,
        mesh=mesh,
        in_specs=placed,
        out_specs=(P(ALL, None), P(ALL, None)),
        check_vma=False,
    )
```

time: 1230 us -> 385 us (0.31)
  waiting for transfers between devices: 772 us -> 44.9 us
  matrix products: 78.8 us -> 0 us
  Pallas kernels: 0 us -> 48.3 us
  local copies, waits for them, and re-layouts: 34.4 us -> 6.36 us
  blocking collectives: 284 us -> 262 us
  other arithmetic: 24.2 us -> 3.72 us
    psum x4 -> x0, waiting for transfers between devices: 565 us -> none  [broadcast(): return lax.psum(kept, axis)]
    dot_general x23 -> x0, matrix products: 78.8 us -> none  [the longest x1 14.7 us: expert_ffn(): jnp.dot(hidden, down_rows, preferred_element_type=jnp.float32)]
    all_to_all x1, waiting for transfers between devices: 123 us -> 44.8 us  [swap(): return lax.all_to_all(value, axis, split_axis=0, concat_axis=0, tiled=True)]
    reduce_scatter x1 -> x0, waiting for transfers between devices: 67.6 us -> none  [on_device(): lax.psum_scatter(jnp.dot(head_out, out_proj, preferred_element_type=jnp.f...]
    pallas_call x0 -> x4, Pallas kernels: none -> 48.3 us  [the longest x1 18.4 us: experts(): pl.pallas_call(expert_kernel, grid=(count // tile,), out_shape=jax.ShapeD...]
    all_gather x1, waiting for transfers between devices: 16.5 us -> 0.01 us  [on_device(): keys = lax.all_gather(keys_here, 'node', axis=0, tiled=True)]
    reduce_sum x10 -> x1, other arithmetic: 16.4 us -> 0.16 us  [listed_prefix(): piece = jnp.sum(arrived.astype(F32), axis=0).astype(BF16)]
    all_gather x1 -> x0, blocking collectives: 16.3 us -> none  [on_device(): piece_rot = lax.all_gather(k_rope, 'node', axis=0, tiled=True)]
  transfers between devices with their start and end apart: 7 -> 2, of which waited for: 7 -> 1; matrix products, arithmetic and copies ran while one was open for 1% -> 2% of each run, Pallas kernels for 0% -> 0%
where the time goes in v1:
time: 385 us; the launch traced here: 384 us
  blocking collectives  262 us (68%)
  Pallas kernels  48.3 us (13%)
  waiting for transfers between devices  44.9 us (12%)
  between operations  14.1 us (4%)
  local copies, waits for them, and re-layouts  6.36 us (2%)
  starting transfers between devices  4.69 us (1%)
    all_to_all x4, blocking collectives, swap(): return lax.all_to_all(value, axis, split_axis=0, concat_axis=0, tiled=True)  262 us
    all_to_all x1, waiting for transfers between devices, swap(): return lax.all_to_all(value, axis, split_axis=0, concat_axis=0, tiled=True)  44.8 us
    pallas_call x1, Pallas kernels, experts(): pl.pallas_call(expert_kernel, grid=(count // tile,), out_shape=jax.ShapeD...  18.4 us
    pallas_call x1, Pallas kernels, attention(): pl.pallas_call(attention_kernel, grid=(rows // tile,), out_shape=jax.Shap...  14.5 us
    pallas_call x1, Pallas kernels, route(): pl.pallas_call(functools.partial(route_kernel, shards=shards, cap=cap), o...  8.5 us
  transfers between devices with their start and end apart: 2, of which 1 were waited for; matrix products, arithmetic and copies ran while one was open for 2% of the time, Pallas kernels for 0%

profile of v1, /device:TPU:1, one launch (start us, length us, event | category | flops | bytes accessed | tf_op | source)
XLA Modules:
  0.0 384.2 jit_solution(1607152044748139775)
XLA Ops:
  7.2 0.0 copy-start
  7.2 0.0 all-gather.2.cloned.1.call-start
  7.2 2.0 pad_maximum_fusion
  9.2 0.0 all-gather.2.cloned.1.call-update
  9.2 0.7 compare_select_fusion
  9.9 1.3 gather_fusion.1
  11.2 0.0 copy-done
  11.2 0.6 gather_fusion
  11.8 0.7 fusion
  12.5 0.1 broadcast_bitcast_fusion
  12.6 0.1 copy_bitcast_fusion
  12.6 0.1 bitcast_select_fusion
  12.8 0.4 reshape.37
  13.3 35.2 %all_to_all.25 = bf16[128,18,128]{2,1,0:T(8,128)(2,1)S(1)} all-to-all(bf16[128,18,128]{2,1,0:T(8,128)(2,1)S(1)} %reshape.37), channel_id=1, replica_groups=mesh['node'=8,'dev'=16] {'node','dev'}, dimensions={0} | all-to-all | bytes 1179648 | tf_op jit(solution)/shard_map/all_to_all | solution.py:25
  48.5 0.2 reduce_sum.12
  48.6 0.1 broadcast_in_dim.47
  48.7 21.3 %all_to_all.26 = bf16[128,18,128]{2,1,0:T(8,128)(2,1)S(1)} all-to-all(bf16[128,18,128]{2,1,0:T(8,128)(2,1)S(1)} %broadcast_in_dim.47), channel_id=1, replica_groups=mesh['node'=8,'dev'=16] {'node','dev'}, dimensions={0} | all-to-all | bytes 1179648 | tf_op jit(solution)/shard_map/all_to_all | solution.py:25
  70.0 1.3 reshape.38.prefix
  71.3 14.5 %attention.1 = bf16[512,3584]{1,0:T(8,128)(2,1)} custom-call(bf16[512,256]{1,0:T(8,128)(2,1)} %q_nope.1, bf16[512,128]{1,0:T(8,128)(2,1)} %q_rope.1, bf16[4608,512]{1,0:T(8,128)(2,1)} %all-gather.2.cloned.1.call-done.keys, bf16[576,512]{1,0:T(8,128)(2,1)} %reshape.38.prefix, bf16[2,128,512]{2,1,0:T(8,128)(2,1)} %absorb_k.1, bf16[2,512,128]{2,1,0:T(8,128)(2,1)} %absorb_v.1, ...), custom_call_target="tpu_custom_call" | custom-call | tf_op jit(solution)/shard_map/attention/pallas_call | solution.py:96
  85.8 0.0 copy-start.1
  85.8 4.6 %all-to-all-start.2 = ((bf16[16,32,3584]{2,1,0:T(8,128)(2,1)}), bf16[16,32,3584]{2,1,0:T(8,128)(2,1)}, u32[]{:S(2)}, u32[]{:S(2)}) async-start(bf16[16,32,3584]{2,1,0:T(8,128)(2,1)} %bitcast.22), calls=%async_computation.2 | async-start | bytes 7340032 | tf_op jit(solution)/shard_map/all_to_all | solution.py:25
  90.5 0.0 copy-done.2
  90.5 0.6 reshape.40.gain
  91.1 0.0 copy-done.3
  91.1 0.7 copy.23.ids
  91.8 1.2 copy.22.router
  93.0 44.8 %all-to-all-done.2.terms = bf16[16,32,3584]{2,1,0:T(8,128)(2,1)} async-done(((bf16[16,32,3584]{2,1,0:T(8,128)(2,1)}), bf16[16,32,3584]{2,1,0:T(8,128)(2,1)}, u32[]{:S(2)}, u32[]{:S(2)}) %all-to-all-start.2) | async-done | bytes 3670048 | tf_op jit(solution)/shard_map/all_to_all | solution.py:25
  137.9 8.5 %route.1 = (bf16[32,3584]{1,0:T(8,128)(2,1)}, bf16[1024,3584]{1,0:T(8,128)(2,1)}, bf16[32,1024]{1,0:T(8,128)(2,1)}) custom-call(bf16[16,32,3584]{2,1,0:T(8,128)(2,1)} %all-to-all-done.2.terms, bf16[32,3584]{1,0:T(8,128)(2,1)} %residual.1, bf16[1,3584]{1,0:T(2,128)(2,1)} %reshape.40.gain, bf16[3584,64]{1,0:T(8,128)(2,1)} %copy.22.router, s32[32,8]{1,0:T(8,128)} %copy.23.ids), custom_call_target="tpu_custom_call" | custom-call | tf_op jit(solution)/shard_map/route/pallas_call | solution.py:169
  146.4 112.6 %all_to_all.27 = bf16[128,8,3584]{2,1,0:T(8,128)(2,1)} all-to-all(bf16[128,8,3584]{2,1,0:T(8,128)(2,1)} %bitcast.23), channel_id=1, replica_groups=mesh['node'=8,'dev'=16] {'node','dev'}, dimensions={0} | all-to-all | bytes 14680064 | tf_op jit(solution)/shard_map/all_to_all | solution.py:25
  259.0 18.4 %experts.1 = bf16[1024,3584]{1,0:T(8,128)(2,1)} custom-call(bf16[1024,3584]{1,0:T(8,128)(2,1)} %bitcast.20, bf16[3584,512]{1,0:T(8,128)(2,1)} %bitcast.24, bf16[3584,512]{1,0:T(8,128)(2,1)} %bitcast.25, bf16[512,3584]{1,0:T(8,128)(2,1)} %bitcast.26), custom_call_target="tpu_custom_call" | custom-call | tf_op jit(solution)/shard_map/experts/pallas_call | solution.py:198
  277.4 93.1 %all_to_all.28 = bf16[128,8,3584]{2,1,0:T(8,128)(2,1)} all-to-all(bf16[128,8,3584]{2,1,0:T(8,128)(2,1)} %bitcast.21), channel_id=1, replica_groups=mesh['node'=8,'dev'=16] {'node','dev'}, dimensions={0} | all-to-all | bytes 14680064 | tf_op jit(solution)/shard_map/all_to_all | solution.py:25
  370.5 6.9 %combine.1 = bf16[32,3584]{1,0:T(8,128)(2,1)} custom-call(bf16[32,1024]{1,0:T(8,128)(2,1)} %get-tuple-element.6.shares, bf16[1024,3584]{1,0:T(8,128)(2,1)} %bitcast.19), custom_call_target="tpu_custom_call" | custom-call | tf_op jit(solution)/shard_map/combine/pallas_call | solution.py:217
  (6 shorter events, 0.1 us)
Async XLA Ops:
  7.2 4.1 %copy-start = (bf16[2,128,512]{2,1,0:T(8,128)(2,1)S(1)}, bf16[2,128,512]{2,1,0:T(8,128)(2,1)}, u32[]{:S(2)}) copy-start(bf16[2,128,512]{2,1,0:T(8,128)(2,1)} %param.21) | copy-start | bytes 786436
  7.2 64.2 %all-gather.2.cloned.1.call-start = ((), (), s32[]{:S(2)}) async-start(), calls=%async_computation.5 | async-start | bytes 5308416 | tf_op jit(solution)/shard_map/all_gather | solution.py:277
  85.8 4.7 %copy-start.2 = (bf16[3584]{0:T(1024)(128)(2,1)S(1)}, bf16[3584]{0:T(1024)(128)(2,1)}, u32[]{:S(2)}) copy-start(bf16[3584]{0:T(1024)(128)(2,1)} %param.28) | copy-start | bytes 21508
  85.8 5.3 %copy-start.3 = (s32[32,8]{0,1:T(8,128)S(1)}, s32[32,8]{0,1:T(8,128)}, u32[]{:S(2)}) copy-start(s32[32,8]{0,1:T(8,128)} %param.30) | copy-start | bytes 3076
  85.8 6.0 %copy-start.1 = (bf16[3584,64]{0,1:T(8,128)(2,1)S(1)}, bf16[3584,64]{0,1:T(8,128)(2,1)}, u32[]{:S(2)}) copy-start(bf16[3584,64]{0,1:T(8,128)(2,1)} %param.29) | copy-start | bytes 1376260
  85.8 52.0 %all-to-all-start.2 = ((bf16[16,32,3584]{2,1,0:T(8,128)(2,1)}), bf16[16,32,3584]{2,1,0:T(8,128)(2,1)}, u32[]{:S(2)}, u32[]{:S(2)}) async-start(bf16[16,32,3584]{2,1,0:T(8,128)(2,1)} %bitcast.22), calls=%async_computation.2 | async-start | bytes 7340032 | tf_op jit(solution)/shard_map/all_to_all | solution.py:25
Sparse Core Ops, SparseCore 0:
  9.7 46.3 all-gather.1

commit v2 on v1

--- a/solution.py
+++ b/solution.py
@@ -118,7 +118,16 @@
     )(q_nope, q_rope, keys, prefix, absorb_k, absorb_v, out_proj)
 
 
-def route_kernel(terms, residual, gain, router, ids, attended, outgoing, shares, *, shards, cap):
+def slot_place(column, nodes, cap, experts):
+    half = cap // 2
+    devs = 2 * experts // nodes
+    device, low = column // half, column % half
+    node, dev = device // devs, device % devs
+    expert = (experts // nodes) * (node // 2 * 2 + dev % 2) + dev // 2
+    return expert, node % 2 * half + low
+
+
+def route_kernel(terms, residual, gain, router, ids, attended, outgoing, shares, *, nodes, cap):
     groups, tokens, width = terms.shape
     experts = router.shape[1]
     top_k = ids.shape[1]
@@ -148,10 +157,10 @@
         jnp.int32, (tokens, tokens), 0
     )
     rank = dot(below.astype(BF16), used).astype(BF16)
-    slots = experts * shards * cap
-    owner = lax.broadcasted_iota(jnp.int32, (experts, slots), 1) // (shards * cap)
+    slots = experts * cap
+    owner, _ = slot_place(lax.broadcasted_iota(jnp.int32, (experts, slots), 1), nodes, cap, experts)
     spread = (owner == lax.broadcasted_iota(jnp.int32, (experts, slots), 0)).astype(BF16)
-    slot = lax.broadcasted_iota(jnp.int32, (tokens, slots), 1) % cap
+    _, slot = slot_place(lax.broadcasted_iota(jnp.int32, (tokens, slots), 1), nodes, cap, experts)
     filled = (dot(used, spread) > 0.5) & (dot(rank, spread) == slot.astype(F32))
     shares[...] = jnp.where(filled, dot(weight, spread), 0.0).astype(BF16)
     fill = filled.astype(F32).astype(BF16)
@@ -162,12 +171,12 @@
         ).astype(BF16)
 
 
-def route(terms, residual, gain, router, ids, shards, cap):
+def route(terms, residual, gain, router, ids, nodes, cap):
     tokens, width = residual.shape
-    slots = router.shape[1] * shards * cap
+    slots = router.shape[1] * cap
     whole = pl.BlockSpec(memory_space=pltpu.VMEM)
     return pl.pallas_call(
-        functools.partial(route_kernel, shards=shards, cap=cap),
+        functools.partial(route_kernel, nodes=nodes, cap=cap),
         out_shape=(
             jax.ShapeDtypeStruct((tokens, width), BF16),
             jax.ShapeDtypeStruct((slots, width), BF16),
@@ -180,30 +189,79 @@
     )(terms, residual, gain, router, ids)
 
 
-def expert_kernel(rows, gate, up, down, out):
+def expert_kernel(rows, *refs):
+    sources, (out, gates, ups, downs, sems) = refs[:12], refs[12:]
+    node, dev = lax.axis_index("node"), lax.axis_index("dev")
+    keeper = node % 2 == dev % 2
+    own, crossed, twin, twin_crossed = (sources[3 * i : 3 * i + 3] for i in range(4))
+    slots = (gates, ups, downs)
+
+    def copy(source, share, part):
+        return pltpu.make_async_copy(
+            source[part].at[0], slots[part].at[share], sems.at[share * 3 + part]
+        )
+
+    order = ((0, 0), (0, 1), (1, 0), (1, 1), (0, 2), (1, 2))
+
+    @pl.when(keeper)
+    def _():
+        for share, part in order:
+            copy((own, crossed)[share], share, part).start()
+
+    @pl.when(jnp.logical_not(keeper))
+    def _():
+        for share, part in order:
+            copy((twin, twin_crossed)[share], share, part).start()
+
     x = rows[...]
-    gate_act = dot(x, gate[...])
-    up_act = dot(x, up[...])
-    hidden = (jax.nn.silu(gate_act) * up_act).astype(BF16)
-    width = down.shape[1]
+    hidden = []
+    for share in range(2):
+        copy(own, share, 0).wait()
+        gate_act = dot(x, gates[share])
+        copy(own, share, 1).wait()
+        up_act = dot(x, ups[share])
+        hidden.append((jax.nn.silu(gate_act) * up_act).astype(BF16))
+    for share in range(2):
+        copy(own, share, 2).wait()
+    width = out.shape[1]
     step = 512
     for c in range(0, width, step):
-        out[:, c : c + step] = dot(hidden, down[:, c : c + step]).astype(BF16)
-
-
-def experts(rows, gate, up, down):
+        part = dot(hidden[0], downs[0, :, c : c + step])
+        part = part + dot(hidden[1], downs[1, :, c : c + step])
+        out[:, c : c + step] = part.astype(BF16)
+
+
+def experts(rows, sources):
     count, width = rows.shape
-    tile = min(256, count)
+    hidden = sources[0].shape[2]
     whole = pl.BlockSpec(memory_space=pltpu.VMEM)
     return pl.pallas_call(
         expert_kernel,
-        grid=(count // tile,),
         out_shape=jax.ShapeDtypeStruct((count, width), BF16),
-        in_specs=[pl.BlockSpec((tile, width), lambda i: (i, 0)), whole, whole, whole],
-        out_specs=pl.BlockSpec((tile, width), lambda i: (i, 0)),
+        in_specs=[whole] + [pl.BlockSpec(memory_space=pl.ANY)] * 12,
+        out_specs=whole,
+        scratch_shapes=[
+            pltpu.VMEM((2, width, hidden), BF16),
+            pltpu.VMEM((2, width, hidden), BF16),
+            pltpu.VMEM((2, hidden, width), BF16),
+            pltpu.SemaphoreType.DMA((6,)),
+        ],
         compiler_params=pltpu.CompilerParams(vmem_limit_bytes=VMEM_BYTES),
         name="experts",
-    )(rows, gate, up, down)
+    )(rows, *sources)
+
+
+def placed_weights(weights, nodes, devs):
+    across, beside = [], []
+    for node in range(nodes):
+        for dev in range(devs):
+            if node % 2 == dev % 2:
+                across.append((node * devs + (dev ^ 1), node * devs + dev))
+                beside.append((node * devs + dev, (node ^ 1) * devs + dev))
+    crossed = [lax.ppermute(w, ALL, across) for w in weights]
+    twin = [lax.ppermute(w, ALL, beside) for w in weights]
+    twin_crossed = [lax.ppermute(w, ALL, beside) for w in crossed]
+    return list(weights) + crossed + twin + twin_crossed
 
 
 def combine_kernel(shares, returned, out):
@@ -270,9 +328,9 @@
     devices = node_count * dev_count
     tokens, width = residual.shape
     expert_count = router.shape[1]
-    shards = devices // expert_count
     cap = max(2, 2 * tokens * expert_ids.shape[1] // expert_count)
 
+    sources = placed_weights((expert_gate, expert_up, expert_down), node_count, dev_count)
     keys_here = jnp.concatenate([kv_latent, k_rope.T], 0)
     keys = lax.all_gather(keys_here, "node", axis=0, tiled=True)
     prefix = listed_prefix(pool_latent, pool_rope, block_table, devices)
@@ -280,14 +338,13 @@
     terms = attention(q_nope, q_rope, keys, prefix, absorb_k, absorb_v, out_proj)
     terms = swap(terms.reshape(dev_count, tokens, width), "dev")
     attended, outgoing, shares = route(
-        terms, residual, norm_gain.reshape(1, width), router, expert_ids, shards, cap
+        terms, residual, norm_gain.reshape(1, width), router, expert_ids, node_count, cap
     )
-    arrived = swap(outgoing.reshape(devices, cap, width), ALL)
-    served = experts(
-        arrived.reshape(devices * cap, width), expert_gate[0], expert_up[0], expert_down[0]
-    )
-    returned = swap(served.reshape(devices, cap, width), ALL)
-    return attended, combine(shares, returned.reshape(devices * cap, width))
+    half = cap // 2
+    arrived = swap(outgoing.reshape(devices, half, width), ALL)
+    served = experts(arrived.reshape(devices * half, width), sources)
+    returned = swap(served.reshape(devices, half, width), ALL)
+    return attended, combine(shares, returned.reshape(devices * half, width))
 
 
 def solution(mesh):

time: 385 us -> 398 us (1.034)
  blocking collectives: 262 us -> 144 us
  waiting for transfers between devices: 44.9 us -> 120 us
  starting transfers between devices: 4.69 us -> 35.5 us
  local copies, waits for them, and re-layouts: 6.36 us -> 34.8 us
    all_to_all x4 -> x3, blocking collectives: 262 us -> 144 us  [swap(): return lax.all_to_all(value, axis, split_axis=0, concat_axis=0, tiled=True)]
    ppermute x0 -> x9, waiting for transfers between devices: none -> 117 us  [the longest x3 117 us: placed_weights(): crossed = [lax.ppermute(w, ALL, across) for w in weights]]
    all_to_all x1 -> x2, waiting for transfers between devices: 44.8 us -> 2.18 us  [swap(): return lax.all_to_all(value, axis, split_axis=0, concat_axis=0, tiled=True)]
    reshape x0 -> x4, local copies, waits for them, and re-layouts: none -> 27.5 us  [the longest x1 7.01 us: on_device(): arrived = swap(outgoing.reshape(devices, half, width), ALL)]
    ppermute x0 -> x9, starting transfers between devices: none -> 23.8 us  [the longest x3 16.1 us: placed_weights(): crossed = [lax.ppermute(w, ALL, across) for w in weights]]
    all_to_all x1 -> x2, starting transfers between devices: 4.65 us -> 11.7 us  [swap(): return lax.all_to_all(value, axis, split_axis=0, concat_axis=0, tiled=True)]
  transfers between devices with their start and end apart: 2 -> 12, of which waited for: 1 -> 4; matrix products, arithmetic and copies ran while one was open for 2% -> 6% of each run, Pallas kernels for 0% -> 5%
where the time goes in v2:
time: 398 us; the launch traced here: 397 us
  blocking collectives  144 us (36%)
  waiting for transfers between devices  120 us (30%)
  Pallas kernels  44.8 us (11%)
  starting transfers between devices  35.5 us (9%)
  local copies, waits for them, and re-layouts  34.8 us (9%)
  between operations  14.2 us (4%)
    all_to_all x3, blocking collectives, swap(): return lax.all_to_all(value, axis, split_axis=0, concat_axis=0, tiled=True)  144 us
    ppermute x3, waiting for transfers between devices, placed_weights(): crossed = [lax.ppermute(w, ALL, across) for w in weights]  117 us
    pallas_call x1, Pallas kernels, experts(): pl.pallas_call(expert_kernel, out_shape=jax.ShapeDtypeStruct((count, widt...  18.2 us
    ppermute x3, starting transfers between devices, placed_weights(): crossed = [lax.ppermute(w, ALL, across) for w in weights]  16.1 us
    pallas_call x1, Pallas kernels, attention(): pl.pallas_call(attention_kernel, grid=(rows // tile,), out_shape=jax.Shap...  14.5 us
    all_to_all x2, starting transfers between devices, swap(): return lax.all_to_all(value, axis, split_axis=0, concat_axis=0, tiled=True)  11.7 us
  transfers between devices with their start and end apart: 12, of which 4 were waited for; matrix products, arithmetic and copies ran while one was open for 6% of the time, Pallas kernels for 5%

profile of v2, /device:TPU:1, one launch (start us, length us, event | category | flops | bytes accessed | tf_op | source)
XLA Modules:
  0.0 396.6 jit_solution(17949339104125646244)
XLA Ops:
  7.2 2.0 pad_maximum_fusion
  9.9 1.3 gather_fusion.1
  13.3 35.2 %all_to_all.25 = bf16[128,18,128]{2,1,0:T(8,128)(2,1)S(1)} all-to-all(bf16[128,18,128]{2,1,0:T(8,128)(2,1)S(1)} %reshape.37), channel_id=1, replica_groups=mesh['node'=8,'dev'=16] {'node','dev'}, dimensions={0} | all-to-all | bytes 1179648 | tf_op jit(solution)/shard_map/all_to_all | solution.py:25
  48.6 1.0 broadcast_in_dim.47
  49.6 5.0 %all-to-all-start.1 = ((bf16[128,18,128]{2,1,0:T(8,128)(2,1)}), bf16[128,18,128]{2,1,0:T(8,128)(2,1)S(1)}, u32[]{:S(2)}, u32[]{:S(2)}) async-start(bf16[128,18,128]{2,1,0:T(8,128)(2,1)} %broadcast_in_dim.47), calls=%async_computation.1 | async-start | bytes 1572864 | tf_op jit(solution)/shard_map/all_to_all | solution.py:25
  54.7 5.3 %collective-permute-start = (bf16[1,3584,512]{2,1,0:T(8,128)(2,1)}, bf16[1,3584,512]{2,1,0:T(8,128)(2,1)}, u32[]{:S(2)}, u32[]{:S(2)}) collective-permute-start(bf16[1,3584,512]{2,1,0:T(8,128)(2,1)} %refs_0_.1), channel_id=1, source_target_pairs={{1,0},{3,2},{5,4},{7,6},{9,8},{11,10},{13,12},{15,14},{16,17},{18,... | collective-permute-start | bytes 11010056 | tf_op jit(solution)/shard_map/ppermute | solution.py:261
  60.0 1.3 collective-permute-start.3
  61.2 7.6 %collective-permute-start.1 = (bf16[1,3584,512]{2,1,0:T(8,128)(2,1)}, bf16[1,3584,512]{2,1,0:T(8,128)(2,1)}, u32[]{:S(2)}, u32[]{:S(2)}) collective-permute-start(bf16[1,3584,512]{2,1,0:T(8,128)(2,1)} %refs_1_.1), channel_id=1, source_target_pairs={{1,0},{3,2},{5,4},{7,6},{9,8},{11,10},{13,12},{15,14},{16,17},{18,... | collective-permute-start | bytes 11010056 | tf_op jit(solution)/shard_map/ppermute | solution.py:261
  68.8 3.2 collective-permute-start.2
  72.0 1.3 reshape.38.prefix
  73.3 14.5 %attention.1 = bf16[512,3584]{1,0:T(8,128)(2,1)} custom-call(bf16[512,256]{1,0:T(8,128)(2,1)} %q_nope.1, bf16[512,128]{1,0:T(8,128)(2,1)} %q_rope.1, bf16[4608,512]{1,0:T(8,128)(2,1)} %all-gather.2.cloned.1.call-done.keys, bf16[576,512]{1,0:T(8,128)(2,1)} %reshape.38.prefix, bf16[2,128,512]{2,1,0:T(8,128)(2,1)} %absorb_k.1, bf16[2,512,128]{2,1,0:T(8,128)(2,1)} %absorb_v.1, ...), custom_call_target="tpu_custom_call" | custom-call | tf_op jit(solution)/shard_map/attention/pallas_call | solution.py:96
  87.8 6.7 %all-to-all-start.2 = ((bf16[16,32,3584]{2,1,0:T(8,128)(2,1)}), bf16[16,32,3584]{2,1,0:T(8,128)(2,1)}, u32[]{:S(2)}, u32[]{:S(2)}) async-start(bf16[16,32,3584]{2,1,0:T(8,128)(2,1)} %bitcast.12), calls=%async_computation.2 | async-start | bytes 7340032 | tf_op jit(solution)/shard_map/all_to_all | solution.py:25
  94.5 1.3 collective-permute-start.4
  95.8 42.7 %collective-permute-done.refs_3_ = bf16[1,3584,512]{2,1,0:T(8,128)(2,1)} collective-permute-done((bf16[1,3584,512]{2,1,0:T(8,128)(2,1)}, bf16[1,3584,512]{2,1,0:T(8,128)(2,1)}, u32[]{:S(2)}, u32[]{:S(2)}) %collective-permute-start) | collective-permute-done | bytes 3670048 | tf_op jit(solution)/shard_map/ppermute | solution.py:261
  138.5 1.3 collective-permute-start.5
  139.8 1.3 collective-permute-start.6
  141.1 36.7 %collective-permute-done.1.refs_4_ = bf16[1,3584,512]{2,1,0:T(8,128)(2,1)} collective-permute-done((bf16[1,3584,512]{2,1,0:T(8,128)(2,1)}, bf16[1,3584,512]{2,1,0:T(8,128)(2,1)}, u32[]{:S(2)}, u32[]{:S(2)}) %collective-permute-start.1) | collective-permute-done | bytes 3670048 | tf_op jit(solution)/shard_map/ppermute | solution.py:261
  177.8 1.3 collective-permute-start.7
  179.1 38.0 %collective-permute-done.2.refs_5_ = bf16[1,512,3584]{2,1,0:T(8,128)(2,1)} collective-permute-done((bf16[1,512,3584]{2,1,0:T(8,128)(2,1)}, bf16[1,512,3584]{2,1,0:T(8,128)(2,1)}, u32[]{:S(2)}, u32[]{:S(2)}) %collective-permute-start.2) | collective-permute-done | bytes 3670048 | tf_op jit(solution)/shard_map/ppermute | solution.py:261
  217.1 1.3 collective-permute-start.8
  219.0 0.7 copy.23.ids
  219.7 1.2 copy.22.router
  220.9 2.2 all-to-all-done.2.terms
  223.1 6.4 %route.1 = (bf16[32,3584]{1,0:T(8,128)(2,1)}, bf16[512,3584]{1,0:T(8,128)(2,1)}, bf16[32,512]{1,0:T(8,128)(2,1)}) custom-call(bf16[16,32,3584]{2,1,0:T(8,128)(2,1)} %all-to-all-done.2.terms, bf16[32,3584]{1,0:T(8,128)(2,1)} %residual.1, bf16[1,3584]{1,0:T(2,128)(2,1)} %reshape.40.gain, bf16[3584,64]{1,0:T(8,128)(2,1)} %copy.22.router, s32[32,8]{1,0:T(8,128)} %copy.23.ids), custom_call_target="tpu_custom_call" | custom-call | tf_op jit(solution)/shard_map/route/pallas_call | solution.py:178
  229.5 7.0 %reshape.41 = bf16[128,4,3584]{2,1,0:T(4,128)(2,1)} reshape(bf16[512,3584]{1,0:T(8,128)(2,1)} %get-tuple-element.7) | data formatting | bytes 7340032 | tf_op jit(solution)/shard_map/reshape | solution.py:344
  236.5 56.5 %all_to_all.26 = bf16[128,4,3584]{2,1,0:T(4,128)(2,1)} all-to-all(bf16[128,4,3584]{2,1,0:T(4,128)(2,1)} %reshape.41), channel_id=1, replica_groups=mesh['node'=8,'dev'=16] {'node','dev'}, dimensions={0} | all-to-all | bytes 7340032 | tf_op jit(solution)/shard_map/all_to_all | solution.py:25
  293.1 6.7 %reshape.42.rows = bf16[512,3584]{1,0:T(8,128)(2,1)} reshape(bf16[128,4,3584]{2,1,0:T(4,128)(2,1)} %all_to_all.26) | data formatting | bytes 7340032 | tf_op jit(solution)/shard_map/reshape | solution.py:345
  299.8 18.2 %experts.1 = bf16[512,3584]{1,0:T(8,128)(2,1)} custom-call(bf16[512,3584]{1,0:T(8,128)(2,1)} %reshape.42.rows, bf16[1,3584,512]{2,1,0:T(8,128)(2,1)} %refs_0_.1, bf16[1,3584,512]{2,1,0:T(8,128)(2,1)} %refs_1_.1, bf16[1,512,3584]{2,1,0:T(8,128)(2,1)} %refs_2_.1, bf16[1,3584,512]{2,1,0:T(8,128)(2,1)} %collective-permute-done.refs_3_, ...), custom_call_target="tpu_custom_call" | custom-call | tf_op jit(solution)/shard_map/experts/pallas_call | solution.py:238
  318.0 7.0 %reshape.43 = bf16[128,4,3584]{2,1,0:T(4,128)(2,1)} reshape(bf16[512,3584]{1,0:T(8,128)(2,1)} %experts.1) | data formatting | bytes 7340032 | tf_op jit(solution)/shard_map/reshape | solution.py:346
  325.0 52.3 %all_to_all.27 = bf16[128,4,3584]{2,1,0:T(4,128)(2,1)} all-to-all(bf16[128,4,3584]{2,1,0:T(4,128)(2,1)} %reshape.43), channel_id=1, replica_groups=mesh['node'=8,'dev'=16] {'node','dev'}, dimensions={0} | all-to-all | bytes 7340032 | tf_op jit(solution)/shard_map/all_to_all | solution.py:25
  377.3 6.8 %reshape.44.returned = bf16[512,3584]{1,0:T(8,128)(2,1)} reshape(bf16[128,4,3584]{2,1,0:T(4,128)(2,1)} %all_to_all.27) | data formatting | bytes 7340032 | tf_op jit(solution)/shard_map/reshape | solution.py:347
  384.0 5.7 %combine.1 = bf16[32,3584]{1,0:T(8,128)(2,1)} custom-call(bf16[32,512]{1,0:T(8,128)(2,1)} %get-tuple-element.6.shares, bf16[512,3584]{1,0:T(8,128)(2,1)} %reshape.44.returned), custom_call_target="tpu_custom_call" | custom-call | tf_op jit(solution)/shard_map/combine/pallas_call | solution.py:275
  (31 shorter events, 3.6 us)
Async XLA Ops:
  7.2 4.1 %copy-start = (bf16[2,128,512]{2,1,0:T(8,128)(2,1)S(1)}, bf16[2,128,512]{2,1,0:T(8,128)(2,1)}, u32[]{:S(2)}) copy-start(bf16[2,128,512]{2,1,0:T(8,128)(2,1)} %param.21) | copy-start | bytes 786436
  7.2 66.1 %all-gather.2.cloned.1.call-start = ((), (), s32[]{:S(2)}) async-start(), calls=%async_computation.5 | async-start | bytes 5308416 | tf_op jit(solution)/shard_map/all_gather | solution.py:335
  49.6 22.4 %all-to-all-start.1 = ((bf16[128,18,128]{2,1,0:T(8,128)(2,1)}), bf16[128,18,128]{2,1,0:T(8,128)(2,1)S(1)}, u32[]{:S(2)}, u32[]{:S(2)}) async-start(bf16[128,18,128]{2,1,0:T(8,128)(2,1)} %broadcast_in_dim.47), calls=%async_computation.1 | async-start | bytes 1572864 | tf_op jit(solution)/shard_map/all_to_all | solution.py:25
  54.7 83.8 %collective-permute-start = (bf16[1,3584,512]{2,1,0:T(8,128)(2,1)}, bf16[1,3584,512]{2,1,0:T(8,128)(2,1)}, u32[]{:S(2)}, u32[]{:S(2)}) collective-permute-start(bf16[1,3584,512]{2,1,0:T(8,128)(2,1)} %refs_0_.1), channel_id=1, source_target_pairs={{1,0},{3,2},{5,4},{7,6},{9,8},{11,10},{13,12},{15,14},{16,17},{18,... | collective-permute-start | bytes 11010056 | tf_op jit(solution)/shard_map/ppermute | solution.py:261
  60.0 79.8 %collective-permute-start.3 = (bf16[1,3584,512]{2,1,0:T(8,128)(2,1)}, bf16[1,3584,512]{2,1,0:T(8,128)(2,1)}, u32[]{:S(2)}, u32[]{:S(2)}) collective-permute-start(bf16[1,3584,512]{2,1,0:T(8,128)(2,1)} %refs_0_.1), channel_id=1, source_target_pairs={{0,16},{2,18},{4,20},{6,22},{8,24},{10,26},{12,28},{14,30},{17,1},... | collective-permute-start | bytes 11010056 | tf_op jit(solution)/shard_map/ppermute | solution.py:262
  61.2 116.5 %collective-permute-start.1 = (bf16[1,3584,512]{2,1,0:T(8,128)(2,1)}, bf16[1,3584,512]{2,1,0:T(8,128)(2,1)}, u32[]{:S(2)}, u32[]{:S(2)}) collective-permute-start(bf16[1,3584,512]{2,1,0:T(8,128)(2,1)} %refs_1_.1), channel_id=1, source_target_pairs={{1,0},{3,2},{5,4},{7,6},{9,8},{11,10},{13,12},{15,14},{16,17},{18,... | collective-permute-start | bytes 11010056 | tf_op jit(solution)/shard_map/ppermute | solution.py:261
  68.8 148.3 %collective-permute-start.2 = (bf16[1,512,3584]{2,1,0:T(8,128)(2,1)}, bf16[1,512,3584]{2,1,0:T(8,128)(2,1)}, u32[]{:S(2)}, u32[]{:S(2)}) collective-permute-start(bf16[1,512,3584]{2,1,0:T(8,128)(2,1)} %refs_2_.1), channel_id=1, source_target_pairs={{1,0},{3,2},{5,4},{7,6},{9,8},{11,10},{13,12},{15,14},{16,17},{18,... | collective-permute-start | bytes 11010056 | tf_op jit(solution)/shard_map/ppermute | solution.py:261
  87.8 130.6 %copy-start.3 = (bf16[3584]{0:T(1024)(128)(2,1)S(1)}, bf16[3584]{0:T(1024)(128)(2,1)}, u32[]{:S(2)}) copy-start(bf16[3584]{0:T(1024)(128)(2,1)} %param.28) | copy-start | bytes 21508
  87.8 131.2 %copy-start.4 = (s32[32,8]{0,1:T(8,128)S(1)}, s32[32,8]{0,1:T(8,128)}, u32[]{:S(2)}) copy-start(s32[32,8]{0,1:T(8,128)} %param.30) | copy-start | bytes 3076
  87.8 131.9 %copy-start.2 = (bf16[3584,64]{0,1:T(8,128)(2,1)S(1)}, bf16[3584,64]{0,1:T(8,128)(2,1)}, u32[]{:S(2)}) copy-start(bf16[3584,64]{0,1:T(8,128)(2,1)} %param.29) | copy-start | bytes 1376260
  87.8 135.3 %all-to-all-start.2 = ((bf16[16,32,3584]{2,1,0:T(8,128)(2,1)}), bf16[16,32,3584]{2,1,0:T(8,128)(2,1)}, u32[]{:S(2)}, u32[]{:S(2)}) async-start(bf16[16,32,3584]{2,1,0:T(8,128)(2,1)} %bitcast.12), calls=%async_computation.2 | async-start | bytes 7340032 | tf_op jit(solution)/shard_map/all_to_all | solution.py:25
  94.5 205.3 %collective-permute-start.4 = (bf16[1,3584,512]{2,1,0:T(8,128)(2,1)}, bf16[1,3584,512]{2,1,0:T(8,128)(2,1)}, u32[]{:S(2)}, u32[]{:S(2)}) collective-permute-start(bf16[1,3584,512]{2,1,0:T(8,128)(2,1)} %refs_1_.1), channel_id=1, source_target_pairs={{0,16},{2,18},{4,20},{6,22},{8,24},{10,26},{12,28},{14,30},{17,1},... | collective-permute-start | bytes 11010056 | tf_op jit(solution)/shard_map/ppermute | solution.py:262
  138.5 161.4 %collective-permute-start.5 = (bf16[1,512,3584]{2,1,0:T(8,128)(2,1)}, bf16[1,512,3584]{2,1,0:T(8,128)(2,1)}, u32[]{:S(2)}, u32[]{:S(2)}) collective-permute-start(bf16[1,512,3584]{2,1,0:T(8,128)(2,1)} %refs_2_.1), channel_id=1, source_target_pairs={{0,16},{2,18},{4,20},{6,22},{8,24},{10,26},{12,28},{14,30},{17,1},... | collective-permute-start | bytes 11010056 | tf_op jit(solution)/shard_map/ppermute | solution.py:262
  139.8 160.1 %collective-permute-start.6 = (bf16[1,3584,512]{2,1,0:T(8,128)(2,1)}, bf16[1,3584,512]{2,1,0:T(8,128)(2,1)}, u32[]{:S(2)}, u32[]{:S(2)}) collective-permute-start(bf16[1,3584,512]{2,1,0:T(8,128)(2,1)} %collective-permute-done.refs_3_), channel_id=1, source_target_pairs={{0,16},{2,18},{4,20},{6,22},{8,24},{10,26},{12,28},{14,30},{17,1},... | collective-permute-start | bytes 11010056 | tf_op jit(solution)/shard_map/ppermute | solution.py:263
  177.8 122.0 %collective-permute-start.7 = (bf16[1,3584,512]{2,1,0:T(8,128)(2,1)}, bf16[1,3584,512]{2,1,0:T(8,128)(2,1)}, u32[]{:S(2)}, u32[]{:S(2)}) collective-permute-start(bf16[1,3584,512]{2,1,0:T(8,128)(2,1)} %collective-permute-done.1.refs_4_), channel_id=1, source_target_pairs={{0,16},{2,18},{4,20},{6,22},{8,24},{10,26},{12,28},{14,30},{17,1},... | collective-permute-start | bytes 11010056 | tf_op jit(solution)/shard_map/ppermute | solution.py:263
  217.1 82.7 %collective-permute-start.8 = (bf16[1,512,3584]{2,1,0:T(8,128)(2,1)}, bf16[1,512,3584]{2,1,0:T(8,128)(2,1)}, u32[]{:S(2)}, u32[]{:S(2)}) collective-permute-start(bf16[1,512,3584]{2,1,0:T(8,128)(2,1)} %collective-permute-done.2.refs_5_), channel_id=1, source_target_pairs={{0,16},{2,18},{4,20},{6,22},{8,24},{10,26},{12,28},{14,30},{17,1},... | collective-permute-start | bytes 11010056 | tf_op jit(solution)/shard_map/ppermute | solution.py:263
  377.3 12.5 %copy-start.1 = (bf16[2,128,512]{2,1,0:T(8,128)(2,1)S(1)}, bf16[2,128,512]{2,1,0:T(8,128)(2,1)}, u32[]{:S(2)}) copy-start(bf16[2,128,512]{2,1,0:T(8,128)(2,1)} %param.21) | copy-start | bytes 786436
Sparse Core Ops, SparseCore 0:
  9.7 46.3 all-gather.1

commit v3 on v2

v3 whole, which is shorter than its diff:
```python
import functools
import math

import jax
import jax.numpy as jnp
from jax import lax
from jax.experimental import pallas as pl
from jax.experimental.pallas import tpu as pltpu
from jax.sharding import PartitionSpec as P

ROUTE_SCALE = 2.827
NORM_EPS = 1e-06
FAR_BELOW = -1e30
ALL = ("node", "dev")
VMEM_BYTES = 60 * 1024 * 1024
F32 = jnp.float32
BF16 = jnp.bfloat16


def dot(a, b, dims=(((1,), (0,)), ((), ()))):
    return lax.dot_general(a, b, dims, preferred_element_type=F32)


def swap(value, axis):
    return lax.all_to_all(value, axis, split_axis=0, concat_axis=0, tiled=True)


def fold(q_lat, q_rope, lat, rot, mask, old, new, scale):
    top, total, mixed = new
    heads, tokens = len(q_lat), q_rope.shape[0]
    rope = q_rope.shape[1] // heads
    for h in range(heads):
        rows = pl.ds(h * tokens, tokens)
        scores = dot(q_lat[h], lat, (((1,), (1,)), ((), ())))
        across = (((1,), (0,)), ((), ())) if rot.shape[0] == rope else (((1,), (1,)), ((), ()))
        scores = scores + dot(q_rope[:, h * rope : (h + 1) * rope], rot, across)
        if mask is not None:
            scores = jnp.where(mask, scores, FAR_BELOW)
        row_top = jnp.max(scores, axis=1, keepdims=True)
        if old is not None:
            old_top = old[0][rows]
            row_top = jnp.maximum(row_top, old_top)
        exp_scores = jnp.exp((scores - row_top) * scale)
        row_sum = jnp.sum(exp_scores, axis=1, keepdims=True)
        mix = dot(exp_scores.astype(BF16), lat)
        if old is not None:
            shrink = jnp.exp((old_top - row_top) * scale)
            row_sum = row_sum + old[1][rows] * shrink
            mix = mix + old[2][rows] * shrink
        top[rows] = row_top
        total[rows] = row_sum
        mixed[rows] = mix


def span_kernel(q_nope, q_rope, keys, absorb_k, q_lat, top, total, mixed, *, block):
    heads, nope, rank = absorb_k.shape
    tokens = q_nope.shape[0]
    rope = q_rope.shape[1] // heads
    span = block - rope
    scale = 1.0 / math.sqrt(nope + rope)
    node = lax.axis_index("node")
    first = pl.program_id(0) * tokens
    for h in range(heads):
        part = dot(q_nope[:, h * nope : (h + 1) * nope], absorb_k[h])
        q_lat[h * tokens : (h + 1) * tokens] = part.astype(BF16)

    def add(at, mask, old):
        q_parts = [q_lat[pl.ds(h * tokens, tokens)] for h in range(heads)]
        lat, rot = keys[pl.ds(at, span)], keys[pl.ds(at + span, rope)]
        fold(q_parts, q_rope, lat, rot, mask, old, (top, total, mixed), scale)

    q_pos = first + lax.broadcasted_iota(jnp.int32, (tokens, span), 0)
    key_pos = lax.broadcasted_iota(jnp.int32, (tokens, span), 1)
    add(pl.multiple_of(node * block, 64), key_pos <= q_pos, None)

    def earlier(j, carry):
        add(pl.multiple_of(j * block, 64), None, (top, total, mixed))
        return carry

    lax.fori_loop(0, node, earlier, 0)


def prefix_kernel(
    q_lat,
    q_rope,
    prefix,
    old_top,
    old_total,
    old_mixed,
    absorb_v,
    out_proj,
    terms,
    top,
    total,
    mixed,
    lat,
    *,
    scale,
):
    heads = absorb_v.shape[0]
    tokens = q_rope.shape[0]
    rope = q_rope.shape[1] // heads
    keys, rank = lat.shape
    for c in range(rank // 128):
        lat[:, c * 128 : (c + 1) * 128] = prefix[c * keys : (c + 1) * keys]
    rot = prefix[rank // 128 * keys : (rank // 128 + 1) * keys, :rope]
    q_parts = [q_lat[h * tokens : (h + 1) * tokens] for h in range(heads)]
    old = (old_top, old_total, old_mixed)
    fold(q_parts, q_rope, lat[...], rot, None, old, (top, total, mixed), scale)
    outs = []
    for h in range(heads):
        rows = pl.ds(h * tokens, tokens)
        head_lat = (mixed[rows] / total[rows]).astype(BF16)
        outs.append(dot(head_lat, absorb_v[h]).astype(BF16))
    head_out = jnp.concatenate(outs, axis=1)
    width = out_proj.shape[1]
    step = 512
    for c in range(0, width, step):
        terms[:, c : c + step] = dot(head_out, out_proj[:, c : c + step]).astype(BF16)


def attend_span(q_nope, q_rope, keys, absorb_k, block):
    rows = q_nope.shape[0]
    tile = min(256, rows)
    heads, nope, rank = absorb_k.shape
    whole = pl.BlockSpec(memory_space=pltpu.VMEM)
    state = [
        jax.ShapeDtypeStruct((heads * rows, rank), BF16),
        jax.ShapeDtypeStruct((heads * rows, 1), F32),
        jax.ShapeDtypeStruct((heads * rows, 1), F32),
        jax.ShapeDtypeStruct((heads * rows, rank), F32),
    ]
    pairs = heads * rows * keys.shape[0]
    return pl.pallas_call(
        functools.partial(span_kernel, block=block),
        grid=(rows // tile,),
        out_shape=state,
        in_specs=[
            pl.BlockSpec((tile, q_nope.shape[1]), lambda i: (i, 0)),
            pl.BlockSpec((tile, q_rope.shape[1]), lambda i: (i, 0)),
            whole,
            whole,
        ],
        out_specs=[pl.BlockSpec((heads * tile, s.shape[1]), lambda i: (i, 0)) for s in state],
        compiler_params=pltpu.CompilerParams(vmem_limit_bytes=VMEM_BYTES),
        cost_estimate=pl.CostEstimate(
            flops=2 * pairs * (2 * rank + 64), bytes_accessed=8 << 20, transcendentals=pairs
        ),
        name="attend_span",
    )(q_nope, q_rope, keys, absorb_k)


def attend_prefix(state, q_rope, prefix, absorb_v, out_proj, nope, keys):
    rows = q_rope.shape[0]
    tile = min(256, rows)
    heads, rank, _ = absorb_v.shape
    rope = q_rope.shape[1] // heads
    width = out_proj.shape[1]
    whole = pl.BlockSpec(memory_space=pltpu.VMEM)
    specs = [pl.BlockSpec((heads * tile, s.shape[1]), lambda i: (i, 0)) for s in state]
    return pl.pallas_call(
        functools.partial(prefix_kernel, scale=1.0 / math.sqrt(nope + rope)),
        grid=(rows // tile,),
        out_shape=jax.ShapeDtypeStruct((rows, width), BF16),
        in_specs=[
            specs[0],
            pl.BlockSpec((tile, q_rope.shape[1]), lambda i: (i, 0)),
            whole,
            specs[1],
            specs[2],
            specs[3],
            whole,
            whole,
        ],
        out_specs=pl.BlockSpec((tile, width), lambda i: (i, 0)),
        scratch_shapes=[
            pltpu.VMEM((heads * tile, 1), F32),
            pltpu.VMEM((heads * tile, 1), F32),
            pltpu.VMEM((heads * tile, rank), F32),
            pltpu.VMEM((keys, rank), BF16),
        ],
        compiler_params=pltpu.CompilerParams(vmem_limit_bytes=VMEM_BYTES),
        cost_estimate=pl.CostEstimate(flops=6 << 30, bytes_accessed=10 << 20, transcendentals=0),
        name="attend_prefix",
    )(state[0], q_rope, prefix, state[1], state[2], state[3], absorb_v, out_proj)


def slot_place(column, nodes, cap, experts):
    half = cap // 2
    devs = 2 * experts // nodes
    device, part, low = column // cap, column % cap // half, column % half
    node, dev = device // devs, device % devs
    expert = (experts // nodes) * (node // 2 * 2 + dev % 2) + dev // 2
    return expert, node % 2 * half + low, part


def route_kernel(terms, residual, gain, router, ids, attended, outgoing, shares, *, nodes, cap):
    groups, tokens, width = terms.shape
    experts = router.shape[1]
    top_k = ids.shape[1]
    acc = terms[0].astype(F32)
    for g in range(1, groups):
        acc = acc + terms[g].astype(F32)
    stream = (residual[...].astype(F32) + acc).astype(BF16)
    attended[...] = stream
    stream = stream.astype(F32)
    mean = jnp.mean(stream * stream, axis=1, keepdims=True)
    normed = (stream * lax.rsqrt(mean + NORM_EPS) * gain[...].astype(F32)).astype(BF16)
    logits = dot(normed, router[...])
    expert = lax.broadcasted_iota(jnp.int32, (tokens, experts), 1)
    hits = [ids[:, j : j + 1] == expert for j in range(top_k)]
    gates = [
        jax.nn.sigmoid(jnp.sum(jnp.where(hit, logits, 0.0), axis=1, keepdims=True)) for hit in hits
    ]
    gate_sum = functools.reduce(lambda a, b: a + b, gates)
    weight = jnp.zeros((tokens, experts), F32)
    used = jnp.zeros((tokens, experts), F32)
    for hit, gate in zip(hits, gates):
        weight = jnp.where(hit, ROUTE_SCALE * gate / gate_sum, weight)
        used = jnp.where(hit, 1.0, used)
    weight = weight.astype(BF16)
    used = used.astype(BF16)
    below = lax.broadcasted_iota(jnp.int32, (tokens, tokens), 1) < lax.broadcasted_iota(
        jnp.int32, (tokens, tokens), 0
    )
    rank = dot(below.astype(BF16), used).astype(BF16)
    rows = 2 * experts * cap
    owner = slot_place(lax.broadcasted_iota(jnp.int32, (experts, rows), 1), nodes, cap, experts)[0]
    spread = (owner == lax.broadcasted_iota(jnp.int32, (experts, rows), 0)).astype(BF16)
    _, slot, part = slot_place(
        lax.broadcasted_iota(jnp.int32, (tokens, rows), 1), nodes, cap, experts
    )
    filled = (dot(used, spread) > 0.5) & (dot(rank, spread) == slot.astype(F32))
    share = jnp.where(filled, dot(weight, spread), 0.0)
    filled = filled.astype(F32)
    share = [jnp.where(part == p, share, 0.0) for p in range(2)]
    filled = [jnp.where(part == p, filled, 0.0) for p in range(2)]
    shares[...] = jnp.concatenate(share, 0).astype(BF16)
    fill = jnp.concatenate(filled, 0).astype(BF16)
    narrow = width // 2
    halves = jnp.concatenate([normed[:, :narrow], normed[:, narrow:]], 0)
    step = narrow // 2
    for c in range(0, narrow, step):
        outgoing[:, c : c + step] = dot(
            fill, halves[:, c : c + step], (((0,), (0,)), ((), ()))
        ).astype(BF16)


def route(terms, residual, gain, router, ids, nodes, cap):
    tokens, width = residual.shape
    rows = 2 * router.shape[1] * cap
    whole = pl.BlockSpec(memory_space=pltpu.VMEM)
    return pl.pallas_call(
        functools.partial(route_kernel, nodes=nodes, cap=cap),
        out_shape=(
            jax.ShapeDtypeStruct((tokens, width), BF16),
            jax.ShapeDtypeStruct((rows, width // 2), BF16),
            jax.ShapeDtypeStruct((2 * tokens, rows), BF16),
        ),
        in_specs=[whole] * 5,
        out_specs=(whole, whole, whole),
        compiler_params=pltpu.CompilerParams(vmem_limit_bytes=VMEM_BYTES),
        name="route",
    )(terms, residual, gain, router, ids)


def expert_kernel(rows, *refs, cap):
    sources, (out, whole_rows, gates, ups, downs, sems) = refs[:12], refs[12:]
    node, dev = lax.axis_index("node"), lax.axis_index("dev")
    keeper = node % 2 == dev % 2
    own, crossed, twin, twin_crossed = (sources[3 * i : 3 * i + 3] for i in range(4))
    slots = (gates, ups, downs)

    def copy(source, share, part):
        return pltpu.make_async_copy(
            source[part].at[0], slots[part].at[share], sems.at[share * 3 + part]
        )

    order = ((0, 0), (0, 1), (1, 0), (1, 1), (0, 2), (1, 2))

    @pl.when(keeper)
    def _():
        for share, part in order:
            copy((own, crossed)[share], share, part).start()

    @pl.when(jnp.logical_not(keeper))
    def _():
        for share, part in order:
            copy((twin, twin_crossed)[share], share, part).start()

    count, narrow = rows.shape
    block = 256
    half = cap // 2
    here = lax.broadcasted_iota(jnp.int32, (block, block), 0)
    there = lax.broadcasted_iota(jnp.int32, (block, block), 1)
    mid = block // 2
    wanted = here % mid // half * cap + here // mid * half + here % half
    order_rows = (there == wanted).astype(F32).astype(BF16)
    for b in range(0, count, block):
        sorted_rows = dot(order_rows, rows[b : b + block]).astype(BF16)
        whole_rows[b // 2 : b // 2 + mid, :narrow] = sorted_rows[:mid]
        whole_rows[b // 2 : b // 2 + mid, narrow:] = sorted_rows[mid:]

    x = whole_rows[...]
    hidden = []
    for share in range(2):
        copy(own, share, 0).wait()
        gate_act = dot(x, gates[share])
        copy(own, share, 1).wait()
        up_act = dot(x, ups[share])
        hidden.append((jax.nn.silu(gate_act) * up_act).astype(BF16))
    for share in range(2):
        copy(own, share, 2).wait()
    step = narrow // 2
    for c in range(0, narrow, step):
        parts = []
        for at in (c, narrow + c):
            part = dot(hidden[0], downs[0, :, at : at + step])
            part = part + dot(hidden[1], downs[1, :, at : at + step])
            parts.append(part.astype(BF16))
        for b in range(0, count, block):
            both = jnp.concatenate([part[b // 2 : b // 2 + mid] for part in parts], 0)
            out[b : b + block, c : c + step] = dot(
                order_rows, both, (((0,), (0,)), ((), ()))
            ).astype(BF16)


def experts(rows, sources, cap):
    count, narrow = rows.shape
    _, width, hidden = sources[0].shape
    whole = pl.BlockSpec(memory_space=pltpu.VMEM)
    return pl.pallas_call(
        functools.partial(expert_kernel, cap=cap),
        out_shape=jax.ShapeDtypeStruct((count, narrow), BF16),
        in_specs=[whole] + [pl.BlockSpec(memory_space=pl.ANY)] * 12,
        out_specs=whole,
        scratch_shapes=[
            pltpu.VMEM((count // 2, width), BF16),
            pltpu.VMEM((2, width, hidden), BF16),
            pltpu.VMEM((2, width, hidden), BF16),
            pltpu.VMEM((2, hidden, width), BF16),
            pltpu.SemaphoreType.DMA((6,)),
        ],
        compiler_params=pltpu.CompilerParams(vmem_limit_bytes=VMEM_BYTES),
        name="experts",
    )(rows, *sources)


def placed_weights(weights, nodes, devs):
    across, beside = [], []
    for node in range(nodes):
        for dev in range(devs):
            if node % 2 == dev % 2:
                across.append((node * devs + (dev ^ 1), node * devs + dev))
                beside.append((node * devs + dev, (node ^ 1) * devs + dev))
    crossed = [lax.ppermute(w, ALL, across) for w in weights]

    def place_last(crossed, last):
        own = list(weights) + [last]
        crossed = list(crossed) + [lax.ppermute(last, ALL, across)]
        twin = [lax.ppermute(w, ALL, beside) for w in own]

        def finish(crossed):
            twin_crossed = [lax.ppermute(w, ALL, beside) for w in crossed]
            return own + list(crossed) + twin + twin_crossed

        return crossed, finish

    return crossed, place_last


def combine_kernel(shares, returned, out):
    tokens, width = out.shape
    tile = returned.shape[1]
    both = dot(shares[...], returned[...]).astype(BF16)
    at = pl.multiple_of(pl.program_id(0) * tile, 128)
    out[:, pl.ds(at, tile)] = both[:tokens]
    at = pl.multiple_of(width // 2 + pl.program_id(0) * tile, 128)
    out[:, pl.ds(at, tile)] = both[tokens:]


def combine(shares, returned):
    tokens, rows = shares.shape[0] // 2, shares.shape[1]
    narrow = returned.shape[1]
    tile = 256
    return pl.pallas_call(
        combine_kernel,
        grid=(narrow // tile,),
        out_shape=jax.ShapeDtypeStruct((tokens, 2 * narrow), BF16),
        in_specs=[
            pl.BlockSpec((2 * tokens, rows), lambda i: (0, 0)),
            pl.BlockSpec((rows, tile), lambda i: (0, i)),
        ],
        out_specs=pl.BlockSpec((tokens, 2 * narrow), lambda i: (0, 0)),
        compiler_params=pltpu.CompilerParams(vmem_limit_bytes=VMEM_BYTES),
        name="combine",
    )(shares, returned)


def listed_kernel(table, lat, rot, out):
    held, block, rank = lat.shape
    rope = rot.shape[2]
    count = table.shape[0]
    me = lax.axis_index("node") * lax.axis_size("dev") + lax.axis_index("dev")
    out[...] = jnp.zeros(out.shape, BF16)
    for b in range(count):
        entry = table[b]
        slot = entry % held

        @pl.when(entry // held == me)
        def _():
            for c in range(rank // 128):
                at = (c * count + b) * block
                out[at : at + block] = lat[slot, :, c * 128 : (c + 1) * 128]
            at = (rank // 128 * count + b) * block
            out[at : at + block, :rope] = rot[slot]


def spread_kernel(arrived, *refs):
    out = refs[-1]
    count = arrived.shape[0]
    piece = arrived[0].astype(F32)
    for d in range(1, count):
        piece = piece + arrived[d].astype(F32)
    out[...] = jnp.broadcast_to(piece.astype(BF16)[None], out.shape)


def listed_prefix(pool_latent, pool_rope, block_table, devices, first):
    held, block, rank = pool_latent.shape
    keys = block_table.shape[0] * block
    rows = -(-keys * (rank // 128 + 1) // (devices * 8)) * devices * 8
    whole = pl.BlockSpec(memory_space=pltpu.VMEM)
    mine = pl.pallas_call(
        listed_kernel,
        out_shape=jax.ShapeDtypeStruct((rows, 128), BF16),
        in_specs=[pl.BlockSpec(memory_space=pltpu.SMEM), whole, whole],
        out_specs=whole,
        compiler_params=pltpu.CompilerParams(vmem_limit_bytes=VMEM_BYTES),
        name="listed",
    )(block_table, pool_latent, pool_rope)
    arrived = swap(mine.reshape(devices, rows // devices, 128), ALL)
    state, crossed, last = first
    spread = pl.pallas_call(
        spread_kernel,
        out_shape=jax.ShapeDtypeStruct(arrived.shape, BF16),
        in_specs=[whole] + [pl.BlockSpec(memory_space=pl.ANY)] * len(state),
        out_specs=whole,
        compiler_params=pltpu.CompilerParams(vmem_limit_bytes=VMEM_BYTES),
        name="spread",
    )(arrived, *state)
    spread, crossed, last = lax.optimization_barrier((spread, crossed, last))
    return swap(spread, ALL).reshape(rows, 128), (state, crossed, last)


def on_device(
    q_nope,
    q_rope,
    kv_latent,
    k_rope,
    pool_latent,
    pool_rope,
    block_table,
    absorb_k,
    absorb_v,
    out_proj,
    residual,
    norm_gain,
    router,
    expert_ids,
    expert_gate,
    expert_up,
    expert_down,
):
    node_count = lax.axis_size("node")
    dev_count = lax.axis_size("dev")
    devices = node_count * dev_count
    prefix_keys = block_table.shape[0] * pool_latent.shape[1]
    tokens, width = residual.shape
    expert_count = router.shape[1]
    cap = max(2, 2 * tokens * expert_ids.shape[1] // expert_count)

    crossed, place_last = placed_weights((expert_gate, expert_up), node_count, dev_count)
    keys_here = jnp.concatenate([kv_latent, k_rope.T], 0)
    keys = lax.all_gather(keys_here, "node", axis=0, tiled=True)
    state = attend_span(q_nope, q_rope, keys, absorb_k, keys_here.shape[0])
    prefix, (state, crossed, expert_down) = listed_prefix(
        pool_latent, pool_rope, block_table, devices, (state, crossed, expert_down)
    )
    crossed, finish = place_last(crossed, expert_down)
    terms = attend_prefix(
        state, q_rope, prefix, absorb_v, out_proj, absorb_k.shape[1], prefix_keys
    )
    terms, crossed[1] = lax.optimization_barrier((terms, crossed[1]))
    terms = swap(terms.reshape(dev_count, tokens, width), "dev")
    terms, crossed[2] = lax.optimization_barrier((terms, crossed[2]))
    attended, outgoing, shares = route(
        terms, residual, norm_gain.reshape(1, width), router, expert_ids, node_count, cap
    )
    arrived = swap(outgoing.reshape(devices, cap, width // 2), ALL)
    served = experts(arrived.reshape(devices * cap, width // 2), finish(crossed), cap)
    returned = swap(served.reshape(devices, cap, width // 2), ALL)
    return attended, combine(shares, returned.reshape(devices * cap, width // 2))


def solution(mesh):
    placed = (
        P("node", "dev"),
        P("node", "dev"),
        P("node", None),
        P("node", None),
        P(ALL, None, None),
        P(ALL, None, None),
        P(),
        P("dev", None, None),
        P("dev", None, None),
        P("dev", None),
        P(ALL, None),
        P(),
        P(),
        P(ALL, None),
        P(ALL, None, None),
        P(ALL, None, None),
        P(ALL, None, None),
    )
    return jax.shard_map(
        on_device,
        mesh=mesh,
        in_specs=placed,
        out_specs=(P(ALL, None), P(ALL, None)),
        check_vma=False,
    )
```

time: 398 us -> 361 us (0.907)
  blocking collectives: 144 us -> 52.3 us
  waiting for transfers between devices: 120 us -> 173 us
  local copies, waits for them, and re-layouts: 34.8 us -> 5.8 us
  starting transfers between devices: 35.5 us -> 59.2 us
  Pallas kernels: 44.8 us -> 54.1 us
    ppermute x3 -> x2, waiting for transfers between devices: 117 us -> 0.01 us  [placed_weights(): crossed = [lax.ppermute(w, ALL, across) for w in weights]]
    all_to_all x2 -> x4, waiting for transfers between devices: 2.18 us -> 98.1 us  [swap(): return lax.all_to_all(value, axis, split_axis=0, concat_axis=0, tiled=True)]
    all_to_all x3 -> x1, blocking collectives: 144 us -> 52.3 us  [swap(): return lax.all_to_all(value, axis, split_axis=0, concat_axis=0, tiled=True)]
    ppermute x6 -> x7, waiting for transfers between devices: 0.02 us -> 50.1 us  [the longest x1 50.1 us: place_last(): crossed = list(crossed) + [lax.ppermute(last, ALL, across)]]
    reshape x6 -> x0, local copies, waits for them, and re-layouts: 29.2 us -> none  [the longest x1 7.01 us: on_device(): arrived = swap(outgoing.reshape(devices, half, width), ALL)]
    all_gather x1, waiting for transfers between devices: 0.01 us -> 24.3 us  [on_device(): keys = lax.all_gather(keys_here, 'node', axis=0, tiled=True)]
    all_to_all x2 -> x4, starting transfers between devices: 11.7 us -> 34.1 us  [swap(): return lax.all_to_all(value, axis, split_axis=0, concat_axis=0, tiled=True)]
    pallas_call x3 -> x6, Pallas kernels: 38.4 us -> 47.6 us  [the longest x1 19.8 us: experts(): pl.pallas_call(functools.partial(expert_kernel, cap=cap), out_shape=jax.S...]
  transfers between devices with their start and end apart: 12 -> 14, of which waited for: 4 -> 6; matrix products, arithmetic and copies ran while one was open for 6% -> 1% of each run, Pallas kernels for 5% -> 8%
where the time goes in v3:
time: 361 us; the launch traced here: 360 us
  waiting for transfers between devices  173 us (48%)
  starting transfers between devices  59.2 us (16%)
  Pallas kernels  54.1 us (15%)
  blocking collectives  52.3 us (14%)
  between operations  14.2 us (4%)
  local copies, waits for them, and re-layouts  5.8 us (2%)
    all_to_all x4, waiting for transfers between devices, swap(): return lax.all_to_all(value, axis, split_axis=0, concat_axis=0, tiled=True)  98.1 us
    all_to_all x1, blocking collectives, swap(): return lax.all_to_all(value, axis, split_axis=0, concat_axis=0, tiled=True)  52.3 us
    ppermute x1, waiting for transfers between devices, place_last(): crossed = list(crossed) + [lax.ppermute(last, ALL, across)]  50.1 us
    all_to_all x4, starting transfers between devices, swap(): return lax.all_to_all(value, axis, split_axis=0, concat_axis=0, tiled=True)  34.1 us
    all_gather x1, waiting for transfers between devices, on_device(): keys = lax.all_gather(keys_here, 'node', axis=0, tiled=True)  24.3 us
    pallas_call x1, Pallas kernels, experts(): pl.pallas_call(functools.partial(expert_kernel, cap=cap), out_shape=jax.S...  19.8 us
    pallas_call x1, Pallas kernels, attend_span(): pl.pallas_call(functools.partial(span_kernel, block=block), grid=(rows //...  9.38 us
    ppermute x2, starting transfers between devices, placed_weights(): crossed = [lax.ppermute(w, ALL, across) for w in weights]  9.32 us
  transfers between devices with their start and end apart: 14, of which 6 were waited for; matrix products, arithmetic and copies ran while one was open for 1% of the time, Pallas kernels for 8%

profile of v3, /device:TPU:1, one launch (start us, length us, event | category | flops | bytes accessed | tf_op | source)
XLA Modules:
  0.0 360.0 jit_solution(1715273327888103636)
XLA Ops:
  7.2 2.0 pad_maximum_fusion
  9.2 6.2 %collective-permute-start = (bf16[1,3584,512]{2,1,0:T(8,128)(2,1)}, bf16[1,3584,512]{2,1,0:T(8,128)(2,1)}, u32[]{:S(2)}, u32[]{:S(2)}) collective-permute-start(bf16[1,3584,512]{2,1,0:T(8,128)(2,1)} %refs_0_.1), channel_id=1, source_target_pairs={{1,0},{3,2},{5,4},{7,6},{9,8},{11,10},{13,12},{15,14},{16,17},{18,... | collective-permute-start | bytes 11010056 | tf_op jit(solution)/shard_map/ppermute | solution.py:356
  15.5 3.1 collective-permute-start.1
  18.5 1.5 copy.19.rot
  20.0 2.0 listed.1
  22.1 9.7 %all-to-all-start = ((bf16[128,24,128]{2,1,0:T(8,128)(2,1)}), bf16[128,24,128]{2,1,0:T(8,128)(2,1)S(1)}, u32[]{:S(2)}, u32[]{:S(2)}) async-start(bf16[128,24,128]{2,1,0:T(8,128)(2,1)} %bitcast.12), calls=%async_computation | async-start | bytes 1572864 | tf_op jit(solution)/shard_map/all_to_all | solution.py:25
  31.7 24.3 %all-gather.2.cloned.1.call-done.keys = bf16[4608,512]{1,0:T(8,128)(2,1)} async-done(((bf16[576,512]{1,0:T(8,128)(2,1)}), bf16[4608,512]{1,0:T(8,128)(2,1)}) %all-gather.2.cloned.1.call-update) | async-done | bytes 4718608 | tf_op jit(solution)/shard_map/all_gather | solution.py:484
  56.0 9.4 %attend_span.1 = (bf16[1024,512]{1,0:T(8,128)(2,1)}, f32[1024,1]{1,0:T(8,128)}, f32[1024,1]{1,0:T(8,128)}, f32[1024,512]{1,0:T(8,128)}) custom-call(bf16[512,256]{1,0:T(8,128)(2,1)} %q_nope.1, bf16[512,128]{1,0:T(8,128)(2,1)} %q_rope.3, bf16[4608,512]{1,0:T(8,128)(2,1)} %all-gather.2.cloned.1.call-done.keys, bf16[2,128,512]{2,1,0:T(8,128)(2,1)} %absorb_k.1), custom_call_target="tpu_custom_call" | custom-call | flops 10267656192 | bytes 8388608 | tf_op jit(solution)/shard_map/attend_span/pallas_call | solution.py:134
  65.4 39.8 %all-to-all-done.arrived = bf16[128,24,128]{2,1,0:T(8,128)(2,1)S(1)} async-done(((bf16[128,24,128]{2,1,0:T(8,128)(2,1)}), bf16[128,24,128]{2,1,0:T(8,128)(2,1)S(1)}, u32[]{:S(2)}, u32[]{:S(2)}) %all-to-all-start) | async-done | bytes 786464 | tf_op jit(solution)/shard_map/all_to_all | solution.py:25
  105.2 0.9 copy-done
  106.1 2.2 spread.1
  108.3 8.0 %all-to-all-start.1 = ((bf16[128,24,128]{2,1,0:T(8,128)(2,1)}), bf16[128,24,128]{2,1,0:T(8,128)(2,1)S(1)}, u32[]{:S(2)}, u32[]{:S(2)}) async-start(bf16[128,24,128]{2,1,0:T(8,128)(2,1)} %spread.1), calls=%async_computation.1 | async-start | bytes 1572864 | tf_op jit(solution)/shard_map/all_to_all | solution.py:25
  116.3 1.3 collective-permute-start.3
  117.6 8.0 %collective-permute-start.2 = (bf16[1,512,3584]{2,1,0:T(8,128)(2,1)}, bf16[1,512,3584]{2,1,0:T(8,128)(2,1)}, u32[]{:S(2)}, u32[]{:S(2)}) collective-permute-start(bf16[1,512,3584]{2,1,0:T(8,128)(2,1)} %refs_2_), channel_id=1, source_target_pairs={{1,0},{3,2},{5,4},{7,6},{9,8},{11,10},{13,12},{15,14},{16,17},{18,... | collective-permute-start | bytes 11010056 | tf_op jit(solution)/shard_map/ppermute | solution.py:360
  125.6 7.2 %all-to-all-done.1 = bf16[128,24,128]{2,1,0:T(8,128)(2,1)S(1)} async-done(((bf16[128,24,128]{2,1,0:T(8,128)(2,1)}), bf16[128,24,128]{2,1,0:T(8,128)(2,1)S(1)}, u32[]{:S(2)}, u32[]{:S(2)}) %all-to-all-start.1) | async-done | bytes 786464 | tf_op jit(solution)/shard_map/all_to_all | solution.py:25
  132.7 0.9 copy-done.1
  133.6 8.4 %attend_prefix.1 = bf16[512,3584]{1,0:T(8,128)(2,1)} custom-call(bf16[1024,512]{1,0:T(8,128)(2,1)} %get-tuple-element.17.refs_0_.q_lat, bf16[512,128]{1,0:T(8,128)(2,1)} %q_rope.3, bf16[3072,128]{1,0:T(8,128)(2,1)} %bitcast.13, f32[1024,1]{1,0:T(8,128)} %get-tuple-element.18.refs_1_.old_top, f32[1024,1]{1,0:T(8,128)} %get-tuple-element.19.refs_2_.old_total, ...), custom_call_target="tpu_custom_call" | custom-call | flops 6442450944 | bytes 10485760 | tf_op jit(solution)/shard_map/attend_prefix/pallas_call | solution.py:161
  142.0 4.6 %all-to-all-start.2 = ((bf16[16,32,3584]{2,1,0:T(8,128)(2,1)}), bf16[16,32,3584]{2,1,0:T(8,128)(2,1)}, u32[]{:S(2)}, u32[]{:S(2)}) async-start(bf16[16,32,3584]{2,1,0:T(8,128)(2,1)} %bitcast.10), calls=%async_computation.2 | async-start | bytes 7340032 | tf_op jit(solution)/shard_map/all_to_all | solution.py:25
  146.7 1.3 collective-permute-start.4
  148.0 1.3 collective-permute-start.5
  149.3 1.3 collective-permute-start.6
  150.6 50.1 %collective-permute-done.2.refs_5_ = bf16[1,512,3584]{2,1,0:T(8,128)(2,1)} collective-permute-done((bf16[1,512,3584]{2,1,0:T(8,128)(2,1)}, bf16[1,512,3584]{2,1,0:T(8,128)(2,1)}, u32[]{:S(2)}, u32[]{:S(2)}) %collective-permute-start.2) | collective-permute-done | bytes 3670048 | tf_op jit(solution)/shard_map/ppermute | solution.py:360
  200.7 1.3 collective-permute-start.7
  202.0 4.8 %all-to-all-done.2.terms = bf16[16,32,3584]{2,1,0:T(8,128)(2,1)} async-done(((bf16[16,32,3584]{2,1,0:T(8,128)(2,1)}), bf16[16,32,3584]{2,1,0:T(8,128)(2,1)}, u32[]{:S(2)}, u32[]{:S(2)}) %all-to-all-start.2) | async-done | bytes 3670048 | tf_op jit(solution)/shard_map/all_to_all | solution.py:25
  206.8 1.3 collective-permute-start.8
  209.4 1.2 copy.20.router
  210.6 6.5 %route.1 = (bf16[32,3584]{1,0:T(8,128)(2,1)}, bf16[1024,1792]{1,0:T(8,128)(2,1)}, bf16[64,1024]{1,0:T(8,128)(2,1)}) custom-call(bf16[16,32,3584]{2,1,0:T(8,128)(2,1)} %all-to-all-done.2.terms, bf16[32,3584]{1,0:T(8,128)(2,1)} %residual.1, bf16[1,3584]{1,0:T(2,128)(2,1)} %reshape.31.gain, bf16[3584,64]{1,0:T(8,128)(2,1)} %copy.20.router, s32[32,8]{1,0:T(8,128)} %copy.21.ids), custom_call_target="tpu_custom_call" | custom-call | tf_op jit(solution)/shard_map/route/pallas_call | solution.py:253
  217.1 11.9 %all-to-all-start.3 = ((bf16[128,8,1792]{2,1,0:T(8,128)(2,1)}), bf16[128,8,1792]{2,1,0:T(8,128)(2,1)}, u32[]{:S(2)}, u32[]{:S(2)}) async-start(bf16[128,8,1792]{2,1,0:T(8,128)(2,1)} %bitcast.11), calls=%async_computation.3 | async-start | bytes 7340032 | tf_op jit(solution)/shard_map/all_to_all | solution.py:25
  229.0 46.3 %all-to-all-done.3 = bf16[128,8,1792]{2,1,0:T(8,128)(2,1)} async-done(((bf16[128,8,1792]{2,1,0:T(8,128)(2,1)}), bf16[128,8,1792]{2,1,0:T(8,128)(2,1)}, u32[]{:S(2)}, u32[]{:S(2)}) %all-to-all-start.3) | async-done | bytes 3670048 | tf_op jit(solution)/shard_map/all_to_all | solution.py:25
  275.3 19.8 %experts.1 = bf16[1024,1792]{1,0:T(8,128)(2,1)} custom-call(bf16[1024,1792]{1,0:T(8,128)(2,1)} %bitcast.5.rows, bf16[1,3584,512]{2,1,0:T(8,128)(2,1)} %refs_0_.1, bf16[1,3584,512]{2,1,0:T(8,128)(2,1)} %refs_1_.1, bf16[1,512,3584]{2,1,0:T(8,128)(2,1)} %refs_2_, bf16[1,3584,512]{2,1,0:T(8,128)(2,1)} %collective-permute-done.refs_3_, ...), custom_call_target="tpu_custom_call" | custom-call | tf_op jit(solution)/shard_map/experts/pallas_call | solution.py:332
  295.1 52.3 %all_to_all.25 = bf16[128,8,1792]{2,1,0:T(8,128)(2,1)} all-to-all(bf16[128,8,1792]{2,1,0:T(8,128)(2,1)} %bitcast.8), channel_id=1, replica_groups=mesh['node'=8,'dev'=16] {'node','dev'}, dimensions={0} | all-to-all | bytes 7340032 | tf_op jit(solution)/shard_map/all_to_all | solution.py:25
  347.4 5.8 %combine.1 = bf16[32,3584]{1,0:T(8,128)(2,1)} custom-call(bf16[64,1024]{1,0:T(8,128)(2,1)} %get-tuple-element.27.shares, bf16[1024,1792]{1,0:T(8,128)(2,1)} %bitcast.9), custom_call_target="tpu_custom_call" | custom-call | tf_op jit(solution)/shard_map/combine/pallas_call | solution.py:386
  (20 shorter events, 1.4 us)
Async XLA Ops:
  7.2 48.9 %all-gather.2.cloned.1.call-start = ((), (), s32[]{:S(2)}) async-start(), calls=%async_computation.5 | async-start | bytes 5308416 | tf_op jit(solution)/shard_map/all_gather | solution.py:484
  9.2 99.1 %collective-permute-start = (bf16[1,3584,512]{2,1,0:T(8,128)(2,1)}, bf16[1,3584,512]{2,1,0:T(8,128)(2,1)}, u32[]{:S(2)}, u32[]{:S(2)}) collective-permute-start(bf16[1,3584,512]{2,1,0:T(8,128)(2,1)} %refs_0_.1), channel_id=1, source_target_pairs={{1,0},{3,2},{5,4},{7,6},{9,8},{11,10},{13,12},{15,14},{16,17},{18,... | collective-permute-start | bytes 11010056 | tf_op jit(solution)/shard_map/ppermute | solution.py:356
  15.5 92.9 %collective-permute-start.1 = (bf16[1,3584,512]{2,1,0:T(8,128)(2,1)}, bf16[1,3584,512]{2,1,0:T(8,128)(2,1)}, u32[]{:S(2)}, u32[]{:S(2)}) collective-permute-start(bf16[1,3584,512]{2,1,0:T(8,128)(2,1)} %refs_1_.1), channel_id=1, source_target_pairs={{1,0},{3,2},{5,4},{7,6},{9,8},{11,10},{13,12},{15,14},{16,17},{18,... | collective-permute-start | bytes 11010056 | tf_op jit(solution)/shard_map/ppermute | solution.py:356
  22.1 83.1 %all-to-all-start = ((bf16[128,24,128]{2,1,0:T(8,128)(2,1)}), bf16[128,24,128]{2,1,0:T(8,128)(2,1)S(1)}, u32[]{:S(2)}, u32[]{:S(2)}) async-start(bf16[128,24,128]{2,1,0:T(8,128)(2,1)} %bitcast.12), calls=%async_computation | async-start | bytes 1572864 | tf_op jit(solution)/shard_map/all_to_all | solution.py:25
  105.2 0.9 copy-start
  108.3 24.4 %all-to-all-start.1 = ((bf16[128,24,128]{2,1,0:T(8,128)(2,1)}), bf16[128,24,128]{2,1,0:T(8,128)(2,1)S(1)}, u32[]{:S(2)}, u32[]{:S(2)}) async-start(bf16[128,24,128]{2,1,0:T(8,128)(2,1)} %spread.1), calls=%async_computation.1 | async-start | bytes 1572864 | tf_op jit(solution)/shard_map/all_to_all | solution.py:25
  116.3 90.5 %collective-permute-start.3 = (bf16[1,3584,512]{2,1,0:T(8,128)(2,1)}, bf16[1,3584,512]{2,1,0:T(8,128)(2,1)}, u32[]{:S(2)}, u32[]{:S(2)}) collective-permute-start(bf16[1,3584,512]{2,1,0:T(8,128)(2,1)} %refs_0_.1), channel_id=1, source_target_pairs={{0,16},{2,18},{4,20},{6,22},{8,24},{10,26},{12,28},{14,30},{17,1},... | collective-permute-start | bytes 11010056 | tf_op jit(solution)/shard_map/ppermute | solution.py:361
  117.6 83.1 %collective-permute-start.2 = (bf16[1,512,3584]{2,1,0:T(8,128)(2,1)}, bf16[1,512,3584]{2,1,0:T(8,128)(2,1)}, u32[]{:S(2)}, u32[]{:S(2)}) collective-permute-start(bf16[1,512,3584]{2,1,0:T(8,128)(2,1)} %refs_2_), channel_id=1, source_target_pairs={{1,0},{3,2},{5,4},{7,6},{9,8},{11,10},{13,12},{15,14},{16,17},{18,... | collective-permute-start | bytes 11010056 | tf_op jit(solution)/shard_map/ppermute | solution.py:360
  132.7 0.9 copy-start.1
  142.0 66.1 %copy-start.3 = (bf16[3584]{0:T(1024)(128)(2,1)S(1)}, bf16[3584]{0:T(1024)(128)(2,1)}, u32[]{:S(2)}) copy-start(bf16[3584]{0:T(1024)(128)(2,1)} %param.28) | copy-start | bytes 21508
  142.0 66.7 %copy-start.4 = (s32[32,8]{0,1:T(8,128)S(1)}, s32[32,8]{0,1:T(8,128)}, u32[]{:S(2)}) copy-start(s32[32,8]{0,1:T(8,128)} %param.30) | copy-start | bytes 3076
  142.0 67.3 %copy-start.2 = (bf16[3584,64]{0,1:T(8,128)(2,1)S(1)}, bf16[3584,64]{0,1:T(8,128)(2,1)}, u32[]{:S(2)}) copy-start(bf16[3584,64]{0,1:T(8,128)(2,1)} %param.29) | copy-start | bytes 1376260
  142.0 64.7 %all-to-all-start.2 = ((bf16[16,32,3584]{2,1,0:T(8,128)(2,1)}), bf16[16,32,3584]{2,1,0:T(8,128)(2,1)}, u32[]{:S(2)}, u32[]{:S(2)}) async-start(bf16[16,32,3584]{2,1,0:T(8,128)(2,1)} %bitcast.10), calls=%async_computation.2 | async-start | bytes 7340032 | tf_op jit(solution)/shard_map/all_to_all | solution.py:25
  146.7 82.3 %collective-permute-start.4 = (bf16[1,3584,512]{2,1,0:T(8,128)(2,1)}, bf16[1,3584,512]{2,1,0:T(8,128)(2,1)}, u32[]{:S(2)}, u32[]{:S(2)}) collective-permute-start(bf16[1,3584,512]{2,1,0:T(8,128)(2,1)} %refs_1_.1), channel_id=1, source_target_pairs={{0,16},{2,18},{4,20},{6,22},{8,24},{10,26},{12,28},{14,30},{17,1},... | collective-permute-start | bytes 11010056 | tf_op jit(solution)/shard_map/ppermute | solution.py:361
  148.0 81.0 %collective-permute-start.5 = (bf16[1,512,3584]{2,1,0:T(8,128)(2,1)}, bf16[1,512,3584]{2,1,0:T(8,128)(2,1)}, u32[]{:S(2)}, u32[]{:S(2)}) collective-permute-start(bf16[1,512,3584]{2,1,0:T(8,128)(2,1)} %refs_2_), channel_id=1, source_target_pairs={{0,16},{2,18},{4,20},{6,22},{8,24},{10,26},{12,28},{14,30},{17,1},... | collective-permute-start | bytes 11010056 | tf_op jit(solution)/shard_map/ppermute | solution.py:361
  149.3 79.7 %collective-permute-start.6 = (bf16[1,3584,512]{2,1,0:T(8,128)(2,1)}, bf16[1,3584,512]{2,1,0:T(8,128)(2,1)}, u32[]{:S(2)}, u32[]{:S(2)}) collective-permute-start(bf16[1,3584,512]{2,1,0:T(8,128)(2,1)} %collective-permute-done.refs_3_), channel_id=1, source_target_pairs={{0,16},{2,18},{4,20},{6,22},{8,24},{10,26},{12,28},{14,30},{17,1},... | collective-permute-start | bytes 11010056 | tf_op jit(solution)/shard_map/ppermute | solution.py:364
  200.7 28.3 %collective-permute-start.7 = (bf16[1,3584,512]{2,1,0:T(8,128)(2,1)}, bf16[1,3584,512]{2,1,0:T(8,128)(2,1)}, u32[]{:S(2)}, u32[]{:S(2)}) collective-permute-start(bf16[1,3584,512]{2,1,0:T(8,128)(2,1)} %collective-permute-done.1.refs_4_), channel_id=1, source_target_pairs={{0,16},{2,18},{4,20},{6,22},{8,24},{10,26},{12,28},{14,30},{17,1},... | collective-permute-start | bytes 11010056 | tf_op jit(solution)/shard_map/ppermute | solution.py:364
  206.8 68.5 %collective-permute-start.8 = (bf16[1,512,3584]{2,1,0:T(8,128)(2,1)}, bf16[1,512,3584]{2,1,0:T(8,128)(2,1)}, u32[]{:S(2)}, u32[]{:S(2)}) collective-permute-start(bf16[1,512,3584]{2,1,0:T(8,128)(2,1)} %collective-permute-done.2.refs_5_), channel_id=1, source_target_pairs={{0,16},{2,18},{4,20},{6,22},{8,24},{10,26},{12,28},{14,30},{17,1},... | collective-permute-start | bytes 11010056 | tf_op jit(solution)/shard_map/ppermute | solution.py:364
  217.1 58.2 %all-to-all-start.3 = ((bf16[128,8,1792]{2,1,0:T(8,128)(2,1)}), bf16[128,8,1792]{2,1,0:T(8,128)(2,1)}, u32[]{:S(2)}, u32[]{:S(2)}) async-start(bf16[128,8,1792]{2,1,0:T(8,128)(2,1)} %bitcast.11), calls=%async_computation.3 | async-start | bytes 7340032 | tf_op jit(solution)/shard_map/all_to_all | solution.py:25
Sparse Core Ops, SparseCore 0:
  9.7 46.3 all-gather.1

commit v4 on v3

--- a/solution.py
+++ b/solution.py
@@ -196,7 +196,7 @@
 
 def route_kernel(terms, residual, gain, router, ids, attended, outgoing, shares, *, nodes, cap):
     groups, tokens, width = terms.shape
-    experts = router.shape[1]
+    experts = router.shape[0]
     top_k = ids.shape[1]
     acc = terms[0].astype(F32)
     for g in range(1, groups):
@@ -206,7 +206,7 @@
     stream = stream.astype(F32)
     mean = jnp.mean(stream * stream, axis=1, keepdims=True)
     normed = (stream * lax.rsqrt(mean + NORM_EPS) * gain[...].astype(F32)).astype(BF16)
-    logits = dot(normed, router[...])
+    logits = dot(normed, router[...], (((1,), (1,)), ((), ())))
     expert = lax.broadcasted_iota(jnp.int32, (tokens, experts), 1)
     hits = [ids[:, j : j + 1] == expert for j in range(top_k)]
     gates = [
@@ -248,7 +248,7 @@
 
 def route(terms, residual, gain, router, ids, nodes, cap):
     tokens, width = residual.shape
-    rows = 2 * router.shape[1] * cap
+    rows = 2 * router.shape[0] * cap
     whole = pl.BlockSpec(memory_space=pltpu.VMEM)
     return pl.pallas_call(
         functools.partial(route_kernel, nodes=nodes, cap=cap),
@@ -352,7 +352,7 @@
         for dev in range(devs):
             if node % 2 == dev % 2:
                 across.append((node * devs + (dev ^ 1), node * devs + dev))
-                beside.append((node * devs + dev, (node ^ 1) * devs + dev))
+            beside.append((node * devs + dev, (node ^ 1) * devs + dev))
     crossed = [lax.ppermute(w, ALL, across) for w in weights]
 
     def place_last(crossed, last):
@@ -369,14 +369,23 @@
     return crossed, place_last
 
 
-def combine_kernel(shares, returned, out):
+def combine_kernel(shares, returned, out, total):
     tokens, width = out.shape
-    tile = returned.shape[1]
-    both = dot(shares[...], returned[...]).astype(BF16)
-    at = pl.multiple_of(pl.program_id(0) * tile, 128)
-    out[:, pl.ds(at, tile)] = both[:tokens]
-    at = pl.multiple_of(width // 2 + pl.program_id(0) * tile, 128)
-    out[:, pl.ds(at, tile)] = both[tokens:]
+    part = dot(shares[...], returned[...])
+    step = pl.program_id(0)
+
+    @pl.when(step == 0)
+    def _():
+        total[...] = part
+
+    @pl.when(step > 0)
+    def _():
+        total[...] += part
+
+    @pl.when(step == pl.num_programs(0) - 1)
+    def _():
+        out[:, : width // 2] = total[:tokens].astype(BF16)
+        out[:, width // 2 :] = total[tokens:].astype(BF16)
 
 
 def combine(shares, returned):
@@ -385,13 +394,14 @@
     tile = 256
     return pl.pallas_call(
         combine_kernel,
-        grid=(narrow // tile,),
+        grid=(rows // tile,),
         out_shape=jax.ShapeDtypeStruct((tokens, 2 * narrow), BF16),
         in_specs=[
-            pl.BlockSpec((2 * tokens, rows), lambda i: (0, 0)),
-            pl.BlockSpec((rows, tile), lambda i: (0, i)),
+            pl.BlockSpec((2 * tokens, tile), lambda i: (0, i)),
+            pl.BlockSpec((tile, narrow), lambda i: (i, 0)),
         ],
         out_specs=pl.BlockSpec((tokens, 2 * narrow), lambda i: (0, 0)),
+        scratch_shapes=[pltpu.VMEM((2 * tokens, narrow), F32)],
         compiler_params=pltpu.CompilerParams(vmem_limit_bytes=VMEM_BYTES),
         name="combine",
     )(shares, returned)
@@ -494,7 +504,7 @@
     terms = swap(terms.reshape(dev_count, tokens, width), "dev")
     terms, crossed[2] = lax.optimization_barrier((terms, crossed[2]))
     attended, outgoing, shares = route(
-        terms, residual, norm_gain.reshape(1, width), router, expert_ids, node_count, cap
+        terms, residual, norm_gain.reshape(1, width), router.T, expert_ids, node_count, cap
     )
     arrived = swap(outgoing.reshape(devices, cap, width // 2), ALL)
     served = experts(arrived.reshape(devices * cap, width // 2), finish(crossed), cap)

time: 361 us -> 354 us (0.981)
  starting transfers between devices: 59.2 us -> 51.6 us
where the time goes in v4:
time: 354 us; the launch traced here: 353 us
  waiting for transfers between devices  176 us (50%)
  Pallas kernels  52.4 us (15%)
  blocking collectives  52.3 us (15%)
  starting transfers between devices  51.6 us (15%)
  between operations  14.1 us (4%)
  local copies, waits for them, and re-layouts  4.6 us (1%)
    all_to_all x4, waiting for transfers between devices, swap(): return lax.all_to_all(value, axis, split_axis=0, concat_axis=0, tiled=True)  100 us
    all_to_all x1, blocking collectives, swap(): return lax.all_to_all(value, axis, split_axis=0, concat_axis=0, tiled=True)  52.3 us
    ppermute x1, waiting for transfers between devices, place_last(): crossed = list(crossed) + [lax.ppermute(last, ALL, across)]  51.7 us
    all_to_all x4, starting transfers between devices, swap(): return lax.all_to_all(value, axis, split_axis=0, concat_axis=0, tiled=True)  32.4 us
    all_gather x1, waiting for transfers between devices, on_device(): keys = lax.all_gather(keys_here, 'node', axis=0, tiled=True)  24.4 us
    pallas_call x1, Pallas kernels, experts(): pl.pallas_call(functools.partial(expert_kernel, cap=cap), out_shape=jax.S...  19.8 us
    pallas_call x1, Pallas kernels, attend_span(): pl.pallas_call(functools.partial(span_kernel, block=block), grid=(rows //...  9.33 us
    ppermute x2, starting transfers between devices, placed_weights(): crossed = [lax.ppermute(w, ALL, across) for w in weights]  9.28 us
  transfers between devices with their start and end apart: 14, of which 6 were waited for; matrix products, arithmetic and copies ran while one was open for 1% of the time, Pallas kernels for 8%

profile of v4, /device:TPU:1, one launch (start us, length us, event | category | flops | bytes accessed | tf_op | source)
XLA Modules:
  0.0 353.5 jit_solution(365105310911405177)
XLA Ops:
  7.2 2.0 pad_maximum_fusion
  9.2 6.2 %collective-permute-start = (bf16[1,3584,512]{2,1,0:T(8,128)(2,1)}, bf16[1,3584,512]{2,1,0:T(8,128)(2,1)}, u32[]{:S(2)}, u32[]{:S(2)}) collective-permute-start(bf16[1,3584,512]{2,1,0:T(8,128)(2,1)} %refs_0_.1), channel_id=1, source_target_pairs={{1,0},{3,2},{5,4},{7,6},{9,8},{11,10},{13,12},{15,14},{16,17},{18,... | collective-permute-start | bytes 11010056 | tf_op jit(solution)/shard_map/ppermute | solution.py:356
  15.4 3.1 collective-permute-start.1
  18.5 1.5 copy.19.rot
  20.0 2.0 listed.1
  22.0 9.7 %all-to-all-start = ((bf16[128,24,128]{2,1,0:T(8,128)(2,1)}), bf16[128,24,128]{2,1,0:T(8,128)(2,1)S(1)}, u32[]{:S(2)}, u32[]{:S(2)}) async-start(bf16[128,24,128]{2,1,0:T(8,128)(2,1)} %bitcast.13), calls=%async_computation | async-start | bytes 1572864 | tf_op jit(solution)/shard_map/all_to_all | solution.py:25
  31.7 24.4 %all-gather.2.cloned.1.call-done.keys = bf16[4608,512]{1,0:T(8,128)(2,1)} async-done(((bf16[576,512]{1,0:T(8,128)(2,1)}), bf16[4608,512]{1,0:T(8,128)(2,1)}) %all-gather.2.cloned.1.call-update) | async-done | bytes 4718608 | tf_op jit(solution)/shard_map/all_gather | solution.py:494
  56.0 9.3 %attend_span.1 = (bf16[1024,512]{1,0:T(8,128)(2,1)}, f32[1024,1]{1,0:T(8,128)}, f32[1024,1]{1,0:T(8,128)}, f32[1024,512]{1,0:T(8,128)}) custom-call(bf16[512,256]{1,0:T(8,128)(2,1)} %q_nope.1, bf16[512,128]{1,0:T(8,128)(2,1)} %q_rope.3, bf16[4608,512]{1,0:T(8,128)(2,1)} %all-gather.2.cloned.1.call-done.keys, bf16[2,128,512]{2,1,0:T(8,128)(2,1)} %absorb_k.1), custom_call_target="tpu_custom_call" | custom-call | flops 10267656192 | bytes 8388608 | tf_op jit(solution)/shard_map/attend_span/pallas_call | solution.py:134
  65.4 39.8 %all-to-all-done.arrived = bf16[128,24,128]{2,1,0:T(8,128)(2,1)S(1)} async-done(((bf16[128,24,128]{2,1,0:T(8,128)(2,1)}), bf16[128,24,128]{2,1,0:T(8,128)(2,1)S(1)}, u32[]{:S(2)}, u32[]{:S(2)}) %all-to-all-start) | async-done | bytes 786464 | tf_op jit(solution)/shard_map/all_to_all | solution.py:25
  105.2 0.9 copy-done
  106.1 2.2 spread.1
  108.4 8.0 %all-to-all-start.1 = ((bf16[128,24,128]{2,1,0:T(8,128)(2,1)}), bf16[128,24,128]{2,1,0:T(8,128)(2,1)S(1)}, u32[]{:S(2)}, u32[]{:S(2)}) async-start(bf16[128,24,128]{2,1,0:T(8,128)(2,1)} %spread.1), calls=%async_computation.1 | async-start | bytes 1572864 | tf_op jit(solution)/shard_map/all_to_all | solution.py:25
  116.3 1.1 collective-permute-start.3
  117.5 4.6 %collective-permute-start.2 = (bf16[1,512,3584]{2,1,0:T(8,128)(2,1)}, bf16[1,512,3584]{2,1,0:T(8,128)(2,1)}, u32[]{:S(2)}, u32[]{:S(2)}) collective-permute-start(bf16[1,512,3584]{2,1,0:T(8,128)(2,1)} %refs_2_), channel_id=1, source_target_pairs={{1,0},{3,2},{5,4},{7,6},{9,8},{11,10},{13,12},{15,14},{16,17},{18,... | collective-permute-start | bytes 11010056 | tf_op jit(solution)/shard_map/ppermute | solution.py:360
  122.1 10.7 %all-to-all-done.1 = bf16[128,24,128]{2,1,0:T(8,128)(2,1)S(1)} async-done(((bf16[128,24,128]{2,1,0:T(8,128)(2,1)}), bf16[128,24,128]{2,1,0:T(8,128)(2,1)S(1)}, u32[]{:S(2)}, u32[]{:S(2)}) %all-to-all-start.1) | async-done | bytes 786464 | tf_op jit(solution)/shard_map/all_to_all | solution.py:25
  132.8 0.9 copy-done.1
  133.7 8.4 %attend_prefix.1 = bf16[512,3584]{1,0:T(8,128)(2,1)} custom-call(bf16[1024,512]{1,0:T(8,128)(2,1)} %get-tuple-element.17.refs_0_.q_lat, bf16[512,128]{1,0:T(8,128)(2,1)} %q_rope.3, bf16[3072,128]{1,0:T(8,128)(2,1)} %bitcast.14, f32[1024,1]{1,0:T(8,128)} %get-tuple-element.18.refs_1_.old_top, f32[1024,1]{1,0:T(8,128)} %get-tuple-element.19.refs_2_.old_total, ...), custom_call_target="tpu_custom_call" | custom-call | flops 6442450944 | bytes 10485760 | tf_op jit(solution)/shard_map/attend_prefix/pallas_call | solution.py:161
  142.1 4.7 %all-to-all-start.2 = ((bf16[16,32,3584]{2,1,0:T(8,128)(2,1)}), bf16[16,32,3584]{2,1,0:T(8,128)(2,1)}, u32[]{:S(2)}, u32[]{:S(2)}) async-start(bf16[16,32,3584]{2,1,0:T(8,128)(2,1)} %bitcast.11), calls=%async_computation.2 | async-start | bytes 7340032 | tf_op jit(solution)/shard_map/all_to_all | solution.py:25
  146.7 1.1 collective-permute-start.4
  147.9 0.1 collective-permute-start.5
  148.0 0.4 collective-permute-start.6
  148.4 51.7 %collective-permute-done.2.refs_5_ = bf16[1,512,3584]{2,1,0:T(8,128)(2,1)} collective-permute-done((bf16[1,512,3584]{2,1,0:T(8,128)(2,1)}, bf16[1,512,3584]{2,1,0:T(8,128)(2,1)}, u32[]{:S(2)}, u32[]{:S(2)}) %collective-permute-start.2) | collective-permute-done | bytes 3670048 | tf_op jit(solution)/shard_map/ppermute | solution.py:360
  200.1 2.5 collective-permute-start.7
  202.6 3.5 %all-to-all-done.2.terms = bf16[16,32,3584]{2,1,0:T(8,128)(2,1)} async-done(((bf16[16,32,3584]{2,1,0:T(8,128)(2,1)}), bf16[16,32,3584]{2,1,0:T(8,128)(2,1)}, u32[]{:S(2)}, u32[]{:S(2)}) %all-to-all-start.2) | async-done | bytes 3670048 | tf_op jit(solution)/shard_map/all_to_all | solution.py:25
  206.1 0.6 reshape.31.gain
  206.7 0.7 copy.20.ids
  207.4 6.5 %route.1 = (bf16[32,3584]{1,0:T(8,128)(2,1)}, bf16[1024,1792]{1,0:T(8,128)(2,1)}, bf16[64,1024]{1,0:T(8,128)(2,1)}) custom-call(bf16[16,32,3584]{2,1,0:T(8,128)(2,1)} %all-to-all-done.2.terms, bf16[32,3584]{1,0:T(8,128)(2,1)} %residual.1, bf16[1,3584]{1,0:T(2,128)(2,1)} %reshape.31.gain, bf16[64,3584]{1,0:T(8,128)(2,1)} %bitcast.15, s32[32,8]{1,0:T(8,128)} %copy.20.ids), custom_call_target="tpu_custom_call" | custom-call | tf_op jit(solution)/shard_map/route/pallas_call | solution.py:253
  213.9 10.1 %all-to-all-start.3 = ((bf16[128,8,1792]{2,1,0:T(8,128)(2,1)}), bf16[128,8,1792]{2,1,0:T(8,128)(2,1)}, u32[]{:S(2)}, u32[]{:S(2)}) async-start(bf16[128,8,1792]{2,1,0:T(8,128)(2,1)} %bitcast.12), calls=%async_computation.3 | async-start | bytes 7340032 | tf_op jit(solution)/shard_map/all_to_all | solution.py:25
  224.1 46.3 %all-to-all-done.3 = bf16[128,8,1792]{2,1,0:T(8,128)(2,1)} async-done(((bf16[128,8,1792]{2,1,0:T(8,128)(2,1)}), bf16[128,8,1792]{2,1,0:T(8,128)(2,1)}, u32[]{:S(2)}, u32[]{:S(2)}) %all-to-all-start.3) | async-done | bytes 3670048 | tf_op jit(solution)/shard_map/all_to_all | solution.py:25
  270.4 19.8 %experts.1 = bf16[1024,1792]{1,0:T(8,128)(2,1)} custom-call(bf16[1024,1792]{1,0:T(8,128)(2,1)} %bitcast.6.rows, bf16[1,3584,512]{2,1,0:T(8,128)(2,1)} %refs_0_.1, bf16[1,3584,512]{2,1,0:T(8,128)(2,1)} %refs_1_.1, bf16[1,512,3584]{2,1,0:T(8,128)(2,1)} %refs_2_, bf16[1,3584,512]{2,1,0:T(8,128)(2,1)} %collective-permute-done.refs_3_, ...), custom_call_target="tpu_custom_call" | custom-call | tf_op jit(solution)/shard_map/experts/pallas_call | solution.py:332
  290.2 52.3 %all_to_all.25 = bf16[128,8,1792]{2,1,0:T(8,128)(2,1)} all-to-all(bf16[128,8,1792]{2,1,0:T(8,128)(2,1)} %bitcast.9), channel_id=1, replica_groups=mesh['node'=8,'dev'=16] {'node','dev'}, dimensions={0} | all-to-all | bytes 7340032 | tf_op jit(solution)/shard_map/all_to_all | solution.py:25
  342.5 4.2 %combine.1 = bf16[32,3584]{1,0:T(8,128)(2,1)} custom-call(bf16[64,1024]{1,0:T(8,128)(2,1)} %get-tuple-element.27.shares, bf16[1024,1792]{1,0:T(8,128)(2,1)} %bitcast.10), custom_call_target="tpu_custom_call" | custom-call | tf_op jit(solution)/shard_map/combine/pallas_call | solution.py:395
  (17 shorter events, 0.1 us)
Async XLA Ops:
  7.2 48.9 %all-gather.2.cloned.1.call-start = ((), (), s32[]{:S(2)}) async-start(), calls=%async_computation.5 | async-start | bytes 5308416 | tf_op jit(solution)/shard_map/all_gather | solution.py:494
  9.2 99.2 %collective-permute-start = (bf16[1,3584,512]{2,1,0:T(8,128)(2,1)}, bf16[1,3584,512]{2,1,0:T(8,128)(2,1)}, u32[]{:S(2)}, u32[]{:S(2)}) collective-permute-start(bf16[1,3584,512]{2,1,0:T(8,128)(2,1)} %refs_0_.1), channel_id=1, source_target_pairs={{1,0},{3,2},{5,4},{7,6},{9,8},{11,10},{13,12},{15,14},{16,17},{18,... | collective-permute-start | bytes 11010056 | tf_op jit(solution)/shard_map/ppermute | solution.py:356
  15.4 93.0 %collective-permute-start.1 = (bf16[1,3584,512]{2,1,0:T(8,128)(2,1)}, bf16[1,3584,512]{2,1,0:T(8,128)(2,1)}, u32[]{:S(2)}, u32[]{:S(2)}) collective-permute-start(bf16[1,3584,512]{2,1,0:T(8,128)(2,1)} %refs_1_.1), channel_id=1, source_target_pairs={{1,0},{3,2},{5,4},{7,6},{9,8},{11,10},{13,12},{15,14},{16,17},{18,... | collective-permute-start | bytes 11010056 | tf_op jit(solution)/shard_map/ppermute | solution.py:356
  22.0 83.2 %all-to-all-start = ((bf16[128,24,128]{2,1,0:T(8,128)(2,1)}), bf16[128,24,128]{2,1,0:T(8,128)(2,1)S(1)}, u32[]{:S(2)}, u32[]{:S(2)}) async-start(bf16[128,24,128]{2,1,0:T(8,128)(2,1)} %bitcast.13), calls=%async_computation | async-start | bytes 1572864 | tf_op jit(solution)/shard_map/all_to_all | solution.py:25
  105.2 0.9 copy-start
  108.4 24.4 %all-to-all-start.1 = ((bf16[128,24,128]{2,1,0:T(8,128)(2,1)}), bf16[128,24,128]{2,1,0:T(8,128)(2,1)S(1)}, u32[]{:S(2)}, u32[]{:S(2)}) async-start(bf16[128,24,128]{2,1,0:T(8,128)(2,1)} %spread.1), calls=%async_computation.1 | async-start | bytes 1572864 | tf_op jit(solution)/shard_map/all_to_all | solution.py:25
  116.3 89.8 %collective-permute-start.3 = (bf16[1,3584,512]{2,1,0:T(8,128)(2,1)}, bf16[1,3584,512]{2,1,0:T(8,128)(2,1)}, u32[]{:S(2)}, u32[]{:S(2)}) collective-permute-start(bf16[1,3584,512]{2,1,0:T(8,128)(2,1)} %refs_0_.1), channel_id=1, source_target_pairs={{0,16},{1,17},{2,18},{3,19},{4,20},{5,21},{6,22},{7,23},{8,24},{9,... | collective-permute-start | bytes 11010056 | tf_op jit(solution)/shard_map/ppermute | solution.py:361
  117.5 82.6 %collective-permute-start.2 = (bf16[1,512,3584]{2,1,0:T(8,128)(2,1)}, bf16[1,512,3584]{2,1,0:T(8,128)(2,1)}, u32[]{:S(2)}, u32[]{:S(2)}) collective-permute-start(bf16[1,512,3584]{2,1,0:T(8,128)(2,1)} %refs_2_), channel_id=1, source_target_pairs={{1,0},{3,2},{5,4},{7,6},{9,8},{11,10},{13,12},{15,14},{16,17},{18,... | collective-permute-start | bytes 11010056 | tf_op jit(solution)/shard_map/ppermute | solution.py:360
  132.8 0.9 copy-start.1
  142.1 64.0 %copy-start.2 = (bf16[3584]{0:T(1024)(128)(2,1)S(1)}, bf16[3584]{0:T(1024)(128)(2,1)}, u32[]{:S(2)}) copy-start(bf16[3584]{0:T(1024)(128)(2,1)} %param.28) | copy-start | bytes 21508
  142.1 64.7 %copy-start.3 = (s32[32,8]{0,1:T(8,128)S(1)}, s32[32,8]{0,1:T(8,128)}, u32[]{:S(2)}) copy-start(s32[32,8]{0,1:T(8,128)} %param.30) | copy-start | bytes 3076
  142.1 64.0 %all-to-all-start.2 = ((bf16[16,32,3584]{2,1,0:T(8,128)(2,1)}), bf16[16,32,3584]{2,1,0:T(8,128)(2,1)}, u32[]{:S(2)}, u32[]{:S(2)}) async-start(bf16[16,32,3584]{2,1,0:T(8,128)(2,1)} %bitcast.11), calls=%async_computation.2 | async-start | bytes 7340032 | tf_op jit(solution)/shard_map/all_to_all | solution.py:25
  146.7 77.3 %collective-permute-start.4 = (bf16[1,3584,512]{2,1,0:T(8,128)(2,1)}, bf16[1,3584,512]{2,1,0:T(8,128)(2,1)}, u32[]{:S(2)}, u32[]{:S(2)}) collective-permute-start(bf16[1,3584,512]{2,1,0:T(8,128)(2,1)} %refs_1_.1), channel_id=1, source_target_pairs={{0,16},{1,17},{2,18},{3,19},{4,20},{5,21},{6,22},{7,23},{8,24},{9,... | collective-permute-start | bytes 11010056 | tf_op jit(solution)/shard_map/ppermute | solution.py:361
  147.9 76.2 %collective-permute-start.5 = (bf16[1,512,3584]{2,1,0:T(8,128)(2,1)}, bf16[1,512,3584]{2,1,0:T(8,128)(2,1)}, u32[]{:S(2)}, u32[]{:S(2)}) collective-permute-start(bf16[1,512,3584]{2,1,0:T(8,128)(2,1)} %refs_2_), channel_id=1, source_target_pairs={{0,16},{1,17},{2,18},{3,19},{4,20},{5,21},{6,22},{7,23},{8,24},{9,... | collective-permute-start | bytes 11010056 | tf_op jit(solution)/shard_map/ppermute | solution.py:361
  148.0 76.1 %collective-permute-start.6 = (bf16[1,3584,512]{2,1,0:T(8,128)(2,1)}, bf16[1,3584,512]{2,1,0:T(8,128)(2,1)}, u32[]{:S(2)}, u32[]{:S(2)}) collective-permute-start(bf16[1,3584,512]{2,1,0:T(8,128)(2,1)} %collective-permute-done.refs_3_), channel_id=1, source_target_pairs={{0,16},{1,17},{2,18},{3,19},{4,20},{5,21},{6,22},{7,23},{8,24},{9,... | collective-permute-start | bytes 11010056 | tf_op jit(solution)/shard_map/ppermute | solution.py:364
  200.1 24.0 %collective-permute-start.7 = (bf16[1,3584,512]{2,1,0:T(8,128)(2,1)}, bf16[1,3584,512]{2,1,0:T(8,128)(2,1)}, u32[]{:S(2)}, u32[]{:S(2)}) collective-permute-start(bf16[1,3584,512]{2,1,0:T(8,128)(2,1)} %collective-permute-done.1.refs_4_), channel_id=1, source_target_pairs={{0,16},{1,17},{2,18},{3,19},{4,20},{5,21},{6,22},{7,23},{8,24},{9,... | collective-permute-start | bytes 11010056 | tf_op jit(solution)/shard_map/ppermute | solution.py:364
  206.1 64.2 %collective-permute-start.8 = (bf16[1,512,3584]{2,1,0:T(8,128)(2,1)}, bf16[1,512,3584]{2,1,0:T(8,128)(2,1)}, u32[]{:S(2)}, u32[]{:S(2)}) collective-permute-start(bf16[1,512,3584]{2,1,0:T(8,128)(2,1)} %collective-permute-done.2.refs_5_), channel_id=1, source_target_pairs={{0,16},{1,17},{2,18},{3,19},{4,20},{5,21},{6,22},{7,23},{8,24},{9,... | collective-permute-start | bytes 11010056 | tf_op jit(solution)/shard_map/ppermute | solution.py:364
  213.9 56.5 %all-to-all-start.3 = ((bf16[128,8,1792]{2,1,0:T(8,128)(2,1)}), bf16[128,8,1792]{2,1,0:T(8,128)(2,1)}, u32[]{:S(2)}, u32[]{:S(2)}) async-start(bf16[128,8,1792]{2,1,0:T(8,128)(2,1)} %bitcast.12), calls=%async_computation.3 | async-start | bytes 7340032 | tf_op jit(solution)/shard_map/all_to_all | solution.py:25
Sparse Core Ops, SparseCore 0:
  9.7 46.3 all-gather.1

commit v5 on v4

--- a/solution.py
+++ b/solution.py
@@ -265,28 +265,35 @@
 
 
 def expert_kernel(rows, *refs, cap):
-    sources, (out, whole_rows, gates, ups, downs, sems) = refs[:12], refs[12:]
+    sources, (out, whole_rows, gates, ups, downs, sems) = refs[:14], refs[14:]
     node, dev = lax.axis_index("node"), lax.axis_index("dev")
     keeper = node % 2 == dev % 2
-    own, crossed, twin, twin_crossed = (sources[3 * i : 3 * i + 3] for i in range(4))
+    own, crossed, twin, twin_crossed = sources[:3], sources[3:7], sources[7:10], sources[10:]
     slots = (gates, ups, downs)
-
-    def copy(source, share, part):
-        return pltpu.make_async_copy(
-            source[part].at[0], slots[part].at[share], sems.at[share * 3 + part]
-        )
-
-    order = ((0, 0), (0, 1), (1, 0), (1, 1), (0, 2), (1, 2))
+    cut = ups.shape[1] // 2
+
+    def copies(first, second):
+        pieces = [(first[p].at[0], slots[p].at[0]) for p in range(3)]
+        pieces.append((second[0].at[0], gates.at[1]))
+        pieces.append((second[1].at[0], ups.at[1, pl.ds(0, cut)]))
+        pieces.append((second[2].at[0], ups.at[1, pl.ds(cut, cut)]))
+        pieces.append((second[3].at[0], downs.at[1]))
+        return [
+            pltpu.make_async_copy(here, there, sems.at[i]) for i, (here, there) in enumerate(pieces)
+        ]
+
+    order = (0, 1, 3, 4, 5, 2, 6)
+    kept, given = copies(own, crossed), copies(twin, twin_crossed)
 
     @pl.when(keeper)
     def _():
-        for share, part in order:
-            copy((own, crossed)[share], share, part).start()
+        for i in order:
+            kept[i].start()
 
     @pl.when(jnp.logical_not(keeper))
     def _():
-        for share, part in order:
-            copy((twin, twin_crossed)[share], share, part).start()
+        for i in order:
+            given[i].start()
 
     count, narrow = rows.shape
     block = 256
@@ -304,13 +311,14 @@
     x = whole_rows[...]
     hidden = []
     for share in range(2):
-        copy(own, share, 0).wait()
+        kept[3 * share].wait()
         gate_act = dot(x, gates[share])
-        copy(own, share, 1).wait()
+        for i in ((1,), (4, 5))[share]:
+            kept[i].wait()
         up_act = dot(x, ups[share])
         hidden.append((jax.nn.silu(gate_act) * up_act).astype(BF16))
-    for share in range(2):
-        copy(own, share, 2).wait()
+    for i in (2, 6):
+        kept[i].wait()
     step = narrow // 2
     for c in range(0, narrow, step):
         parts = []
@@ -332,14 +340,14 @@
     return pl.pallas_call(
         functools.partial(expert_kernel, cap=cap),
         out_shape=jax.ShapeDtypeStruct((count, narrow), BF16),
-        in_specs=[whole] + [pl.BlockSpec(memory_space=pl.ANY)] * 12,
+        in_specs=[whole] + [pl.BlockSpec(memory_space=pl.ANY)] * 14,
         out_specs=whole,
         scratch_shapes=[
             pltpu.VMEM((count // 2, width), BF16),
             pltpu.VMEM((2, width, hidden), BF16),
             pltpu.VMEM((2, width, hidden), BF16),
             pltpu.VMEM((2, hidden, width), BF16),
-            pltpu.SemaphoreType.DMA((6,)),
+            pltpu.SemaphoreType.DMA((7,)),
         ],
         compiler_params=pltpu.CompilerParams(vmem_limit_bytes=VMEM_BYTES),
         name="experts",
@@ -353,16 +361,17 @@
             if node % 2 == dev % 2:
                 across.append((node * devs + (dev ^ 1), node * devs + dev))
             beside.append((node * devs + dev, (node ^ 1) * devs + dev))
-    crossed = [lax.ppermute(w, ALL, across) for w in weights]
+    gate, up, down = weights
+    cut = up.shape[1] // 2
+    crossed = [lax.ppermute(w, ALL, across) for w in (gate, up[:, :cut], up[:, cut:])]
 
     def place_last(crossed, last):
-        own = list(weights) + [last]
         crossed = list(crossed) + [lax.ppermute(last, ALL, across)]
-        twin = [lax.ppermute(w, ALL, beside) for w in own]
+        twin = [lax.ppermute(w, ALL, beside) for w in weights]
 
         def finish(crossed):
             twin_crossed = [lax.ppermute(w, ALL, beside) for w in crossed]
-            return own + list(crossed) + twin + twin_crossed
+            return list(weights) + list(crossed) + twin + twin_crossed
 
         return crossed, finish
 
@@ -489,20 +498,22 @@
     expert_count = router.shape[1]
     cap = max(2, 2 * tokens * expert_ids.shape[1] // expert_count)
 
-    crossed, place_last = placed_weights((expert_gate, expert_up), node_count, dev_count)
+    crossed, place_last = placed_weights(
+        (expert_gate, expert_up, expert_down), node_count, dev_count
+    )
     keys_here = jnp.concatenate([kv_latent, k_rope.T], 0)
     keys = lax.all_gather(keys_here, "node", axis=0, tiled=True)
     state = attend_span(q_nope, q_rope, keys, absorb_k, keys_here.shape[0])
-    prefix, (state, crossed, expert_down) = listed_prefix(
-        pool_latent, pool_rope, block_table, devices, (state, crossed, expert_down)
-    )
-    crossed, finish = place_last(crossed, expert_down)
+    prefix, (state, crossed[:2], down) = listed_prefix(
+        pool_latent, pool_rope, block_table, devices, (state, crossed[:2], expert_down)
+    )
+    crossed, finish = place_last(crossed, down)
     terms = attend_prefix(
         state, q_rope, prefix, absorb_v, out_proj, absorb_k.shape[1], prefix_keys
     )
-    terms, crossed[1] = lax.optimization_barrier((terms, crossed[1]))
+    terms, crossed[:3] = lax.optimization_barrier((terms, crossed[:3]))
     terms = swap(terms.reshape(dev_count, tokens, width), "dev")
-    terms, crossed[2] = lax.optimization_barrier((terms, crossed[2]))
+    terms, crossed[3] = lax.optimization_barrier((terms, crossed[3]))
     attended, outgoing, shares = route(
         terms, residual, norm_gain.reshape(1, width), router.T, expert_ids, node_count, cap
     )

time: 354 us -> 339 us (0.958)
  waiting for transfers between devices: 176 us -> 154 us
  starting transfers between devices: 51.6 us -> 55.9 us
    all_to_all x4, waiting for transfers between devices: 100 us -> 76.8 us  [swap(): return lax.all_to_all(value, axis, split_axis=0, concat_axis=0, tiled=True)]
    all_gather x1, waiting for transfers between devices: 24.4 us -> 17.3 us  [on_device(): keys = lax.all_gather(keys_here, 'node', axis=0, tiled=True)]
    ppermute x3 -> x4, waiting for transfers between devices: 0.01 us -> 6.09 us  [finish(): twin_crossed = [lax.ppermute(w, ALL, beside) for w in crossed]]
    slice x0 -> x1, local copies, waits for them, and re-layouts: none -> 3.61 us  [placed_weights(): up[:, cut:]]
    ppermute x5 -> x6, starting transfers between devices: 11.6 us -> 14.6 us  [the longest x3 13.4 us: placed_weights(): lax.ppermute(w, ALL, across)]
  transfers between devices with their start and end apart: 14 -> 16, of which waited for: 6 -> 8; matrix products, arithmetic and copies ran while one was open for 1% -> 2% of each run, Pallas kernels for 8% -> 8%
where the time goes in v5:
time: 339 us; the launch traced here: 338 us
  waiting for transfers between devices  154 us (45%)
  starting transfers between devices  55.9 us (16%)
  Pallas kernels  52.6 us (16%)
  blocking collectives  52.3 us (15%)
  between operations  14.1 us (4%)
  local copies, waits for them, and re-layouts  7.47 us (2%)
    all_to_all x4, waiting for transfers between devices, swap(): return lax.all_to_all(value, axis, split_axis=0, concat_axis=0, tiled=True)  76.8 us
    ppermute x1, waiting for transfers between devices, place_last(): crossed = list(crossed) + [lax.ppermute(last, ALL, across)]  53.7 us
    all_to_all x1, blocking collectives, swap(): return lax.all_to_all(value, axis, split_axis=0, concat_axis=0, tiled=True)  52.3 us
    all_to_all x4, starting transfers between devices, swap(): return lax.all_to_all(value, axis, split_axis=0, concat_axis=0, tiled=True)  34.2 us
    pallas_call x1, Pallas kernels, experts(): pl.pallas_call(functools.partial(expert_kernel, cap=cap), out_shape=jax.S...  19.8 us
    all_gather x1, waiting for transfers between devices, on_device(): keys = lax.all_gather(keys_here, 'node', axis=0, tiled=True)  17.3 us
    ppermute x3, starting transfers between devices, placed_weights(): lax.ppermute(w, ALL, across)  13.4 us
    pallas_call x1, Pallas kernels, attend_span(): pl.pallas_call(functools.partial(span_kernel, block=block), grid=(rows //...  9.41 us
  transfers between devices with their start and end apart: 16, of which 8 were waited for; matrix products, arithmetic and copies ran while one was open for 2% of the time, Pallas kernels for 8%

profile of v5, /device:TPU:1, one launch (start us, length us, event | category | flops | bytes accessed | tf_op | source)
XLA Modules:
  0.0 338.3 jit_solution(12190578405630969961)
XLA Ops:
  7.2 2.0 pad_maximum_fusion
  9.2 6.2 %collective-permute-start = (bf16[1,3584,512]{2,1,0:T(8,128)(2,1)}, bf16[1,3584,512]{2,1,0:T(8,128)(2,1)}, u32[]{:S(2)}, u32[]{:S(2)}) collective-permute-start(bf16[1,3584,512]{2,1,0:T(8,128)(2,1)} %refs_0_.1), channel_id=1, source_target_pairs={{1,0},{3,2},{5,4},{7,6},{9,8},{11,10},{13,12},{15,14},{16,17},{18,... | collective-permute-start | bytes 11010056 | tf_op jit(solution)/shard_map/ppermute | solution.py:366
  15.4 3.6 %fusion = (bf16[1,1792,512]{2,1,0:T(8,128)(2,1)S(1)}, bf16[1,1792,512]{2,1,0:T(8,128)(2,1)}) fusion(bf16[1,3584,512]{2,1,0:T(8,128)(2,1)} %refs_1_.1), kind=kLoop, calls=%fused_computation.1 | loop fusion | bytes 7340032 | tf_op jit(solution)/shard_map/slice | solution.py:366
  19.0 2.6 collective-permute-start.1
  21.5 0.7 copy.19.rot
  22.3 2.0 listed.1
  24.3 9.6 %all-to-all-start = ((bf16[128,24,128]{2,1,0:T(8,128)(2,1)}), bf16[128,24,128]{2,1,0:T(8,128)(2,1)S(1)}, u32[]{:S(2)}, u32[]{:S(2)}) async-start(bf16[128,24,128]{2,1,0:T(8,128)(2,1)} %bitcast.13), calls=%async_computation | async-start | bytes 1572864 | tf_op jit(solution)/shard_map/all_to_all | solution.py:25
  34.0 4.7 %collective-permute-start.2 = (bf16[1,1792,512]{2,1,0:T(8,128)(2,1)S(1)}, bf16[1,1792,512]{2,1,0:T(8,128)(2,1)}, u32[]{:S(2)}, u32[]{:S(2)}) collective-permute-start(bf16[1,1792,512]{2,1,0:T(8,128)(2,1)S(1)} %get-tuple-element.36), channel_id=1, source_target_pairs={{1,0},{3,2},{5,4},{7,6},{9,8},{11,10},{13,12},{15,14},{16,17},{18,... | collective-permute-start | bytes 5505032 | tf_op jit(solution)/shard_map/ppermute | solution.py:366
  38.6 17.3 %all-gather.2.cloned.1.call-done.keys = bf16[4608,512]{1,0:T(8,128)(2,1)} async-done(((bf16[576,512]{1,0:T(8,128)(2,1)}), bf16[4608,512]{1,0:T(8,128)(2,1)}) %all-gather.2.cloned.1.call-update) | async-done | bytes 4718608 | tf_op jit(solution)/shard_map/all_gather | solution.py:505
  55.9 9.4 %attend_span.1 = (bf16[1024,512]{1,0:T(8,128)(2,1)}, f32[1024,1]{1,0:T(8,128)}, f32[1024,1]{1,0:T(8,128)}, f32[1024,512]{1,0:T(8,128)}) custom-call(bf16[512,256]{1,0:T(8,128)(2,1)} %q_nope.1, bf16[512,128]{1,0:T(8,128)(2,1)} %q_rope.3, bf16[4608,512]{1,0:T(8,128)(2,1)} %all-gather.2.cloned.1.call-done.keys, bf16[2,128,512]{2,1,0:T(8,128)(2,1)} %absorb_k.1), custom_call_target="tpu_custom_call" | custom-call | flops 10267656192 | bytes 8388608 | tf_op jit(solution)/shard_map/attend_span/pallas_call | solution.py:134
  65.4 20.2 %all-to-all-done.arrived = bf16[128,24,128]{2,1,0:T(8,128)(2,1)S(1)} async-done(((bf16[128,24,128]{2,1,0:T(8,128)(2,1)}), bf16[128,24,128]{2,1,0:T(8,128)(2,1)S(1)}, u32[]{:S(2)}, u32[]{:S(2)}) %all-to-all-start) | async-done | bytes 786464 | tf_op jit(solution)/shard_map/all_to_all | solution.py:25
  85.5 0.9 copy-done
  86.4 2.2 spread.1
  88.7 8.0 %all-to-all-start.1 = ((bf16[128,24,128]{2,1,0:T(8,128)(2,1)}), bf16[128,24,128]{2,1,0:T(8,128)(2,1)S(1)}, u32[]{:S(2)}, u32[]{:S(2)}) async-start(bf16[128,24,128]{2,1,0:T(8,128)(2,1)} %spread.1), calls=%async_computation.1 | async-start | bytes 1572864 | tf_op jit(solution)/shard_map/all_to_all | solution.py:25
  96.7 5.4 %collective-permute-start.3 = (bf16[1,512,3584]{2,1,0:T(8,128)(2,1)}, bf16[1,512,3584]{2,1,0:T(8,128)(2,1)}, u32[]{:S(2)}, u32[]{:S(2)}) collective-permute-start(bf16[1,512,3584]{2,1,0:T(8,128)(2,1)} %refs_2_.1), channel_id=1, source_target_pairs={{1,0},{3,2},{5,4},{7,6},{9,8},{11,10},{13,12},{15,14},{16,17},{18,... | collective-permute-start | bytes 11010056 | tf_op jit(solution)/shard_map/ppermute | solution.py:369
  102.0 11.6 %all-to-all-done.1 = bf16[128,24,128]{2,1,0:T(8,128)(2,1)S(1)} async-done(((bf16[128,24,128]{2,1,0:T(8,128)(2,1)}), bf16[128,24,128]{2,1,0:T(8,128)(2,1)S(1)}, u32[]{:S(2)}, u32[]{:S(2)}) %all-to-all-start.1) | async-done | bytes 786464 | tf_op jit(solution)/shard_map/all_to_all | solution.py:25
  113.7 0.9 copy-done.2
  114.6 8.4 %attend_prefix.1 = bf16[512,3584]{1,0:T(8,128)(2,1)} custom-call(bf16[1024,512]{1,0:T(8,128)(2,1)} %get-tuple-element.19.refs_0_.q_lat, bf16[512,128]{1,0:T(8,128)(2,1)} %q_rope.3, bf16[3072,128]{1,0:T(8,128)(2,1)} %bitcast.14, f32[1024,1]{1,0:T(8,128)} %get-tuple-element.20.refs_1_.old_top, f32[1024,1]{1,0:T(8,128)} %get-tuple-element.21.refs_2_.old_total, ...), custom_call_target="tpu_custom_call" | custom-call | flops 6442450944 | bytes 10485760 | tf_op jit(solution)/shard_map/attend_prefix/pallas_call | solution.py:161
  123.0 5.5 %all-to-all-start.2 = ((bf16[16,32,3584]{2,1,0:T(8,128)(2,1)}), bf16[16,32,3584]{2,1,0:T(8,128)(2,1)}, u32[]{:S(2)}, u32[]{:S(2)}) async-start(bf16[16,32,3584]{2,1,0:T(8,128)(2,1)} %bitcast.12), calls=%async_computation.2 | async-start | bytes 7340032 | tf_op jit(solution)/shard_map/all_to_all | solution.py:25
  128.5 0.8 collective-permute-start.4
  129.9 53.7 %collective-permute-done.3.refs_6_ = bf16[1,512,3584]{2,1,0:T(8,128)(2,1)} collective-permute-done((bf16[1,512,3584]{2,1,0:T(8,128)(2,1)}, bf16[1,512,3584]{2,1,0:T(8,128)(2,1)}, u32[]{:S(2)}, u32[]{:S(2)}) %collective-permute-start.3) | collective-permute-done | bytes 3670048 | tf_op jit(solution)/shard_map/ppermute | solution.py:369
  183.6 6.2 %all-to-all-done.2.terms = bf16[16,32,3584]{2,1,0:T(8,128)(2,1)} async-done(((bf16[16,32,3584]{2,1,0:T(8,128)(2,1)}), bf16[16,32,3584]{2,1,0:T(8,128)(2,1)}, u32[]{:S(2)}, u32[]{:S(2)}) %all-to-all-start.2) | async-done | bytes 3670048 | tf_op jit(solution)/shard_map/all_to_all | solution.py:25
  190.4 0.7 copy.20.ids
  191.1 6.5 %route.1 = (bf16[32,3584]{1,0:T(8,128)(2,1)}, bf16[1024,1792]{1,0:T(8,128)(2,1)}, bf16[64,1024]{1,0:T(8,128)(2,1)}) custom-call(bf16[16,32,3584]{2,1,0:T(8,128)(2,1)} %all-to-all-done.2.terms, bf16[32,3584]{1,0:T(8,128)(2,1)} %residual.1, bf16[1,3584]{1,0:T(2,128)(2,1)} %reshape.31.gain, bf16[64,3584]{1,0:T(8,128)(2,1)} %bitcast.15, s32[32,8]{1,0:T(8,128)} %copy.20.ids), custom_call_target="tpu_custom_call" | custom-call | tf_op jit(solution)/shard_map/route/pallas_call | solution.py:253
  197.6 11.2 %all-to-all-start.3 = ((bf16[128,8,1792]{2,1,0:T(8,128)(2,1)}), bf16[128,8,1792]{2,1,0:T(8,128)(2,1)}, u32[]{:S(2)}, u32[]{:S(2)}) async-start(bf16[128,8,1792]{2,1,0:T(8,128)(2,1)} %bitcast.11), calls=%async_computation.3 | async-start | bytes 7340032 | tf_op jit(solution)/shard_map/all_to_all | solution.py:25
  208.8 1.2 collective-permute-start.8
  210.3 3.3 collective-permute-done.8.refs_11_
  213.6 2.8 collective-permute-done.9.refs_12_
  216.3 38.8 %all-to-all-done.3 = bf16[128,8,1792]{2,1,0:T(8,128)(2,1)} async-done(((bf16[128,8,1792]{2,1,0:T(8,128)(2,1)}), bf16[128,8,1792]{2,1,0:T(8,128)(2,1)}, u32[]{:S(2)}, u32[]{:S(2)}) %all-to-all-start.3) | async-done | bytes 3670048 | tf_op jit(solution)/shard_map/all_to_all | solution.py:25
  255.1 19.8 %experts.1 = bf16[1024,1792]{1,0:T(8,128)(2,1)} custom-call(bf16[1024,1792]{1,0:T(8,128)(2,1)} %bitcast.6.rows, bf16[1,3584,512]{2,1,0:T(8,128)(2,1)} %refs_0_.1, bf16[1,3584,512]{2,1,0:T(8,128)(2,1)} %refs_1_.1, bf16[1,512,3584]{2,1,0:T(8,128)(2,1)} %refs_2_.1, bf16[1,3584,512]{2,1,0:T(8,128)(2,1)} %collective-permute-done.refs_3_, ...), custom_call_target="tpu_custom_call" | custom-call | tf_op jit(solution)/shard_map/experts/pallas_call | solution.py:340
  275.0 52.3 %all_to_all.25 = bf16[128,8,1792]{2,1,0:T(8,128)(2,1)} all-to-all(bf16[128,8,1792]{2,1,0:T(8,128)(2,1)} %bitcast.9), channel_id=1, replica_groups=mesh['node'=8,'dev'=16] {'node','dev'}, dimensions={0} | all-to-all | bytes 7340032 | tf_op jit(solution)/shard_map/all_to_all | solution.py:25
  327.2 4.2 %combine.1 = bf16[32,3584]{1,0:T(8,128)(2,1)} custom-call(bf16[64,1024]{1,0:T(8,128)(2,1)} %get-tuple-element.30.shares, bf16[1024,1792]{1,0:T(8,128)(2,1)} %bitcast.10), custom_call_target="tpu_custom_call" | custom-call | tf_op jit(solution)/shard_map/combine/pallas_call | solution.py:404
  (26 shorter events, 1.6 us)
Async XLA Ops:
  7.2 48.8 %all-gather.2.cloned.1.call-start = ((), (), s32[]{:S(2)}) async-start(), calls=%async_computation.5 | async-start | bytes 5308416 | tf_op jit(solution)/shard_map/all_gather | solution.py:505
  9.2 12.3 %copy-start.3 = (bf16[2,128,64]{1,2,0:T(8,128)(2,1)S(1)}, bf16[2,128,64]{1,2,0:T(8,128)(2,1)}, u32[]{:S(2)}) copy-start(bf16[2,128,64]{1,2,0:T(8,128)(2,1)} %param.22) | copy-start | bytes 98308
  9.2 79.5 %collective-permute-start = (bf16[1,3584,512]{2,1,0:T(8,128)(2,1)}, bf16[1,3584,512]{2,1,0:T(8,128)(2,1)}, u32[]{:S(2)}, u32[]{:S(2)}) collective-permute-start(bf16[1,3584,512]{2,1,0:T(8,128)(2,1)} %refs_0_.1), channel_id=1, source_target_pairs={{1,0},{3,2},{5,4},{7,6},{9,8},{11,10},{13,12},{15,14},{16,17},{18,... | collective-permute-start | bytes 11010056 | tf_op jit(solution)/shard_map/ppermute | solution.py:366
  19.0 69.7 %collective-permute-start.1 = (bf16[1,1792,512]{2,1,0:T(8,128)(2,1)}, bf16[1,1792,512]{2,1,0:T(8,128)(2,1)}, u32[]{:S(2)}, u32[]{:S(2)}) collective-permute-start(bf16[1,1792,512]{2,1,0:T(8,128)(2,1)} %get-tuple-element.37), channel_id=1, source_target_pairs={{1,0},{3,2},{5,4},{7,6},{9,8},{11,10},{13,12},{15,14},{16,17},{18,... | collective-permute-start | bytes 5505032 | tf_op jit(solution)/shard_map/ppermute | solution.py:366
  24.3 61.2 %all-to-all-start = ((bf16[128,24,128]{2,1,0:T(8,128)(2,1)}), bf16[128,24,128]{2,1,0:T(8,128)(2,1)S(1)}, u32[]{:S(2)}, u32[]{:S(2)}) async-start(bf16[128,24,128]{2,1,0:T(8,128)(2,1)} %bitcast.13), calls=%async_computation | async-start | bytes 1572864 | tf_op jit(solution)/shard_map/all_to_all | solution.py:25
  34.0 89.1 %collective-permute-start.2 = (bf16[1,1792,512]{2,1,0:T(8,128)(2,1)S(1)}, bf16[1,1792,512]{2,1,0:T(8,128)(2,1)}, u32[]{:S(2)}, u32[]{:S(2)}) collective-permute-start(bf16[1,1792,512]{2,1,0:T(8,128)(2,1)S(1)} %get-tuple-element.36), channel_id=1, source_target_pairs={{1,0},{3,2},{5,4},{7,6},{9,8},{11,10},{13,12},{15,14},{16,17},{18,... | collective-permute-start | bytes 5505032 | tf_op jit(solution)/shard_map/ppermute | solution.py:366
  85.5 0.9 copy-start
  88.7 25.0 %all-to-all-start.1 = ((bf16[128,24,128]{2,1,0:T(8,128)(2,1)}), bf16[128,24,128]{2,1,0:T(8,128)(2,1)S(1)}, u32[]{:S(2)}, u32[]{:S(2)}) async-start(bf16[128,24,128]{2,1,0:T(8,128)(2,1)} %spread.1), calls=%async_computation.1 | async-start | bytes 1572864 | tf_op jit(solution)/shard_map/all_to_all | solution.py:25
  96.7 87.0 %collective-permute-start.3 = (bf16[1,512,3584]{2,1,0:T(8,128)(2,1)}, bf16[1,512,3584]{2,1,0:T(8,128)(2,1)}, u32[]{:S(2)}, u32[]{:S(2)}) collective-permute-start(bf16[1,512,3584]{2,1,0:T(8,128)(2,1)} %refs_2_.1), channel_id=1, source_target_pairs={{1,0},{3,2},{5,4},{7,6},{9,8},{11,10},{13,12},{15,14},{16,17},{18,... | collective-permute-start | bytes 11010056 | tf_op jit(solution)/shard_map/ppermute | solution.py:369
  113.7 0.9 copy-start.2
  123.0 66.8 %copy-start.4 = (bf16[3584]{0:T(1024)(128)(2,1)S(1)}, bf16[3584]{0:T(1024)(128)(2,1)}, u32[]{:S(2)}) copy-start(bf16[3584]{0:T(1024)(128)(2,1)} %param.28) | copy-start | bytes 21508
  123.0 67.4 %copy-start.5 = (s32[32,8]{0,1:T(8,128)S(1)}, s32[32,8]{0,1:T(8,128)}, u32[]{:S(2)}) copy-start(s32[32,8]{0,1:T(8,128)} %param.30) | copy-start | bytes 3076
  123.0 66.8 %all-to-all-start.2 = ((bf16[16,32,3584]{2,1,0:T(8,128)(2,1)}), bf16[16,32,3584]{2,1,0:T(8,128)(2,1)}, u32[]{:S(2)}, u32[]{:S(2)}) async-start(bf16[16,32,3584]{2,1,0:T(8,128)(2,1)} %bitcast.12), calls=%async_computation.2 | async-start | bytes 7340032 | tf_op jit(solution)/shard_map/all_to_all | solution.py:25
  128.5 80.2 %collective-permute-start.4 = (bf16[1,3584,512]{2,1,0:T(8,128)(2,1)}, bf16[1,3584,512]{2,1,0:T(8,128)(2,1)}, u32[]{:S(2)}, u32[]{:S(2)}) collective-permute-start(bf16[1,3584,512]{2,1,0:T(8,128)(2,1)} %refs_0_.1), channel_id=1, source_target_pairs={{0,16},{1,17},{2,18},{3,19},{4,20},{5,21},{6,22},{7,23},{8,24},{9,... | collective-permute-start | bytes 11010056 | tf_op jit(solution)/shard_map/ppermute | solution.py:370
  129.3 80.7 %collective-permute-start.5 = (bf16[1,3584,512]{2,1,0:T(8,128)(2,1)}, bf16[1,3584,512]{2,1,0:T(8,128)(2,1)}, u32[]{:S(2)}, u32[]{:S(2)}) collective-permute-start(bf16[1,3584,512]{2,1,0:T(8,128)(2,1)} %refs_1_.1), channel_id=1, source_target_pairs={{0,16},{1,17},{2,18},{3,19},{4,20},{5,21},{6,22},{7,23},{8,24},{9,... | collective-permute-start | bytes 11010056 | tf_op jit(solution)/shard_map/ppermute | solution.py:370
  129.4 80.9 %collective-permute-start.6 = (bf16[1,512,3584]{2,1,0:T(8,128)(2,1)}, bf16[1,512,3584]{2,1,0:T(8,128)(2,1)}, u32[]{:S(2)}, u32[]{:S(2)}) collective-permute-start(bf16[1,512,3584]{2,1,0:T(8,128)(2,1)} %refs_2_.1), channel_id=1, source_target_pairs={{0,16},{1,17},{2,18},{3,19},{4,20},{5,21},{6,22},{7,23},{8,24},{9,... | collective-permute-start | bytes 11010056 | tf_op jit(solution)/shard_map/ppermute | solution.py:370
  129.8 86.5 %collective-permute-start.7 = (bf16[1,3584,512]{2,1,0:T(8,128)(2,1)}, bf16[1,3584,512]{2,1,0:T(8,128)(2,1)}, u32[]{:S(2)}, u32[]{:S(2)}) collective-permute-start(bf16[1,3584,512]{2,1,0:T(8,128)(2,1)} %collective-permute-done.refs_3_), channel_id=1, source_target_pairs={{0,16},{1,17},{2,18},{3,19},{4,20},{5,21},{6,22},{7,23},{8,24},{9,... | collective-permute-start | bytes 11010056 | tf_op jit(solution)/shard_map/ppermute | solution.py:373
  189.8 65.3 %collective-permute-start.10 = (bf16[1,512,3584]{2,1,0:T(8,128)(2,1)}, bf16[1,512,3584]{2,1,0:T(8,128)(2,1)}, u32[]{:S(2)}, u32[]{:S(2)}) collective-permute-start(bf16[1,512,3584]{2,1,0:T(8,128)(2,1)} %collective-permute-done.3.refs_6_), channel_id=1, source_target_pairs={{0,16},{1,17},{2,18},{3,19},{4,20},{5,21},{6,22},{7,23},{8,24},{9,... | collective-permute-start | bytes 11010056 | tf_op jit(solution)/shard_map/ppermute | solution.py:373
  197.6 57.5 %all-to-all-start.3 = ((bf16[128,8,1792]{2,1,0:T(8,128)(2,1)}), bf16[128,8,1792]{2,1,0:T(8,128)(2,1)}, u32[]{:S(2)}, u32[]{:S(2)}) async-start(bf16[128,8,1792]{2,1,0:T(8,128)(2,1)} %bitcast.11), calls=%async_computation.3 | async-start | bytes 7340032 | tf_op jit(solution)/shard_map/all_to_all | solution.py:25
  208.8 4.8 %collective-permute-start.8 = (bf16[1,1792,512]{2,1,0:T(8,128)(2,1)}, bf16[1,1792,512]{2,1,0:T(8,128)(2,1)S(1)}, u32[]{:S(2)}, u32[]{:S(2)}) collective-permute-start(bf16[1,1792,512]{2,1,0:T(8,128)(2,1)} %collective-permute-done.1.refs_4_), channel_id=1, source_target_pairs={{0,16},{1,17},{2,18},{3,19},{4,20},{5,21},{6,22},{7,23},{8,24},{9,... | collective-permute-start | bytes 5505032 | tf_op jit(solution)/shard_map/ppermute | solution.py:373
  210.0 6.4 %collective-permute-start.9 = (bf16[1,1792,512]{2,1,0:T(8,128)(2,1)}, bf16[1,1792,512]{2,1,0:T(8,128)(2,1)}, u32[]{:S(2)}, u32[]{:S(2)}) collective-permute-start(bf16[1,1792,512]{2,1,0:T(8,128)(2,1)} %collective-permute-done.2.refs_5_), channel_id=1, source_target_pairs={{0,16},{1,17},{2,18},{3,19},{4,20},{5,21},{6,22},{7,23},{8,24},{9,... | collective-permute-start | bytes 5505032 | tf_op jit(solution)/shard_map/ppermute | solution.py:373
  213.6 41.5 %copy-start.1 = (bf16[1,1792,512]{2,1,0:T(8,128)(2,1)}, bf16[1,1792,512]{2,1,0:T(8,128)(2,1)S(1)}, u32[]{:S(2)}) copy-start(bf16[1,1792,512]{2,1,0:T(8,128)(2,1)S(1)} %collective-permute-done.8.refs_11_) | copy-start | bytes 5505028
Sparse Core Ops, SparseCore 0:
  9.7 46.2 all-gather.1

commit v6 on v5

--- a/solution.py
+++ b/solution.py
@@ -303,6 +303,8 @@
     mid = block // 2
     wanted = here % mid // half * cap + here // mid * half + here % half
     order_rows = (there == wanted).astype(F32).astype(BF16)
+    wanted = there % mid // half * cap + there // mid * half + there % half
+    order_back = (here == wanted).astype(F32).astype(BF16)
     for b in range(0, count, block):
         sorted_rows = dot(order_rows, rows[b : b + block]).astype(BF16)
         whole_rows[b // 2 : b // 2 + mid, :narrow] = sorted_rows[:mid]
@@ -328,9 +330,7 @@
             parts.append(part.astype(BF16))
         for b in range(0, count, block):
             both = jnp.concatenate([part[b // 2 : b // 2 + mid] for part in parts], 0)
-            out[b : b + block, c : c + step] = dot(
-                order_rows, both, (((0,), (0,)), ((), ()))
-            ).astype(BF16)
+            out[b : b + block, c : c + step] = dot(order_back, both).astype(BF16)
 
 
 def experts(rows, sources, cap):

time: 339 us -> 339 us (level)
  no operation moved by 1% of the time
where the time goes in v6:
time: 339 us; the launch traced here: 338 us
  waiting for transfers between devices  154 us (45%)
  starting transfers between devices  55.9 us (16%)
  Pallas kernels  52.6 us (16%)
  blocking collectives  52.3 us (15%)
  between operations  14.1 us (4%)
  local copies, waits for them, and re-layouts  7.47 us (2%)
    all_to_all x4, waiting for transfers between devices, swap(): return lax.all_to_all(value, axis, split_axis=0, concat_axis=0, tiled=True)  76.8 us
    ppermute x1, waiting for transfers between devices, place_last(): crossed = list(crossed) + [lax.ppermute(last, ALL, across)]  53.7 us
    all_to_all x1, blocking collectives, swap(): return lax.all_to_all(value, axis, split_axis=0, concat_axis=0, tiled=True)  52.3 us
    all_to_all x4, starting transfers between devices, swap(): return lax.all_to_all(value, axis, split_axis=0, concat_axis=0, tiled=True)  34.2 us
    pallas_call x1, Pallas kernels, experts(): pl.pallas_call(functools.partial(expert_kernel, cap=cap), out_shape=jax.S...  19.8 us
    all_gather x1, waiting for transfers between devices, on_device(): keys = lax.all_gather(keys_here, 'node', axis=0, tiled=True)  17.3 us
    ppermute x3, starting transfers between devices, placed_weights(): lax.ppermute(w, ALL, across)  13.4 us
    pallas_call x1, Pallas kernels, attend_span(): pl.pallas_call(functools.partial(span_kernel, block=block), grid=(rows //...  9.41 us
  transfers between devices with their start and end apart: 16, of which 8 were waited for; matrix products, arithmetic and copies ran while one was open for 2% of the time, Pallas kernels for 8%

profile of v6, /device:TPU:1, one launch (start us, length us, event | category | flops | bytes accessed | tf_op | source)
XLA Modules:
  0.0 338.3 jit_solution(15901862364357854743)
XLA Ops:
  7.2 2.0 pad_maximum_fusion
  9.2 6.2 %collective-permute-start = (bf16[1,3584,512]{2,1,0:T(8,128)(2,1)}, bf16[1,3584,512]{2,1,0:T(8,128)(2,1)}, u32[]{:S(2)}, u32[]{:S(2)}) collective-permute-start(bf16[1,3584,512]{2,1,0:T(8,128)(2,1)} %refs_0_.1), channel_id=1, source_target_pairs={{1,0},{3,2},{5,4},{7,6},{9,8},{11,10},{13,12},{15,14},{16,17},{18,... | collective-permute-start | bytes 11010056 | tf_op jit(solution)/shard_map/ppermute | solution.py:366
  15.4 3.6 %fusion = (bf16[1,1792,512]{2,1,0:T(8,128)(2,1)S(1)}, bf16[1,1792,512]{2,1,0:T(8,128)(2,1)}) fusion(bf16[1,3584,512]{2,1,0:T(8,128)(2,1)} %refs_1_.1), kind=kLoop, calls=%fused_computation.1 | loop fusion | bytes 7340032 | tf_op jit(solution)/shard_map/slice | solution.py:366
  19.0 2.6 collective-permute-start.1
  21.5 0.7 copy.19.rot
  22.3 2.0 listed.1
  24.3 9.6 %all-to-all-start = ((bf16[128,24,128]{2,1,0:T(8,128)(2,1)}), bf16[128,24,128]{2,1,0:T(8,128)(2,1)S(1)}, u32[]{:S(2)}, u32[]{:S(2)}) async-start(bf16[128,24,128]{2,1,0:T(8,128)(2,1)} %bitcast.13), calls=%async_computation | async-start | bytes 1572864 | tf_op jit(solution)/shard_map/all_to_all | solution.py:25
  34.0 4.7 %collective-permute-start.2 = (bf16[1,1792,512]{2,1,0:T(8,128)(2,1)S(1)}, bf16[1,1792,512]{2,1,0:T(8,128)(2,1)}, u32[]{:S(2)}, u32[]{:S(2)}) collective-permute-start(bf16[1,1792,512]{2,1,0:T(8,128)(2,1)S(1)} %get-tuple-element.36), channel_id=1, source_target_pairs={{1,0},{3,2},{5,4},{7,6},{9,8},{11,10},{13,12},{15,14},{16,17},{18,... | collective-permute-start | bytes 5505032 | tf_op jit(solution)/shard_map/ppermute | solution.py:366
  38.6 17.3 %all-gather.2.cloned.1.call-done.keys = bf16[4608,512]{1,0:T(8,128)(2,1)} async-done(((bf16[576,512]{1,0:T(8,128)(2,1)}), bf16[4608,512]{1,0:T(8,128)(2,1)}) %all-gather.2.cloned.1.call-update) | async-done | bytes 4718608 | tf_op jit(solution)/shard_map/all_gather | solution.py:505
  55.9 9.4 %attend_span.1 = (bf16[1024,512]{1,0:T(8,128)(2,1)}, f32[1024,1]{1,0:T(8,128)}, f32[1024,1]{1,0:T(8,128)}, f32[1024,512]{1,0:T(8,128)}) custom-call(bf16[512,256]{1,0:T(8,128)(2,1)} %q_nope.1, bf16[512,128]{1,0:T(8,128)(2,1)} %q_rope.3, bf16[4608,512]{1,0:T(8,128)(2,1)} %all-gather.2.cloned.1.call-done.keys, bf16[2,128,512]{2,1,0:T(8,128)(2,1)} %absorb_k.1), custom_call_target="tpu_custom_call" | custom-call | flops 10267656192 | bytes 8388608 | tf_op jit(solution)/shard_map/attend_span/pallas_call | solution.py:134
  65.4 20.2 %all-to-all-done.arrived = bf16[128,24,128]{2,1,0:T(8,128)(2,1)S(1)} async-done(((bf16[128,24,128]{2,1,0:T(8,128)(2,1)}), bf16[128,24,128]{2,1,0:T(8,128)(2,1)S(1)}, u32[]{:S(2)}, u32[]{:S(2)}) %all-to-all-start) | async-done | bytes 786464 | tf_op jit(solution)/shard_map/all_to_all | solution.py:25
  85.5 0.9 copy-done
  86.4 2.2 spread.1
  88.7 8.0 %all-to-all-start.1 = ((bf16[128,24,128]{2,1,0:T(8,128)(2,1)}), bf16[128,24,128]{2,1,0:T(8,128)(2,1)S(1)}, u32[]{:S(2)}, u32[]{:S(2)}) async-start(bf16[128,24,128]{2,1,0:T(8,128)(2,1)} %spread.1), calls=%async_computation.1 | async-start | bytes 1572864 | tf_op jit(solution)/shard_map/all_to_all | solution.py:25
  96.7 5.4 %collective-permute-start.3 = (bf16[1,512,3584]{2,1,0:T(8,128)(2,1)}, bf16[1,512,3584]{2,1,0:T(8,128)(2,1)}, u32[]{:S(2)}, u32[]{:S(2)}) collective-permute-start(bf16[1,512,3584]{2,1,0:T(8,128)(2,1)} %refs_2_.1), channel_id=1, source_target_pairs={{1,0},{3,2},{5,4},{7,6},{9,8},{11,10},{13,12},{15,14},{16,17},{18,... | collective-permute-start | bytes 11010056 | tf_op jit(solution)/shard_map/ppermute | solution.py:369
  102.0 11.6 %all-to-all-done.1 = bf16[128,24,128]{2,1,0:T(8,128)(2,1)S(1)} async-done(((bf16[128,24,128]{2,1,0:T(8,128)(2,1)}), bf16[128,24,128]{2,1,0:T(8,128)(2,1)S(1)}, u32[]{:S(2)}, u32[]{:S(2)}) %all-to-all-start.1) | async-done | bytes 786464 | tf_op jit(solution)/shard_map/all_to_all | solution.py:25
  113.7 0.9 copy-done.2
  114.6 8.4 %attend_prefix.1 = bf16[512,3584]{1,0:T(8,128)(2,1)} custom-call(bf16[1024,512]{1,0:T(8,128)(2,1)} %get-tuple-element.19.refs_0_.q_lat, bf16[512,128]{1,0:T(8,128)(2,1)} %q_rope.3, bf16[3072,128]{1,0:T(8,128)(2,1)} %bitcast.14, f32[1024,1]{1,0:T(8,128)} %get-tuple-element.20.refs_1_.old_top, f32[1024,1]{1,0:T(8,128)} %get-tuple-element.21.refs_2_.old_total, ...), custom_call_target="tpu_custom_call" | custom-call | flops 6442450944 | bytes 10485760 | tf_op jit(solution)/shard_map/attend_prefix/pallas_call | solution.py:161
  123.0 5.5 %all-to-all-start.2 = ((bf16[16,32,3584]{2,1,0:T(8,128)(2,1)}), bf16[16,32,3584]{2,1,0:T(8,128)(2,1)}, u32[]{:S(2)}, u32[]{:S(2)}) async-start(bf16[16,32,3584]{2,1,0:T(8,128)(2,1)} %bitcast.12), calls=%async_computation.2 | async-start | bytes 7340032 | tf_op jit(solution)/shard_map/all_to_all | solution.py:25
  128.5 0.8 collective-permute-start.4
  129.9 53.7 %collective-permute-done.3.refs_6_ = bf16[1,512,3584]{2,1,0:T(8,128)(2,1)} collective-permute-done((bf16[1,512,3584]{2,1,0:T(8,128)(2,1)}, bf16[1,512,3584]{2,1,0:T(8,128)(2,1)}, u32[]{:S(2)}, u32[]{:S(2)}) %collective-permute-start.3) | collective-permute-done | bytes 3670048 | tf_op jit(solution)/shard_map/ppermute | solution.py:369
  183.6 6.2 %all-to-all-done.2.terms = bf16[16,32,3584]{2,1,0:T(8,128)(2,1)} async-done(((bf16[16,32,3584]{2,1,0:T(8,128)(2,1)}), bf16[16,32,3584]{2,1,0:T(8,128)(2,1)}, u32[]{:S(2)}, u32[]{:S(2)}) %all-to-all-start.2) | async-done | bytes 3670048 | tf_op jit(solution)/shard_map/all_to_all | solution.py:25
  190.4 0.7 copy.20.ids
  191.1 6.5 %route.1 = (bf16[32,3584]{1,0:T(8,128)(2,1)}, bf16[1024,1792]{1,0:T(8,128)(2,1)}, bf16[64,1024]{1,0:T(8,128)(2,1)}) custom-call(bf16[16,32,3584]{2,1,0:T(8,128)(2,1)} %all-to-all-done.2.terms, bf16[32,3584]{1,0:T(8,128)(2,1)} %residual.1, bf16[1,3584]{1,0:T(2,128)(2,1)} %reshape.31.gain, bf16[64,3584]{1,0:T(8,128)(2,1)} %bitcast.15, s32[32,8]{1,0:T(8,128)} %copy.20.ids), custom_call_target="tpu_custom_call" | custom-call | tf_op jit(solution)/shard_map/route/pallas_call | solution.py:253
  197.6 11.2 %all-to-all-start.3 = ((bf16[128,8,1792]{2,1,0:T(8,128)(2,1)}), bf16[128,8,1792]{2,1,0:T(8,128)(2,1)}, u32[]{:S(2)}, u32[]{:S(2)}) async-start(bf16[128,8,1792]{2,1,0:T(8,128)(2,1)} %bitcast.11), calls=%async_computation.3 | async-start | bytes 7340032 | tf_op jit(solution)/shard_map/all_to_all | solution.py:25
  208.8 1.2 collective-permute-start.8
  210.3 3.3 collective-permute-done.8.refs_11_
  213.6 2.8 collective-permute-done.9.refs_12_
  216.3 38.8 %all-to-all-done.3 = bf16[128,8,1792]{2,1,0:T(8,128)(2,1)} async-done(((bf16[128,8,1792]{2,1,0:T(8,128)(2,1)}), bf16[128,8,1792]{2,1,0:T(8,128)(2,1)}, u32[]{:S(2)}, u32[]{:S(2)}) %all-to-all-start.3) | async-done | bytes 3670048 | tf_op jit(solution)/shard_map/all_to_all | solution.py:25
  255.1 19.8 %experts.1 = bf16[1024,1792]{1,0:T(8,128)(2,1)} custom-call(bf16[1024,1792]{1,0:T(8,128)(2,1)} %bitcast.6.rows, bf16[1,3584,512]{2,1,0:T(8,128)(2,1)} %refs_0_.1, bf16[1,3584,512]{2,1,0:T(8,128)(2,1)} %refs_1_.1, bf16[1,512,3584]{2,1,0:T(8,128)(2,1)} %refs_2_.1, bf16[1,3584,512]{2,1,0:T(8,128)(2,1)} %collective-permute-done.refs_3_, ...), custom_call_target="tpu_custom_call" | custom-call | tf_op jit(solution)/shard_map/experts/pallas_call | solution.py:340
  275.0 52.3 %all_to_all.25 = bf16[128,8,1792]{2,1,0:T(8,128)(2,1)} all-to-all(bf16[128,8,1792]{2,1,0:T(8,128)(2,1)} %bitcast.9), channel_id=1, replica_groups=mesh['node'=8,'dev'=16] {'node','dev'}, dimensions={0} | all-to-all | bytes 7340032 | tf_op jit(solution)/shard_map/all_to_all | solution.py:25
  327.2 4.2 %combine.1 = bf16[32,3584]{1,0:T(8,128)(2,1)} custom-call(bf16[64,1024]{1,0:T(8,128)(2,1)} %get-tuple-element.30.shares, bf16[1024,1792]{1,0:T(8,128)(2,1)} %bitcast.10), custom_call_target="tpu_custom_call" | custom-call | tf_op jit(solution)/shard_map/combine/pallas_call | solution.py:404
  (26 shorter events, 1.6 us)
Async XLA Ops:
  7.2 48.8 %all-gather.2.cloned.1.call-start = ((), (), s32[]{:S(2)}) async-start(), calls=%async_computation.5 | async-start | bytes 5308416 | tf_op jit(solution)/shard_map/all_gather | solution.py:505
  9.2 12.3 %copy-start.3 = (bf16[2,128,64]{1,2,0:T(8,128)(2,1)S(1)}, bf16[2,128,64]{1,2,0:T(8,128)(2,1)}, u32[]{:S(2)}) copy-start(bf16[2,128,64]{1,2,0:T(8,128)(2,1)} %param.22) | copy-start | bytes 98308
  9.2 79.5 %collective-permute-start = (bf16[1,3584,512]{2,1,0:T(8,128)(2,1)}, bf16[1,3584,512]{2,1,0:T(8,128)(2,1)}, u32[]{:S(2)}, u32[]{:S(2)}) collective-permute-start(bf16[1,3584,512]{2,1,0:T(8,128)(2,1)} %refs_0_.1), channel_id=1, source_target_pairs={{1,0},{3,2},{5,4},{7,6},{9,8},{11,10},{13,12},{15,14},{16,17},{18,... | collective-permute-start | bytes 11010056 | tf_op jit(solution)/shard_map/ppermute | solution.py:366
  19.0 69.7 %collective-permute-start.1 = (bf16[1,1792,512]{2,1,0:T(8,128)(2,1)}, bf16[1,1792,512]{2,1,0:T(8,128)(2,1)}, u32[]{:S(2)}, u32[]{:S(2)}) collective-permute-start(bf16[1,1792,512]{2,1,0:T(8,128)(2,1)} %get-tuple-element.37), channel_id=1, source_target_pairs={{1,0},{3,2},{5,4},{7,6},{9,8},{11,10},{13,12},{15,14},{16,17},{18,... | collective-permute-start | bytes 5505032 | tf_op jit(solution)/shard_map/ppermute | solution.py:366
  24.3 61.2 %all-to-all-start = ((bf16[128,24,128]{2,1,0:T(8,128)(2,1)}), bf16[128,24,128]{2,1,0:T(8,128)(2,1)S(1)}, u32[]{:S(2)}, u32[]{:S(2)}) async-start(bf16[128,24,128]{2,1,0:T(8,128)(2,1)} %bitcast.13), calls=%async_computation | async-start | bytes 1572864 | tf_op jit(solution)/shard_map/all_to_all | solution.py:25
  34.0 89.1 %collective-permute-start.2 = (bf16[1,1792,512]{2,1,0:T(8,128)(2,1)S(1)}, bf16[1,1792,512]{2,1,0:T(8,128)(2,1)}, u32[]{:S(2)}, u32[]{:S(2)}) collective-permute-start(bf16[1,1792,512]{2,1,0:T(8,128)(2,1)S(1)} %get-tuple-element.36), channel_id=1, source_target_pairs={{1,0},{3,2},{5,4},{7,6},{9,8},{11,10},{13,12},{15,14},{16,17},{18,... | collective-permute-start | bytes 5505032 | tf_op jit(solution)/shard_map/ppermute | solution.py:366
  85.5 0.9 copy-start
  88.7 25.0 %all-to-all-start.1 = ((bf16[128,24,128]{2,1,0:T(8,128)(2,1)}), bf16[128,24,128]{2,1,0:T(8,128)(2,1)S(1)}, u32[]{:S(2)}, u32[]{:S(2)}) async-start(bf16[128,24,128]{2,1,0:T(8,128)(2,1)} %spread.1), calls=%async_computation.1 | async-start | bytes 1572864 | tf_op jit(solution)/shard_map/all_to_all | solution.py:25
  96.7 87.0 %collective-permute-start.3 = (bf16[1,512,3584]{2,1,0:T(8,128)(2,1)}, bf16[1,512,3584]{2,1,0:T(8,128)(2,1)}, u32[]{:S(2)}, u32[]{:S(2)}) collective-permute-start(bf16[1,512,3584]{2,1,0:T(8,128)(2,1)} %refs_2_.1), channel_id=1, source_target_pairs={{1,0},{3,2},{5,4},{7,6},{9,8},{11,10},{13,12},{15,14},{16,17},{18,... | collective-permute-start | bytes 11010056 | tf_op jit(solution)/shard_map/ppermute | solution.py:369
  113.7 0.9 copy-start.2
  123.0 66.8 %copy-start.4 = (bf16[3584]{0:T(1024)(128)(2,1)S(1)}, bf16[3584]{0:T(1024)(128)(2,1)}, u32[]{:S(2)}) copy-start(bf16[3584]{0:T(1024)(128)(2,1)} %param.28) | copy-start | bytes 21508
  123.0 67.4 %copy-start.5 = (s32[32,8]{0,1:T(8,128)S(1)}, s32[32,8]{0,1:T(8,128)}, u32[]{:S(2)}) copy-start(s32[32,8]{0,1:T(8,128)} %param.30) | copy-start | bytes 3076
  123.0 66.8 %all-to-all-start.2 = ((bf16[16,32,3584]{2,1,0:T(8,128)(2,1)}), bf16[16,32,3584]{2,1,0:T(8,128)(2,1)}, u32[]{:S(2)}, u32[]{:S(2)}) async-start(bf16[16,32,3584]{2,1,0:T(8,128)(2,1)} %bitcast.12), calls=%async_computation.2 | async-start | bytes 7340032 | tf_op jit(solution)/shard_map/all_to_all | solution.py:25
  128.5 80.2 %collective-permute-start.4 = (bf16[1,3584,512]{2,1,0:T(8,128)(2,1)}, bf16[1,3584,512]{2,1,0:T(8,128)(2,1)}, u32[]{:S(2)}, u32[]{:S(2)}) collective-permute-start(bf16[1,3584,512]{2,1,0:T(8,128)(2,1)} %refs_0_.1), channel_id=1, source_target_pairs={{0,16},{1,17},{2,18},{3,19},{4,20},{5,21},{6,22},{7,23},{8,24},{9,... | collective-permute-start | bytes 11010056 | tf_op jit(solution)/shard_map/ppermute | solution.py:370
  129.3 80.7 %collective-permute-start.5 = (bf16[1,3584,512]{2,1,0:T(8,128)(2,1)}, bf16[1,3584,512]{2,1,0:T(8,128)(2,1)}, u32[]{:S(2)}, u32[]{:S(2)}) collective-permute-start(bf16[1,3584,512]{2,1,0:T(8,128)(2,1)} %refs_1_.1), channel_id=1, source_target_pairs={{0,16},{1,17},{2,18},{3,19},{4,20},{5,21},{6,22},{7,23},{8,24},{9,... | collective-permute-start | bytes 11010056 | tf_op jit(solution)/shard_map/ppermute | solution.py:370
  129.4 80.9 %collective-permute-start.6 = (bf16[1,512,3584]{2,1,0:T(8,128)(2,1)}, bf16[1,512,3584]{2,1,0:T(8,128)(2,1)}, u32[]{:S(2)}, u32[]{:S(2)}) collective-permute-start(bf16[1,512,3584]{2,1,0:T(8,128)(2,1)} %refs_2_.1), channel_id=1, source_target_pairs={{0,16},{1,17},{2,18},{3,19},{4,20},{5,21},{6,22},{7,23},{8,24},{9,... | collective-permute-start | bytes 11010056 | tf_op jit(solution)/shard_map/ppermute | solution.py:370
  129.8 86.5 %collective-permute-start.7 = (bf16[1,3584,512]{2,1,0:T(8,128)(2,1)}, bf16[1,3584,512]{2,1,0:T(8,128)(2,1)}, u32[]{:S(2)}, u32[]{:S(2)}) collective-permute-start(bf16[1,3584,512]{2,1,0:T(8,128)(2,1)} %collective-permute-done.refs_3_), channel_id=1, source_target_pairs={{0,16},{1,17},{2,18},{3,19},{4,20},{5,21},{6,22},{7,23},{8,24},{9,... | collective-permute-start | bytes 11010056 | tf_op jit(solution)/shard_map/ppermute | solution.py:373
  189.8 65.3 %collective-permute-start.10 = (bf16[1,512,3584]{2,1,0:T(8,128)(2,1)}, bf16[1,512,3584]{2,1,0:T(8,128)(2,1)}, u32[]{:S(2)}, u32[]{:S(2)}) collective-permute-start(bf16[1,512,3584]{2,1,0:T(8,128)(2,1)} %collective-permute-done.3.refs_6_), channel_id=1, source_target_pairs={{0,16},{1,17},{2,18},{3,19},{4,20},{5,21},{6,22},{7,23},{8,24},{9,... | collective-permute-start | bytes 11010056 | tf_op jit(solution)/shard_map/ppermute | solution.py:373
  197.6 57.5 %all-to-all-start.3 = ((bf16[128,8,1792]{2,1,0:T(8,128)(2,1)}), bf16[128,8,1792]{2,1,0:T(8,128)(2,1)}, u32[]{:S(2)}, u32[]{:S(2)}) async-start(bf16[128,8,1792]{2,1,0:T(8,128)(2,1)} %bitcast.11), calls=%async_computation.3 | async-start | bytes 7340032 | tf_op jit(solution)/shard_map/all_to_all | solution.py:25
  208.8 4.8 %collective-permute-start.8 = (bf16[1,1792,512]{2,1,0:T(8,128)(2,1)}, bf16[1,1792,512]{2,1,0:T(8,128)(2,1)S(1)}, u32[]{:S(2)}, u32[]{:S(2)}) collective-permute-start(bf16[1,1792,512]{2,1,0:T(8,128)(2,1)} %collective-permute-done.1.refs_4_), channel_id=1, source_target_pairs={{0,16},{1,17},{2,18},{3,19},{4,20},{5,21},{6,22},{7,23},{8,24},{9,... | collective-permute-start | bytes 5505032 | tf_op jit(solution)/shard_map/ppermute | solution.py:373
  210.0 6.4 %collective-permute-start.9 = (bf16[1,1792,512]{2,1,0:T(8,128)(2,1)}, bf16[1,1792,512]{2,1,0:T(8,128)(2,1)}, u32[]{:S(2)}, u32[]{:S(2)}) collective-permute-start(bf16[1,1792,512]{2,1,0:T(8,128)(2,1)} %collective-permute-done.2.refs_5_), channel_id=1, source_target_pairs={{0,16},{1,17},{2,18},{3,19},{4,20},{5,21},{6,22},{7,23},{8,24},{9,... | collective-permute-start | bytes 5505032 | tf_op jit(solution)/shard_map/ppermute | solution.py:373
  213.6 41.5 %copy-start.1 = (bf16[1,1792,512]{2,1,0:T(8,128)(2,1)}, bf16[1,1792,512]{2,1,0:T(8,128)(2,1)S(1)}, u32[]{:S(2)}) copy-start(bf16[1,1792,512]{2,1,0:T(8,128)(2,1)S(1)} %collective-permute-done.8.refs_11_) | copy-start | bytes 5505028
Sparse Core Ops, SparseCore 0:
  9.7 46.2 all-gather.1
